TPU v7x, 32 devices: a whole 2x2x4 slice. The times are simulated.
32 devices in a mesh: dp: 8 (over y, x, core), tensor: 4 (over z).
Axes of the slice: x: 2, y: 2, z: 4, core: 2. Of those that a mesh axis runs over, the one named last changes fastest.
Arguments:
- tokens: bfloat16 [16384, 1536], P(('dp', 'tensor')), may hold values from -6 to 6
- granularity: int32 [16], P('dp'), may hold values from 0 to 3, as said below
- gain_one: float32 [1536], replicated, may hold values from 0.5 to 1.5
- shift_one: float32 [1536], replicated, may hold values from -1.5 to 1.5
- w_qkv: bfloat16 [3, 1536, 1536], P(None, None, 'tensor'), may hold values from -0.15625 to 0.15625
- w_out: bfloat16 [1536, 1536], P('tensor'), may hold values from -0.625 to 0.625
- gain_two: float32 [1536], replicated, may hold values from 0.5 to 1.5
- shift_two: float32 [1536], replicated, may hold values from -1.5 to 1.5
- w_up: bfloat16 [1536, 6144], P(None, 'tensor'), may hold values from -0.15625 to 0.15625
- w_down: bfloat16 [6144, 1536], P('tensor'), may hold values from -0.15625 to 0.15625
- cotangent: bfloat16 [16384, 1536], P(('dp', 'tensor')), may hold values from -6 to 6
Outputs:
- layer_out: bfloat16 [16384, 1536], P(('dp', 'tensor'))
- grad_tokens: float32 [16384, 1536], P(('dp', 'tensor'))
- grad_gain_one: float32 [1536], replicated
- grad_shift_one: float32 [1536], replicated
- grad_qkv: float32 [3, 1536, 1536], P(None, None, 'tensor')
- grad_out: float32 [1536, 1536], P('tensor')
- grad_gain_two: float32 [1536], replicated
- grad_shift_two: float32 [1536], replicated
- grad_up: float32 [1536, 6144], P(None, 'tensor')
- grad_down: float32 [6144, 1536], P('tensor')
Inputs may be any that keep to these rules, and one draw needn't show every extreme that they name: hidden unit j serves the tokens of sequence s when j < 6144 // 8 * 2**granularity[s].
All inputs are finite; a program needn't handle non-finite values.
Results may differ from a plain program's by a relative error of at most 0.015.
Values may be sent and summed in bfloat16 or wider, within the bound.
No kernel may reach another device: no remote copies, remote signals or barrier semaphores. Data moves between devices by JAX's collectives and lax.ppermute only.
A program may use at most 192 MiB of HBM per device.

v0:
```python
import math

import jax
import jax.numpy as jnp
from jax import lax
from jax.sharding import PartitionSpec as P

HD = 128
FF = 6144


def norm_apply(values, gain, shift):
    center = values - jnp.mean(values, axis=-1, keepdims=True)
    spread = jnp.mean(center * center, axis=-1, keepdims=True)
    return center * lax.rsqrt(spread + 1e-05) * gain + shift


def rope_tables(length, head_dim):
    half_dim = head_dim // 2
    frequency = jnp.exp(
        jnp.arange(half_dim, dtype=jnp.float32) * (-2.0 * math.log(10000.0) / head_dim)
    )
    angles = jnp.arange(length, dtype=jnp.float32)[:, None] * frequency[None, :]
    return (jnp.cos(angles)[:, None, :], jnp.sin(angles)[:, None, :])


def rotate(values, cos_part, sin_part):
    half_dim = values.shape[-1] // 2
    low_half = values[..., :half_dim]
    high_half = values[..., half_dim:]
    return jnp.concatenate(
        [low_half * cos_part - high_half * sin_part, high_half * cos_part + low_half * sin_part],
        axis=-1,
    )


def unrotate(grads, cos_part, sin_part):
    half_dim = grads.shape[-1] // 2
    low_half = grads[..., :half_dim]
    high_half = grads[..., half_dim:]
    return jnp.concatenate(
        [low_half * cos_part + high_half * sin_part, high_half * cos_part - low_half * sin_part],
        axis=-1,
    )


def causal_scores(queries, key_rows, score_scale):
    length = queries.shape[0]
    raw_scores = (
        jnp.einsum("qhd,khd->hqk", queries, key_rows, preferred_element_type=jnp.float32)
        * score_scale
    )
    row_place = lax.broadcasted_iota(jnp.int32, (length, length), 0)
    col_place = lax.broadcasted_iota(jnp.int32, (length, length), 1)
    return jnp.where((row_place >= col_place)[None], raw_scores, -1e30)


def settle(first_grad, second_grad):
    reduced = (
        lax.psum_scatter(first_grad, "dp", scatter_dimension=1, tiled=True),
        lax.psum_scatter(second_grad, "dp", scatter_dimension=1, tiled=True),
    )
    return (
        lax.all_gather(reduced[0].astype(jnp.bfloat16), "dp", axis=1, tiled=True).astype(
            jnp.float32
        ),
        lax.all_gather(reduced[1].astype(jnp.bfloat16), "dp", axis=1, tiled=True).astype(
            jnp.float32
        ),
    )


def shards(
    tokens,
    granularity,
    gain_one,
    shift_one,
    w_qkv,
    w_out,
    gain_two,
    shift_two,
    w_up,
    w_down,
    cotangent,
):
    tensor_size = lax.axis_size("tensor")
    tensor_rank = lax.axis_index("tensor")
    local_rows = tokens.shape[0]
    seq_count = granularity.shape[0]
    group_rows = local_rows * tensor_size
    seq_len = group_rows // seq_count
    heads_here = w_qkv.shape[2] // HD
    hidden_here = w_up.shape[1]
    score_scale = HD ** (-0.5)
    cos_part, sin_part = rope_tables(seq_len, HD)
    tokens_wide = tokens.astype(jnp.float32)
    normed_one, pull_one = jax.vjp(norm_apply, tokens_wide, gain_one, shift_one)
    gathered_one = lax.all_gather(normed_one.astype(jnp.bfloat16), "tensor", axis=0, tiled=True)
    projected = jnp.einsum("rd,cde->cre", gathered_one, w_qkv, preferred_element_type=jnp.float32)
    projected = projected.reshape(3, seq_count, seq_len, heads_here, HD)
    queries = rotate(projected[0], cos_part, sin_part).astype(jnp.bfloat16)
    key_rows = rotate(projected[1], cos_part, sin_part).astype(jnp.bfloat16)
    value_rows = projected[2].astype(jnp.bfloat16)

    def attend_full(members):
        query_one, key_one, value_one = members
        scores = causal_scores(query_one, key_one, score_scale)
        log_total = jax.nn.logsumexp(scores, axis=-1, keepdims=True)
        attn_probs = jnp.exp(scores - log_total)
        blended = jnp.einsum(
            "hqk,khd->qhd",
            attn_probs.astype(jnp.bfloat16),
            value_one,
            preferred_element_type=jnp.float32,
        )
        return (blended.astype(jnp.bfloat16), log_total, attn_probs)

    def attend_light(members):
        blended, log_total, attn_probs = attend_full(members)
        return (blended, log_total)

    attended, log_totals = lax.map(attend_light, (queries, key_rows, value_rows))
    attn_flat = attended.reshape(group_rows, heads_here * HD)
    resid = tokens_wide + lax.psum_scatter(
        jnp.dot(attn_flat, w_out, preferred_element_type=jnp.float32),
        "tensor",
        scatter_dimension=0,
        tiled=True,
    )
    normed_two, pull_two = jax.vjp(norm_apply, resid, gain_two, shift_two)
    normed_low = normed_two.astype(jnp.bfloat16)
    unit_limit = jnp.left_shift(jnp.ones_like(granularity), granularity) * (FF // 8)
    gathered_two = lax.all_gather(normed_low, "tensor", axis=0, tiled=True)
    pre_act = jnp.dot(gathered_two, w_up, preferred_element_type=jnp.float32).reshape(
        seq_count, seq_len, hidden_here
    )
    unit_index = tensor_rank * hidden_here + jnp.arange(hidden_here, dtype=jnp.int32)
    unit_mask = (unit_index[None, :] < unit_limit[:, None]).astype(jnp.float32)[:, None, :]

    def activate(pre_values):
        return jax.nn.gelu(pre_values, approximate=True) * unit_mask

    hidden, pull_gelu = jax.vjp(activate, pre_act)
    hidden_flat = hidden.astype(jnp.bfloat16).reshape(group_rows, hidden_here)
    output = resid + lax.psum_scatter(
        jnp.dot(hidden_flat, w_down, preferred_element_type=jnp.float32).astype(jnp.bfloat16),
        "tensor",
        scatter_dimension=0,
        tiled=True,
    ).astype(jnp.float32)
    layer_out = output.astype(jnp.bfloat16)
    grad_rows = lax.all_gather(cotangent, "tensor", axis=0, tiled=True)
    grad_down_part = jnp.einsum(
        "rf,rd->fd", hidden_flat, grad_rows, preferred_element_type=jnp.float32
    )
    grad_hidden = jnp.einsum("rd,fd->rf", grad_rows, w_down, preferred_element_type=jnp.float32)
    grad_pre = pull_gelu(grad_hidden.reshape(seq_count, seq_len, hidden_here))[0]
    grad_pre = grad_pre.astype(jnp.bfloat16).reshape(group_rows, hidden_here)
    grad_up_part = jnp.einsum(
        "rd,rf->df", gathered_two, grad_pre, preferred_element_type=jnp.float32
    )
    grad_normed_two = lax.psum_scatter(
        jnp.einsum("rf,df->rd", grad_pre, w_up, preferred_element_type=jnp.float32),
        "tensor",
        scatter_dimension=0,
        tiled=True,
    )
    grad_resid, grad_gain_two, grad_shift_two = pull_two(grad_normed_two)
    grad_resid = cotangent.astype(jnp.float32) + grad_resid
    grad_up, grad_down = (grad_up_part, grad_down_part)
    grad_attn_rows = lax.all_gather(grad_resid.astype(jnp.bfloat16), "tensor", axis=0, tiled=True)
    grad_out_part = jnp.einsum(
        "re,rd->ed", attn_flat, grad_attn_rows, preferred_element_type=jnp.float32
    )
    grad_attended = jnp.einsum(
        "rd,ed->re", grad_attn_rows, w_out, preferred_element_type=jnp.float32
    )
    grad_attended = grad_attended.astype(jnp.bfloat16).reshape(seq_count, seq_len, heads_here, HD)

    def back_one(query_one, key_one, value_one, attn_probs, grad_one):
        grad_probs = jnp.einsum(
            "qhd,khd->hqk", grad_one, value_one, preferred_element_type=jnp.float32
        )
        grad_value = jnp.einsum(
            "hqk,qhd->khd",
            attn_probs.astype(jnp.bfloat16),
            grad_one,
            preferred_element_type=jnp.float32,
        )
        row_inner = jnp.sum(grad_probs * attn_probs, axis=-1, keepdims=True)
        grad_scores = (attn_probs * (grad_probs - row_inner) * score_scale).astype(jnp.bfloat16)
        grad_query = jnp.einsum(
            "hqk,khd->qhd", grad_scores, key_one, preferred_element_type=jnp.float32
        )
        grad_key = jnp.einsum(
            "hqk,qhd->khd", grad_scores, query_one, preferred_element_type=jnp.float32
        )
        return (
            unrotate(grad_query, cos_part, sin_part).astype(jnp.bfloat16),
            unrotate(grad_key, cos_part, sin_part).astype(jnp.bfloat16),
            grad_value.astype(jnp.bfloat16),
        )

    def back_again(members):
        query_one, key_one, value_one, log_total, grad_one = members
        attn_probs = jnp.exp(causal_scores(query_one, key_one, score_scale) - log_total)
        return back_one(query_one, key_one, value_one, attn_probs, grad_one)

    grad_query, grad_key, grad_value = lax.map(
        back_again, (queries, key_rows, value_rows, log_totals, grad_attended)
    )
    grad_proj = jnp.stack([grad_query, grad_key, grad_value]).reshape(
        3, group_rows, heads_here * HD
    )
    grad_qkv_part = jnp.einsum(
        "rd,cre->cde", gathered_one, grad_proj, preferred_element_type=jnp.float32
    )
    grad_normed_one = lax.psum_scatter(
        jnp.einsum("cre,cde->rd", grad_proj, w_qkv, preferred_element_type=jnp.float32).astype(
            jnp.bfloat16
        ),
        "tensor",
        scatter_dimension=0,
        tiled=True,
    ).astype(jnp.float32)
    grad_local, grad_gain_one, grad_shift_one = pull_one(grad_normed_one)
    grad_tokens = grad_resid + grad_local
    gain_sums = lax.psum(
        (grad_gain_one, grad_shift_one, grad_gain_two, grad_shift_two), ("dp", "tensor")
    )
    grad_qkv, grad_out = settle(grad_qkv_part, grad_out_part)
    grad_up, grad_down = settle(grad_up, grad_down)
    return (
        layer_out,
        grad_tokens,
        gain_sums[0],
        gain_sums[1],
        grad_qkv,
        grad_out,
        gain_sums[2],
        gain_sums[3],
        grad_up,
        grad_down,
    )


def solution(mesh):
    placed = (
        P(("dp", "tensor"), None),
        P("dp"),
        P(),
        P(),
        P(None, None, "tensor"),
        P("tensor", None),
        P(),
        P(),
        P(None, "tensor"),
        P("tensor", None),
        P(("dp", "tensor"), None),
    )
    return jax.shard_map(
        shards,
        mesh=mesh,
        in_specs=placed,
        out_specs=(
            P(("dp", "tensor"), None),
            P(("dp", "tensor"), None),
            P(),
            P(),
            P(None, None, "tensor"),
            P("tensor", None),
            P(),
            P(),
            P(None, "tensor"),
            P("tensor", None),
        ),
        check_vma=False,
    )
```

profile of v0, /device:TPU:0, one launch (start us, length us, event | category | flops | bytes accessed | tf_op | source)
XLA Modules:
  0.0 1777.5 jit_solution(11508736577069865268)
XLA Ops:
  16.5 115.8 %all-gather.9.cloned.1.call-done = bf16[2048,1536]{1,0:T(8,128)(2,1)} async-done(((bf16[512,1536]{1,0:T(8,128)(2,1)}), bf16[2048,1536]{1,0:T(8,128)(2,1)}) %all-gather.9.cloned.1.call-update) | async-done | bytes 6291472 | tf_op jit(solution)/shard_map/all_gather | solution.py:98
  132.3 10.3 fusion.122
  196.6 52.9 %while.29 = (s32[]{:T(128)}, bf16[2,1024,3,128]{1,3,2,0:T(8,128)(2,1)}, f32[2,3,1024,1]{2,1,3,0:T(4,128)}, bf16[2,1024,3,128]{1,3,2,0:T(8,128)(2,1)}, bf16[2,102...) while((s32[]{:T(128)}, bf16[2,1024,3,128]{1,3,2,0:T(8,128)(2,1)}, ...), condition=%wide.region_5.6_spmd, body=%wide.region_2.5_spmd.sunk | while | flops 1646682112 | bytes 64325860 | solution.py:122
  197.3 8.4 fusion.193
  223.6 8.4 fusion.193
  260.8 210.2 %reduce-scatter.11.cloned.1.call-done = f32[512,1536]{1,0:T(8,128)} async-done(((f32[2048,1536]{1,0:T(8,128)}), f32[512,1536]{1,0:T(8,128)}) %reduce-scatter.11.cloned.1.call-update) | async-done | bytes 3145744 | tf_op jit(solution)/shard_map/reduce_scatter | solution.py:124
  479.1 114.6 %all-gather.11.cloned.1.call-done = bf16[2048,1536]{1,0:T(8,128)(2,1)} async-done(((bf16[512,1536]{1,0:T(8,128)(2,1)}), bf16[2048,1536]{1,0:T(8,128)(2,1)}) %all-gather.11.cloned.1.call-update) | async-done | bytes 6291472 | tf_op jit(solution)/shard_map/all_gather | solution.py:133
  593.7 19.1 %fusion.113 = (bf16[2048,1536]{1,0:T(8,128)(2,1)}, f32[2048,1536]{1,0:T(8,128)}) fusion(f32[2,1536]{1,0:T(2,128)} %compare_convert_fusion, bf16[2048,1536]{1,0:T(8,128)(2,1)} %all-gather.11.cloned.1.call-done, bf16[1536,1536]{1,0:T(8,128)(2,1)} %param.23), kind=kOutput, calls=%fused_computation.107 | convolution fusion | flops 9695133696 | bytes 29896704 | tf_op jit(solution)/shard_map/dot_general | solution.py:134
  612.8 95.9 %all-gather.13.cloned.1.call-done = bf16[2048,1536]{1,0:T(8,128)(2,1)} async-done(((bf16[512,1536]{1,0:T(8,128)(2,1)}), bf16[2048,1536]{1,0:T(8,128)(2,1)}) %all-gather.13.cloned.1.call-update) | async-done | bytes 6291472 | tf_op jit(solution)/shard_map/all_gather | solution.py:152
  708.8 21.7 %fusion.112 = bf16[2048,1536]{1,0:T(8,128)(2,1)S(1)} fusion(f32[2048,1536]{1,0:T(8,128)} %get-tuple-element.385, bf16[2048,1536]{1,0:T(8,128)(2,1)} %all-gather.13.cloned.1.call-done, bf16[1536,1536]{1,0:T(8,128)(2,1)} %param.24, f32[2,1536]{1,0:T(2,128)} %compare_convert_fusion), kind=kOutput, calls=%fused_computation.106 | convolution fusion | flops 9729736704 | bytes 29896704 | tf_op jit(solution)/shard_map/rd,fd->rf/dot_general | solution.py:156
  733.2 15.0 fusion.145
  748.3 15.0 convolution_convert_fusion
  763.4 195.1 %reduce-scatter.15.cloned.1.call-done = f32[512,1536]{1,0:T(8,128)} async-done(((f32[2048,1536]{1,0:T(8,128)}), f32[512,1536]{1,0:T(8,128)}) %reduce-scatter.15.cloned.1.call-update) | async-done | bytes 3145744 | tf_op jit(solution)/shard_map/reduce_scatter | solution.py:162
  964.2 108.8 %reduce-scatter.13.cloned.1.call-done = bf16[512,1536]{1,0:T(8,128)(2,1)} async-done(((bf16[2048,1536]{1,0:T(8,128)(2,1)}), bf16[512,1536]{1,0:T(8,128)(2,1)}) %reduce-scatter.13.cloned.1.call-update) | async-done | bytes 1572880 | tf_op jit(solution)/shard_map/reduce_scatter | solution.py:145
  1081.3 15.5 fusion.147
  1096.8 15.7 fusion.148
  1117.5 79.7 %all-gather.15.cloned.1.call-done = bf16[2048,1536]{1,0:T(8,128)(2,1)} async-done(((bf16[512,1536]{1,0:T(8,128)(2,1)}), bf16[2048,1536]{1,0:T(8,128)(2,1)}) %all-gather.15.cloned.1.call-update) | async-done | bytes 6291472 | tf_op jit(solution)/shard_map/all_gather | solution.py:171
  1213.8 8.4 fusion.146
  1226.3 138.1 %while.30 = (s32[]{:T(128)}, bf16[2,1024,3,128]{1,3,2,0:T(8,128)(2,1)}, bf16[2,1024,3,128]{1,3,2,0:T(8,128)(2,1)}, bf16[2,1024,3,128]{1,3,2,0:T(8,128)(2,1)}, bf...) while((s32[]{:T(128)}, ...), condition=%wide.region_15.16_spmd.clone.clone.clone, body=%wide.region_13.15_spmd.clone.clone.clone.sunk | while | flops 4116127744 | bytes 255438448 | solution.py:209
  1245.4 22.3 %fusion.210 = f32[1024,3,128]{0,2,1:T(8,128)} fusion(f32[3,1024,1024]{1,2,0:T(8,128)} %fusion.207, f32[3,1024,1024]{1,2,0:T(8,128)} %copy-done.1, f32[3,1024]{1,0:T(4,128)S(1)} %dynamic-slice_bitcast_fusion.2, pred[1024,1024]{0,1:T(8,128)(4,1)} %copy-done.6, bf16[2,1024,3,128]{3,1,2,0:T(8,128)(2,1)} %get-tuple-element.553, s32[]{:T(128)S(6)} %copy.174), kind=kOutput, calls=%fused_computation.48.clone.1 | convolution fusion | flops 839913472 | bytes 54820868 | tf_op jit(solution)/shard_map/while/body/eval_jaxpr/hqk,khd->qhd/dot_general | solution.py:192
  1267.7 21.6 %fusion.209 = f32[1024,3,128]{0,2,1:T(8,128)} fusion(f32[3,1024,1024]{1,2,0:T(8,128)} %fusion.207, f32[3,1024,1024]{1,2,0:T(8,128)} %copy-done.1, f32[3,1024]{1,0:T(4,128)S(1)} %dynamic-slice_bitcast_fusion.2, pred[1024,1024]{0,1:T(8,128)(4,1)} %copy-done.6, bf16[2,1024,3,128]{3,1,2,0:T(8,128)(2,1)} %get-tuple-element.554, s32[]{:T(128)S(6)} %copy.174), kind=kOutput, calls=%fused_computation.49.clone.1 | convolution fusion | flops 839913472 | bytes 54820868 | tf_op jit(solution)/shard_map/while/body/eval_jaxpr/hqk,qhd->khd/dot_general | solution.py:195
  1314.7 22.1 %fusion.210 = f32[1024,3,128]{0,2,1:T(8,128)} fusion(f32[3,1024,1024]{1,2,0:T(8,128)} %fusion.207, f32[3,1024,1024]{1,2,0:T(8,128)} %copy-done.1, f32[3,1024]{1,0:T(4,128)S(1)} %dynamic-slice_bitcast_fusion.2, pred[1024,1024]{0,1:T(8,128)(4,1)} %copy-done.6, bf16[2,1024,3,128]{3,1,2,0:T(8,128)(2,1)} %get-tuple-element.553, s32[]{:T(128)S(6)} %copy.174), kind=kOutput, calls=%fused_computation.48.clone.1 | convolution fusion | flops 839913472 | bytes 54820868 | tf_op jit(solution)/shard_map/while/body/eval_jaxpr/hqk,khd->qhd/dot_general | solution.py:192
  1336.8 22.3 %fusion.209 = f32[1024,3,128]{0,2,1:T(8,128)} fusion(f32[3,1024,1024]{1,2,0:T(8,128)} %fusion.207, f32[3,1024,1024]{1,2,0:T(8,128)} %copy-done.1, f32[3,1024]{1,0:T(4,128)S(1)} %dynamic-slice_bitcast_fusion.2, pred[1024,1024]{0,1:T(8,128)(4,1)} %copy-done.6, bf16[2,1024,3,128]{3,1,2,0:T(8,128)(2,1)} %get-tuple-element.554, s32[]{:T(128)S(6)} %copy.174), kind=kOutput, calls=%fused_computation.49.clone.1 | convolution fusion | flops 839913472 | bytes 54820868 | tf_op jit(solution)/shard_map/while/body/eval_jaxpr/hqk,qhd->khd/dot_general | solution.py:195
  1398.0 9.9 fusion.125
  1407.9 10.7 copy.146
  1432.3 13.4 bitcast_convert_fusion
  1445.8 44.6 %reduce-scatter.25.cloned.1.call-done = f32[192,1152]{1,0:T(8,128)} async-done(((f32[1536,1152]{1,0:T(8,128)}), f32[192,1152]{1,0:T(8,128)}) %reduce-scatter.25.cloned.1.call-update) | async-done | bytes 884752
  1494.6 37.1 %all-gather.21.cloned.1.call-done = bf16[1536,1536]{0,1:T(8,128)(2,1)} async-done(((bf16[1536,192]{0,1:T(8,128)(2,1)}), bf16[1536,1536]{0,1:T(8,128)(2,1)}) %all-gather.21.cloned.1.call-update) | async-done | bytes 4718608 | tf_op jit(solution)/shard_map/all_gather | solution.py:64
  1539.1 33.4 %all-gather.23.cloned.1.call-done = bf16[1536,1536]{0,1:T(8,128)(2,1)} async-done(((bf16[1536,192]{0,1:T(8,128)(2,1)}), bf16[1536,1536]{0,1:T(8,128)(2,1)}) %all-gather.23.cloned.1.call-update) | async-done | bytes 4718608 | tf_op jit(solution)/shard_map/all_gather | solution.py:67
  1579.9 18.4 %all-gather.19.cloned.1.call-done = bf16[384,1536]{0,1:T(8,128)(2,1)} async-done(((bf16[384,192]{0,1:T(8,128)(2,1)}), bf16[384,1536]{0,1:T(8,128)(2,1)}) %all-gather.19.cloned.1.call-update) | async-done | bytes 1179664 | tf_op jit(solution)/shard_map/all_gather | solution.py:67
  1601.1 110.2 %reduce-scatter.17.cloned.1.call-done = bf16[512,1536]{1,0:T(8,128)(2,1)} async-done(((bf16[2048,1536]{1,0:T(8,128)(2,1)}), bf16[512,1536]{1,0:T(8,128)(2,1)}) %reduce-scatter.17.cloned.1.call-update) | async-done | bytes 1572880 | tf_op jit(solution)/shard_map/reduce_scatter | solution.py:218
  1717.6 42.0 %all-reduce = (f32[1536]{0:T(1024)}, f32[1536]{0:T(1024)}, f32[1536]{0:T(1024)}, f32[1536]{0:T(1024)}) all-reduce(f32[1536]{0:T(1024)} %get-tuple-element.316, f32[1536]{0:T(1024)} %get-tuple-element.319, f32[1536]{0:T(1024)} %get-tuple-element.314, f32[1536]{0:T(1024)} %get-tuple-element.318), channel_id=1, replica_groups=mesh['dp'=8,'tensor'=4] {'dp','tensor'}, use_global_device_ids=true, to_apply=%region_20.21 | all-reduce | flops 6144 | bytes 49152 | tf_op jit(solution)/shard_map/psum | solution.py:228
  (243 shorter events, 295.7 us)
Async XLA Ops:
  7.2 125.1 %copy-start = (bf16[3,1536,384]{2,1,0:T(8,128)(2,1)S(1)}, bf16[3,1536,384]{2,1,0:T(8,128)(2,1)}, u32[]{:S(2)}) copy-start(bf16[3,1536,384]{2,1,0:T(8,128)(2,1)} %param.19) | copy-start | bytes 10616836
  7.2 125.1 %all-gather.9.cloned.1.call-start = ((), (), s32[]{:S(2)}) async-start(), calls=%async_computation.8 | async-start | bytes 7864320 | tf_op jit(solution)/shard_map/all_gather | solution.py:98
  14.1 456.9 %reduce-scatter.11.cloned.1.call-start = ((), (), s32[]{:S(2)}) async-start(), calls=%async_computation.9 | async-start | bytes 15728640 | tf_op jit(solution)/shard_map/reduce_scatter | solution.py:124
  205.8 7.5 copy-start.18
  205.8 7.5 copy-start.21
  213.3 8.2 copy-start.24
  232.0 7.5 copy-start.18
  232.0 7.5 copy-start.21
  239.5 8.2 copy-start.24
  260.8 333.0 %all-gather.11.cloned.1.call-start = ((), (), s32[]{:S(2)}) async-start(), calls=%async_computation.10 | async-start | bytes 7864320 | tf_op jit(solution)/shard_map/all_gather | solution.py:133
  477.2 231.6 %all-gather.13.cloned.1.call-start = ((), (), s32[]{:S(2)}) async-start(), calls=%async_computation.12 | async-start | bytes 7864320 | tf_op jit(solution)/shard_map/all_gather | solution.py:152
  477.7 480.7 %reduce-scatter.15.cloned.1.call-start = ((), (), s32[]{:S(2)}) async-start(), calls=%async_computation.13 | async-start | bytes 15728640 | tf_op jit(solution)/shard_map/reduce_scatter | solution.py:162
  748.2 324.8 %reduce-scatter.13.cloned.1.call-start = ((), (), s32[]{:S(2)}) async-start(), calls=%async_computation.11 | async-start | bytes 7864320 | tf_op jit(solution)/shard_map/reduce_scatter | solution.py:145
  763.4 433.9 %all-gather.15.cloned.1.call-start = ((), (), s32[]{:S(2)}) async-start(), calls=%async_computation.14 | async-start | bytes 7864320 | tf_op jit(solution)/shard_map/all_gather | solution.py:171
  1073.0 6.6 copy-start.10
  1081.2 344.8 %reduce-scatter.21.cloned.1.call-start = ((), (), s32[]{:S(2)}) async-start(), calls=%async_computation.19 | async-start | bytes 10616832 | tf_op jit(solution)/shard_map/reduce_scatter | solution.py:60
  1096.8 331.5 %reduce-scatter.23.cloned.1.call-start = ((), (), s32[]{:S(2)}) async-start(), calls=%async_computation.21 | async-start | bytes 10616832 | tf_op jit(solution)/shard_map/reduce_scatter | solution.py:61
  1112.5 318.0 %reduce-scatter.19.cloned.1.call-start = ((), (), s32[]{:S(2)}) async-start(), calls=%async_computation.17 | async-start | bytes 2654208 | tf_op jit(solution)/shard_map/reduce_scatter | solution.py:61
  1222.2 268.2 %reduce-scatter.25.cloned.1.call-start = ((), (), s32[]{:S(2)}) async-start(), calls=%async_computation.23 | async-start | bytes 7962624
  1233.6 5.4 copy-start.1
  1233.6 5.4 copy-start.7
  1302.6 5.7 copy-start.1
  1302.6 5.7 copy-start.7
  1392.4 5.6 copy-start.40
  1426.0 105.7 %all-gather.21.cloned.1.call-start = ((), (), s32[]{:S(2)}) async-start(), calls=%async_computation.20 | async-start | bytes 5308416 | tf_op jit(solution)/shard_map/all_gather | solution.py:64
  1428.2 144.3 %all-gather.23.cloned.1.call-start = ((), (), s32[]{:S(2)}) async-start(), calls=%async_computation.22 | async-start | bytes 5308416 | tf_op jit(solution)/shard_map/all_gather | solution.py:67
  1430.5 167.9 %all-gather.19.cloned.1.call-start = ((), (), s32[]{:S(2)}) async-start(), calls=%async_computation.18 | async-start | bytes 1327104 | tf_op jit(solution)/shard_map/all_gather | solution.py:67
  1432.3 279.0 %reduce-scatter.17.cloned.1.call-start = ((), (), s32[]{:S(2)}) async-start(), calls=%async_computation.15 | async-start | bytes 7864320 | tf_op jit(solution)/shard_map/reduce_scatter | solution.py:218
  1445.8 319.5 %all-gather.17.cloned.1.call-start = ((), (), s32[]{:S(2)}) async-start(), calls=%async_computation.16 | async-start | bytes 3981312 | tf_op jit(solution)/shard_map/all_gather | solution.py:64
  1579.9 131.4 %copy-start.27 = (f32[1536]{0:T(1024)S(1)}, f32[1536]{0:T(1024)}, u32[]{:S(2)}) copy-start(f32[1536]{0:T(1024)} %param.17) | copy-start | bytes 18436
  1579.9 131.4 %copy-start.30 = (f32[512]{0:T(512)S(1)}, f32[512]{0:T(512)}, u32[]{:S(2)}) copy-start(f32[512]{0:T(512)} %copy-done.29) | copy-start | bytes 6148
  1579.9 135.5 %copy-start.32 = (f32[512]{0:T(512)S(1)}, f32[512]{0:T(512)}, u32[]{:S(2)}) copy-start(f32[512]{0:T(512)} %copy-done.31) | copy-start | bytes 6148
  (39 other events, 95.0 us)
Sparse Core Ops, SparseCore 0:
  14.2 118.0 all-gather.8
  260.9 210.0 reduce-scatter.10
  477.3 116.4 all-gather.10
  595.1 113.5 all-gather.12
  748.4 210.0 reduce-scatter.14
  961.2 111.7 reduce-scatter.12
  1081.3 115.8 all-gather.14
  1201.3 74.6 reduce-scatter.20
  1279.5 76.4 reduce-scatter.22
  1359.9 42.4 reduce-scatter.18
  1426.1 64.3 reduce-scatter.24
  1492.8 38.8 all-gather.20
  1533.6 38.9 all-gather.22
  1574.3 24.0 all-gather.18
  1600.5 110.7 reduce-scatter.16
  1713.6 34.9 all-gather.16
where the time goes:
time: 1790 us; the launch traced here: 1780 us
  waiting for transfers between devices  1160 us (65%)
  matrix products  309 us (17%)
  local copies, waits for them, and re-layouts  157 us (9%)
  other arithmetic  87.7 us (5%)
  blocking collectives  42 us (2%)
    reduce_scatter x1, waiting for transfers between devices, shards(): lax.psum_scatter(jnp.dot(attn_flat, w_out, preferred_element_type=jnp.flo...  210 us
    reduce_scatter x1, waiting for transfers between devices, shards(): lax.psum_scatter(jnp.einsum('rf,df->rd', grad_pre, w_up, preferred_elemen...  195 us
    all_gather x1, waiting for transfers between devices, shards(): lax.all_gather(normed_one.astype(jnp.bfloat16), 'tensor', axis=0, tiled=T...  116 us
    all_gather x1, waiting for transfers between devices, shards(): gathered_two = lax.all_gather(normed_low, 'tensor', axis=0, tiled=True)  115 us
    reduce_scatter x1, waiting for transfers between devices, shards(): lax.psum_scatter(jnp.einsum('cre,cde->rd', grad_proj, w_qkv, preferred_el...  110 us
    reduce_scatter x1, waiting for transfers between devices, shards(): lax.psum_scatter(jnp.dot(hidden_flat, w_down, preferred_element_type=jnp....  109 us
    all_gather x1, waiting for transfers between devices, shards(): grad_rows = lax.all_gather(cotangent, 'tensor', axis=0, tiled=True)  95.9 us
    all_gather x1, waiting for transfers between devices, shards(): lax.all_gather(grad_resid.astype(jnp.bfloat16), 'tensor', axis=0, tiled=T...  79.7 us
  transfers between devices with their start and end apart: 16, of which 12 were waited for; matrix products, arithmetic and copies ran while one was open for 20% of the time, Pallas kernels for 0%

commit v1 on v0

v1 whole, which is shorter than its diff:
```python
import functools
import math

import jax
import jax.numpy as jnp
from jax import lax
from jax.experimental import pallas as pl
from jax.experimental.pallas import tpu as pltpu
from jax.sharding import PartitionSpec as P

HD = 128
FF = 6144
EPS = 1e-05
AXES = ("dp", "tensor")
BF = jnp.bfloat16
F32 = jnp.float32
LOG2E = 1.4426950408889634
VMEM_LIMIT = 56 * 1024 * 1024


def swap(value, dp_bits, tensor_bits):
    dp_size = lax.axis_size("dp")
    tensor_size = lax.axis_size("tensor")
    pairs = [
        (d * tensor_size + t, (d ^ dp_bits) * tensor_size + (t ^ tensor_bits))
        for d in range(dp_size)
        for t in range(tensor_size)
    ]
    return lax.ppermute(value, AXES, pairs)


def fetch(weight):
    dp_size = lax.axis_size("dp")
    rows = weight.shape[0] // dp_size
    piece = lax.dynamic_slice_in_dim(weight, lax.axis_index("dp") * rows, rows, 0)
    return lax.all_gather(swap(piece, 0, 2), "dp", axis=0, tiled=True)


def scatter_step(value, bit):
    side = (lax.axis_index("dp") >> bit) & 1
    rows = value.shape[1] // 2
    keep = lax.dynamic_slice_in_dim(value, side * rows, rows, 1)
    send = lax.dynamic_slice_in_dim(value, (1 - side) * rows, rows, 1)
    return (keep.astype(F32) + swap(send, 1 << bit, 0).astype(F32)).astype(BF)


def settle(pair, order):
    for bit in order:
        pair = scatter_step(pair, bit)
    piece = (pair[0].astype(F32) + swap(pair[1], 0, 2).astype(F32)).astype(BF)
    whole = lax.all_gather(piece, "dp", axis=0, tiled=True)
    count = len(order)
    blocks = whole.reshape((2,) * count + piece.shape)
    axes = [count - 1 - bit for bit in order] + [count, count + 1]
    return blocks.transpose(axes).reshape(whole.shape).astype(F32)


def rope_tables(length):
    half_dim = HD // 2
    frequency = jnp.exp(
        jnp.arange(half_dim, dtype=F32) * (-2.0 * math.log(10000.0) / HD)
    )
    angles = jnp.arange(length, dtype=F32)[:, None] * frequency[None, :]
    cos_part, sin_part = jnp.cos(angles), jnp.sin(angles)
    return (
        jnp.concatenate([cos_part, cos_part], axis=1),
        jnp.concatenate([-sin_part, sin_part], axis=1),
    )


def project_body(x_ref, w_ref, cos_ref, sin_ref, out_ref):
    result = jnp.dot(x_ref[...], w_ref[0], preferred_element_type=F32)
    which = pl.program_id(0)

    @pl.when(which < 2)
    def _():
        for h in range(result.shape[1] // HD):
            part = result[:, h * HD : (h + 1) * HD]
            turned = part * cos_ref[...] + pltpu.roll(part, HD // 2, 1) * sin_ref[...]
            out_ref[0, :, h * HD : (h + 1) * HD] = turned.astype(BF)

    @pl.when(which == 2)
    def _():
        out_ref[0] = result.astype(BF)


def project(rows, weight, tables):
    length, depth = rows.shape
    width = weight.shape[2]
    return pl.pallas_call(
        project_body,
        grid=(3,),
        in_specs=[
            pl.BlockSpec((length, depth), lambda c: (0, 0)),
            pl.BlockSpec((1, depth, width), lambda c: (c, 0, 0)),
            pl.BlockSpec((length, HD), lambda c: (0, 0)),
            pl.BlockSpec((length, HD), lambda c: (0, 0)),
        ],
        out_specs=pl.BlockSpec((1, length, width), lambda c: (c, 0, 0)),
        out_shape=jax.ShapeDtypeStruct((3, length, width), BF),
        compiler_params=pltpu.CompilerParams(vmem_limit_bytes=VMEM_LIMIT),
        cost_estimate=pl.CostEstimate(
            flops=6 * length * depth * width,
            bytes_accessed=2 * (length * depth + 3 * depth * width + 3 * length * width),
            transcendentals=0,
        ),
    )(rows, weight, *tables)


QB = 256
NT = (((1,), (1,)), ((), ()))
TN = (((0,), (0,)), ((), ()))


def mm(a, b, dims=(((1,), (0,)), ((), ()))):
    return lax.dot_general(a, b, dims, preferred_element_type=F32)


def probs_t(q, k, first):
    scores = mm(k, q, NT)
    size = scores.shape[0]
    key_at = lax.broadcasted_iota(jnp.int32, scores.shape, 0)
    row_at = lax.broadcasted_iota(jnp.int32, scores.shape, 1) + first
    scores = jnp.where(key_at <= row_at, scores, -1e30)
    top = jnp.max(scores, axis=0, keepdims=True)
    scale = HD ** (-0.5) * LOG2E
    weights = jnp.exp2((scores - top) * scale)
    total = jnp.sum(weights, axis=0, keepdims=True)
    return weights, 1.0 / total


def attend_body(q_ref, k_ref, v_ref, out_ref):
    length = q_ref.shape[1]
    for first in range(0, length, QB):
        last = first + QB
        q = q_ref[0, first:last]
        weights, inverse = probs_t(q, k_ref[0, :last], first)
        blended = mm(v_ref[0, :last], (weights * inverse).astype(BF), TN)
        out_ref[first:last, :] = blended.T.astype(BF)


def attend(qkv):
    _, length, width = qkv.shape
    heads = width // HD
    spec = lambda c: pl.BlockSpec((1, length, HD), lambda h: (c, 0, h))
    return pl.pallas_call(
        attend_body,
        grid=(heads,),
        in_specs=[spec(0), spec(1), spec(2)],
        out_specs=pl.BlockSpec((length, HD), lambda h: (0, h)),
        out_shape=jax.ShapeDtypeStruct((length, width), BF),
        compiler_params=pltpu.CompilerParams(vmem_limit_bytes=VMEM_LIMIT),
        cost_estimate=pl.CostEstimate(
            flops=8 * length * length * width,
            bytes_accessed=8 * length * width,
            transcendentals=heads * length * length,
        ),
    )(qkv, qkv, qkv)


def back_body(q_ref, k_ref, v_ref, g_ref, cos_ref, sin_ref, out_ref, dk_ref, dv_ref):
    length = q_ref.shape[1]

    def unturn(grads, cos_part, sin_part):
        return (grads * cos_part - pltpu.roll(grads, HD // 2, 1) * sin_part).astype(BF)

    for first in reversed(range(0, length, QB)):
        last = first + QB
        q = q_ref[0, first:last]
        g = g_ref[first:last]
        k = k_ref[0, :last]
        v = v_ref[0, :last]
        weights, inverse = probs_t(q, k, first)
        probs = weights * inverse
        grad_probs = mm(v, g, NT)
        inner = jnp.sum(probs * grad_probs, axis=0, keepdims=True)
        grad_scores = (probs * (grad_probs - inner) * HD ** (-0.5)).astype(BF)
        grad_v = mm(probs.astype(BF), g)
        grad_k = mm(grad_scores, q)
        if last == length:
            dv_ref[...] = grad_v
            dk_ref[...] = grad_k
        else:
            dv_ref[:last] += grad_v
            dk_ref[:last] += grad_k
        grad_q = mm(grad_scores, k, TN)
        out_ref[0, first:last] = unturn(grad_q, cos_ref[first:last], sin_ref[first:last])
    out_ref[1] = unturn(dk_ref[...], cos_ref[...], sin_ref[...])
    out_ref[2] = dv_ref[...].astype(BF)


def attend_back(qkv, grads, tables):
    _, length, width = qkv.shape
    heads = width // HD
    spec = lambda c: pl.BlockSpec((1, length, HD), lambda h: (c, 0, h))
    table = pl.BlockSpec((length, HD), lambda h: (0, 0))
    return pl.pallas_call(
        back_body,
        grid=(heads,),
        in_specs=[
            spec(0),
            spec(1),
            spec(2),
            pl.BlockSpec((length, HD), lambda h: (0, h)),
            table,
            table,
        ],
        out_specs=pl.BlockSpec((3, length, HD), lambda h: (0, 0, h)),
        out_shape=jax.ShapeDtypeStruct((3, length, width), BF),
        scratch_shapes=[pltpu.VMEM((length, HD), F32), pltpu.VMEM((length, HD), F32)],
        compiler_params=pltpu.CompilerParams(vmem_limit_bytes=VMEM_LIMIT),
        cost_estimate=pl.CostEstimate(
            flops=20 * length * length * width,
            bytes_accessed=14 * length * width,
            transcendentals=heads * length * length,
        ),
    )(qkv, qkv, qkv, grads, *tables)


def norm_stats(values):
    center = values - jnp.mean(values, axis=-1, keepdims=True)
    spread = jnp.mean(center * center, axis=-1, keepdims=True)
    inverse = lax.rsqrt(spread + EPS)
    return center * inverse, inverse


def norm_back(grads, normal, inverse, gain):
    scaled = grads * gain
    mean_one = jnp.mean(scaled, axis=-1, keepdims=True)
    mean_two = jnp.mean(scaled * normal, axis=-1, keepdims=True)
    return (
        inverse * (scaled - mean_one - normal * mean_two),
        jnp.sum(grads * normal, axis=0),
        jnp.sum(grads, axis=0),
    )


def gelu_pair(v):
    c = math.sqrt(2.0 / math.pi)
    square = v * v
    t = jnp.tanh(c * v * (1.0 + 0.044715 * square))
    half = 0.5 * (1.0 + t)
    slope = half + 0.5 * v * (1.0 - t * t) * (c * (1.0 + 3.0 * 0.044715 * square))
    return v * half, slope


def shards(
    tokens,
    granularity,
    gain_one,
    shift_one,
    w_qkv,
    w_out,
    gain_two,
    shift_two,
    w_up,
    w_down,
    cotangent,
):
    tensor_size = lax.axis_size("tensor")
    dp_size = lax.axis_size("dp")
    rank = lax.axis_index("tensor")
    local_rows, depth = tokens.shape
    seq_len = local_rows * tensor_size // granularity.shape[0]
    assert tensor_size == 4 and seq_len == 2 * local_rows
    half = local_rows // 2
    hidden_here = w_up.shape[1]
    head_width = w_qkv.shape[2]
    odd = rank % 2
    tables = rope_tables(seq_len)
    dp_bits = [b for b in range(dp_size.bit_length() - 1)]
    other_bits = [0, 2, 1] + dp_bits[3:]

    def in_place(own, other):
        return jnp.where(
            odd == 0,
            jnp.concatenate([own, other], axis=0),
            jnp.concatenate([other, own], axis=0),
        )

    def own_rows(full):
        return lax.dynamic_slice_in_dim(full, odd * local_rows, local_rows, 0)

    def partner_rows(full):
        return lax.dynamic_slice_in_dim(full, (1 - odd) * local_rows, local_rows, 0)

    tokens_wide = tokens.astype(F32)
    normal_one, inverse_one = norm_stats(tokens_wide)
    normed_one = (normal_one * gain_one + shift_one).astype(BF)
    rows_one = in_place(normed_one, swap(normed_one, 0, 1))

    w_qkv_far = fetch(w_qkv.reshape(3 * depth, head_width)).reshape(w_qkv.shape)
    w_out_far = fetch(w_out)
    w_up_far = fetch(w_up)
    w_down_far = fetch(w_down)
    grad_rows = jnp.concatenate(
        [cotangent, swap(cotangent[:half], 0, 1), swap(cotangent[half:], 0, 3)], axis=0
    )

    qkv_near = project(rows_one, w_qkv, tables)
    att_near = attend(qkv_near)
    qkv_far = project(rows_one, w_qkv_far, tables)
    att_far = attend(qkv_far)

    def out_rows(pick):
        return mm(pick(att_near), w_out) + mm(pick(att_far), w_out_far)

    leaving = out_rows(partner_rows).astype(BF)
    arrived_b = swap(leaving[half:], 0, 1)
    arrived_a = swap(leaving[:half], 0, 1)
    staying = out_rows(own_rows)
    resid = tokens_wide + staying + jnp.concatenate([arrived_a, arrived_b], axis=0).astype(F32)

    normal_two, inverse_two = norm_stats(resid)
    normed_two = (normal_two * gain_two + shift_two).astype(BF)
    rows_two = jnp.concatenate(
        [normed_two, swap(normed_two[:half], 0, 1), swap(normed_two[half:], 0, 3)], axis=0
    )
    limits = jnp.left_shift(jnp.ones_like(granularity), granularity) * (FF // 8)
    near_limit = jnp.where(rank < 2, limits[0], limits[1])
    away_limit = jnp.where(rank < 2, limits[1], limits[0])
    row_limit = jnp.where(jnp.arange(4 * half) < 3 * half, near_limit, away_limit)[:, None]
    unit = jnp.arange(hidden_here, dtype=jnp.int32)[None, :]

    def feed(w_up_one, w_down_one, place):
        mask = (unit + place * hidden_here < row_limit).astype(F32)
        value, slope = gelu_pair(mm(rows_two, w_up_one))
        grad_hidden = mm(grad_rows, w_down_one, NT)
        return (value * mask).astype(BF), (grad_hidden * mask * slope).astype(BF)

    hidden_near, pre_near = feed(w_up, w_down, rank)
    hidden_far, pre_far = feed(w_up_far, w_down_far, rank ^ 2)

    def back_two(lo, hi):
        return mm(pre_near[lo:hi], w_up, NT) + mm(pre_far[lo:hi], w_up_far, NT)

    def down(lo, hi):
        return mm(hidden_near[lo:hi], w_down) + mm(hidden_far[lo:hi], w_down_far)

    leave_two = back_two(2 * half, 4 * half).astype(BF)
    back_a = swap(leave_two[:half], 0, 1)
    back_b = swap(leave_two[half:], 0, 3)
    grad_two = back_two(0, 2 * half) + jnp.concatenate([back_a, back_b], axis=0).astype(F32)
    grad_resid, grad_gain_two, grad_shift_two = norm_back(
        grad_two, normal_two, inverse_two, gain_two
    )
    grad_resid = grad_resid + cotangent.astype(F32)
    grad_low = grad_resid.astype(BF)
    grad_full = in_place(grad_low, swap(grad_low, 0, 1))

    leave_out = down(2 * half, 4 * half).astype(BF)
    down_a = swap(leave_out[:half], 0, 1)
    down_b = swap(leave_out[half:], 0, 3)
    layer_out = resid + down(0, 2 * half) + jnp.concatenate([down_a, down_b], axis=0).astype(F32)
    layer_out = layer_out.astype(BF)

    up_pair = jnp.stack(
        [mm(rows_two, pre_near, TN).astype(BF), mm(rows_two, pre_far, TN).astype(BF)]
    )
    down_pair = jnp.stack(
        [mm(hidden_near, grad_rows, TN).astype(BF), mm(hidden_far, grad_rows, TN).astype(BF)]
    )
    grad_up = settle(up_pair, dp_bits)
    grad_down = settle(down_pair, other_bits)

    grad_att_near = mm(grad_full, w_out, NT).astype(BF)
    grad_att_far = mm(grad_full, w_out_far, NT).astype(BF)
    out_pair = jnp.stack(
        [mm(att_near, grad_full, TN).astype(BF), mm(att_far, grad_full, TN).astype(BF)]
    )
    grad_out = settle(out_pair, dp_bits)
    proj_near = attend_back(qkv_near, grad_att_near, tables)
    proj_far = attend_back(qkv_far, grad_att_far, tables)

    def back_one(offset):
        total = 0.0
        for proj, weight in ((proj_near, w_qkv), (proj_far, w_qkv_far)):
            for c in range(3):
                part = lax.dynamic_slice_in_dim(proj[c], offset, local_rows, 0)
                total = total + mm(part, weight[c], NT)
        return total

    leave_one = back_one((1 - odd) * local_rows).astype(BF)
    back_arrived = swap(leave_one, 0, 1)
    grad_one = back_one(odd * local_rows) + back_arrived.astype(F32)
    grad_local, grad_gain_one, grad_shift_one = norm_back(
        grad_one, normal_one, inverse_one, gain_one
    )
    grad_tokens = grad_resid + grad_local

    def qkv_grad(proj):
        return jnp.concatenate([mm(rows_one, proj[c], TN).astype(BF) for c in range(3)], axis=0)

    qkv_pair = jnp.stack([qkv_grad(proj_near), qkv_grad(proj_far)])
    grad_qkv = settle(qkv_pair, dp_bits).reshape(w_qkv.shape)

    gain_sums = lax.psum(
        jnp.stack([grad_gain_one, grad_shift_one, grad_gain_two, grad_shift_two]), AXES
    )
    return (
        layer_out,
        grad_tokens,
        gain_sums[0],
        gain_sums[1],
        grad_qkv,
        grad_out,
        gain_sums[2],
        gain_sums[3],
        grad_up,
        grad_down,
    )


def solution(mesh):
    rows = P(AXES, None)
    params = (P(), P(), P(None, None, "tensor"), P("tensor", None))
    wide = (P(None, "tensor"), P("tensor", None))
    return jax.shard_map(
        shards,
        mesh=mesh,
        in_specs=(rows, P("dp")) + params + (P(), P()) + wide + (rows,),
        out_specs=(rows, rows) + params + (P(), P()) + wide,
        check_vma=False,
    )
```

time: 1790 us -> 945 us (0.53)
  waiting for transfers between devices: 1160 us -> 477 us
  matrix products: 309 us -> 167 us
  local copies, waits for them, and re-layouts: 157 us -> 44 us
  Pallas kernels: 0 us -> 61.8 us
  starting transfers between devices: 0.66 us -> 45.8 us
    reduce_scatter x7 -> x0, waiting for transfers between devices: 624 us -> none  [the longest x1 210 us: shards(): lax.psum_scatter(jnp.dot(attn_flat, w_out, preferred_element_type=jnp.flo...]
    all_gather x8, waiting for transfers between devices: 495 us -> 0.01 us  [the longest x4 0.01 us: fetch(): return lax.all_gather(swap(piece, 0, 2), 'dp', axis=0, tiled=True)]
    ppermute x0 -> x33, waiting for transfers between devices: none -> 477 us  [swap(): return lax.ppermute(value, AXES, pairs)]
    dot_general x26 -> x42, matrix products: 309 us -> 167 us  [mm(): return lax.dot_general(a, b, dims, preferred_element_type=F32)]
    pallas_call x0 -> x6, Pallas kernels: none -> 61.8 us  [the longest x2 25.9 us: attend_back(): pl.pallas_call(back_body, grid=(heads,), in_specs=[spec(0), spec(1), spec...]
    unnamed x17 -> x8, waiting for transfers between devices: 45.4 us -> 0.13 us
    ppermute x0 -> x33, starting transfers between devices: none -> 45.2 us  [swap(): return lax.ppermute(value, AXES, pairs)]
    unnamed x69 -> x168, local copies, waits for them, and re-layouts: 60.4 us -> 17.4 us
  transfers between devices with their start and end apart: 16 -> 41, of which waited for: 12 -> 24; matrix products, arithmetic and copies ran while one was open for 20% -> 21% of each run, Pallas kernels for 0% -> 4%
where the time goes in v1:
time: 945 us; the launch traced here: 940 us
  waiting for transfers between devices  477 us (50%)
  matrix products  167 us (18%)
  other arithmetic  84.8 us (9%)
  Pallas kernels  61.8 us (7%)
  starting transfers between devices  45.8 us (5%)
  local copies, waits for them, and re-layouts  44 us (5%)
  blocking collectives  40.7 us (4%)
  between operations  18.6 us (2%)
    ppermute x33, waiting for transfers between devices, swap(): return lax.ppermute(value, AXES, pairs)  477 us
    dot_general x42, matrix products, mm(): return lax.dot_general(a, b, dims, preferred_element_type=F32)  167 us
    ppermute x33, starting transfers between devices, swap(): return lax.ppermute(value, AXES, pairs)  45.2 us
    psum x1, blocking collectives, shards(): lax.psum(jnp.stack([grad_gain_one, grad_shift_one, grad_gain_two, grad_sh...  40.7 us
    pallas_call x2, Pallas kernels, attend_back(): pl.pallas_call(back_body, grid=(heads,), in_specs=[spec(0), spec(1), spec...  25.9 us
    another operation x3, other arithmetic, shards(): qkv_pair = jnp.stack([qkv_grad(proj_near), qkv_grad(proj_far)])  22.3 us
    convert_element_type x12, other arithmetic, scatter_step(): return (keep.astype(F32) + swap(send, 1 << bit, 0).astype(F32)).astype(BF)  22.1 us
    pallas_call x2, Pallas kernels, project(): pl.pallas_call(project_body, grid=(3,), in_specs=[pl.BlockSpec((length, d...  19.5 us
  transfers between devices with their start and end apart: 41, of which 24 were waited for; matrix products, arithmetic and copies ran while one was open for 21% of the time, Pallas kernels for 4%

profile of v1, /device:TPU:0, one launch (start us, length us, event | category | flops | bytes accessed | tf_op | source)
XLA Modules:
  0.0 939.8 jit_solution(13837309806428468490)
XLA Ops:
  12.6 19.6 %collective-permute-done.1 = bf16[576,384]{1,0:T(8,128)(2,1)S(1)} collective-permute-done((bf16[576,384]{1,0:T(8,128)(2,1)S(1)}, bf16[576,384]{1,0:T(8,128)(2,1)S(1)}, u32[]{:S(2)}, u32[]{:S(2)}) %collective-permute-start.1) | collective-permute-done | bytes 442400 | tf_op jit(solution)/shard_map/ppermute | solution.py:29
  33.2 9.1 collective-permute-done.2
  44.3 23.8 %collective-permute-done.7 = bf16[192,1536]{1,0:T(8,128)(2,1)S(1)} collective-permute-done((bf16[192,1536]{1,0:T(8,128)(2,1)S(1)}, bf16[192,1536]{1,0:T(8,128)(2,1)S(1)}, u32[]{:S(2)}, u32[]{:S(2)}) %collective-permute-start.7) | collective-permute-done | bytes 589856 | tf_op jit(solution)/shard_map/ppermute | solution.py:29
  82.6 39.4 %collective-permute-done = bf16[512,1536]{1,0:T(8,128)(2,1)} collective-permute-done((bf16[512,1536]{1,0:T(8,128)(2,1)}, bf16[512,1536]{1,0:T(8,128)(2,1)}, u32[]{:S(2)}, u32[]{:S(2)}) %collective-permute-start) | collective-permute-done | bytes 1572896 | tf_op jit(solution)/shard_map/ppermute | solution.py:29
  126.7 9.8 %shard_map.186.q_ref.k_ref.v_ref = bf16[3,1024,384]{2,1,0:T(8,128)(2,1)} custom-call(bf16[1024,1536]{1,0:T(8,128)(2,1)} %maximum_select_fusion.x_ref, bf16[3,1536,384]{2,1,0:T(8,128)(2,1)} %w_ref.1, f32[1024,128]{1,0:T(8,128)} %get-tuple-element.52.cos_ref, f32[1024,128]{1,0:T(8,128)} %get-tuple-element.53.sin_ref), custom_call_target="tpu_custom_call" | custom-call | flops 3623878656 | bytes 9043968 | tf_op jit(solution)/shard_map/pallas_call | solution.py:90
  148.3 9.7 %shard_map.188.q_ref.k_ref.v_ref = bf16[3,1024,384]{2,1,0:T(8,128)(2,1)} custom-call(bf16[1024,1536]{1,0:T(8,128)(2,1)} %maximum_select_fusion.x_ref, bf16[3,1536,384]{2,1,0:T(8,128)(2,1)} %bitcast.174, f32[1024,128]{1,0:T(8,128)} %get-tuple-element.52.cos_ref, f32[1024,128]{1,0:T(8,128)} %get-tuple-element.53.sin_ref), custom_call_target="tpu_custom_call" | custom-call | flops 3623878656 | bytes 9043968 | tf_op jit(solution)/shard_map/pallas_call | solution.py:90
  179.3 11.9 %collective-permute-done.4 = bf16[256,1536]{1,0:T(8,128)(2,1)} collective-permute-done((bf16[256,1536]{1,0:T(8,128)(2,1)}, bf16[256,1536]{1,0:T(8,128)(2,1)}, u32[]{:S(2)}, u32[]{:S(2)}) %collective-permute-start.4) | collective-permute-done | bytes 786464 | tf_op jit(solution)/shard_map/ppermute | solution.py:29
  191.3 8.4 collective-permute-done.3
  215.0 15.8 %collective-permute-done.6 = bf16[256,1536]{1,0:T(8,128)(2,1)S(1)} collective-permute-done((bf16[256,1536]{1,0:T(8,128)(2,1)S(1)}, bf16[256,1536]{1,0:T(8,128)(2,1)S(1)}, u32[]{:S(2)}, u32[]{:S(2)}) %collective-permute-start.6) | collective-permute-done | bytes 786464 | tf_op jit(solution)/shard_map/ppermute | solution.py:29
  230.8 13.9 %collective-permute-done.5 = bf16[256,1536]{1,0:T(8,128)(2,1)S(1)} collective-permute-done((bf16[256,1536]{1,0:T(8,128)(2,1)S(1)}, bf16[256,1536]{1,0:T(8,128)(2,1)S(1)}, u32[]{:S(2)}, u32[]{:S(2)}) %collective-permute-start.5) | collective-permute-done | bytes 786464 | tf_op jit(solution)/shard_map/ppermute | solution.py:29
  250.7 8.8 fusion.6
  265.5 15.7 %fusion.7 = (bf16[1024,1536]{1,0:T(8,128)(2,1)}, bf16[1024,1536]{1,0:T(8,128)(2,1)}, f32[1024,1536]{1,0:T(8,128)}) fusion(s32[1536]{0:T(1024)S(1)} %iota_add_fusion, s32[1024]{0:T(1024)S(1)} %fusion.143, f32[1024,1536]{1,0:T(8,128)} %copy-done.73, s32[1536]{0:T(1024)S(1)} %iota_add_fusion.1, bf16[1536,1536]{1,0:T(8,128)(2,1)} %all-gather.13.cloned.1.call-done, ...), kind=kOutput, calls=%fused_computation.33 | convolution fusion | flops 4875878400 | bytes 26755072 | tf_op jit(solution)/shard_map/dot_general | solution.py:116
  281.3 12.2 %fusion.9 = bf16[1024,1536]{1,0:T(8,128)(2,1)S(1)} fusion(f32[1024,1536]{1,0:T(8,128)} %get-tuple-element.49, bf16[1024,1536]{1,0:T(8,128)(2,1)} %copy-done.38, bf16[1536,1536]{1,0:T(8,128)(2,1)} %all-gather.15.cloned.1.call-done, s32[1536]{0:T(1024)S(1)} %iota_add_fusion, s32[1024]{0:T(1024)S(1)} %fusion.143), kind=kOutput, calls=%fused_computation.35 | convolution fusion | flops 4863295488 | bytes 17311744 | tf_op jit(solution)/shard_map/dot_general | solution.py:116
  303.4 15.2 %collective-permute-done.14 = bf16[256,1536]{1,0:T(8,128)(2,1)S(1)} collective-permute-done((bf16[256,1536]{1,0:T(8,128)(2,1)S(1)}, bf16[256,1536]{1,0:T(8,128)(2,1)S(1)}, u32[]{:S(2)}, u32[]{:S(2)}) %collective-permute-start.14) | collective-permute-done | bytes 786464 | tf_op jit(solution)/shard_map/ppermute | solution.py:29
  318.6 14.2 %collective-permute-done.13 = bf16[256,1536]{1,0:T(8,128)(2,1)S(1)} collective-permute-done((bf16[256,1536]{1,0:T(8,128)(2,1)S(1)}, bf16[256,1536]{1,0:T(8,128)(2,1)S(1)}, u32[]{:S(2)}, u32[]{:S(2)}) %collective-permute-start.13) | collective-permute-done | bytes 786464 | tf_op jit(solution)/shard_map/ppermute | solution.py:29
  347.4 26.9 %collective-permute-done.15 = bf16[512,1536]{1,0:T(8,128)(2,1)S(1)} collective-permute-done((bf16[512,1536]{1,0:T(8,128)(2,1)}, bf16[512,1536]{1,0:T(8,128)(2,1)S(1)}, u32[]{:S(2)}, u32[]{:S(2)}) %collective-permute-start.15) | collective-permute-done | bytes 1572896 | tf_op jit(solution)/shard_map/ppermute | solution.py:29
  379.5 12.9 %shard_map.190 = bf16[3,1024,384]{2,1,0:T(8,128)(2,1)} custom-call(bf16[3,1024,384]{2,1,0:T(8,128)(2,1)} %shard_map.186.q_ref.k_ref.v_ref, bf16[3,1024,384]{2,1,0:T(8,128)(2,1)} %shard_map.186.q_ref.k_ref.v_ref, bf16[3,1024,384]{2,1,0:T(8,128)(2,1)} %shard_map.186.q_ref.k_ref.v_ref, bf16[1024,384]{1,0:T(8,128)(2,1)} %convolution_convert_fusion.13.g_ref, ...), custom_call_target="tpu_custom_call" | custom-call | flops 8053063680 | bytes 5505024 | tf_op jit(solution)/shard_map/pallas_call | solution.py:197
  405.9 13.0 %shard_map.191 = bf16[3,1024,384]{2,1,0:T(8,128)(2,1)} custom-call(bf16[3,1024,384]{2,1,0:T(8,128)(2,1)} %shard_map.188.q_ref.k_ref.v_ref, bf16[3,1024,384]{2,1,0:T(8,128)(2,1)} %shard_map.188.q_ref.k_ref.v_ref, bf16[3,1024,384]{2,1,0:T(8,128)(2,1)} %shard_map.188.q_ref.k_ref.v_ref, bf16[1024,384]{1,0:T(8,128)(2,1)} %convolution_convert_fusion.12.g_ref, ...), custom_call_target="tpu_custom_call" | custom-call | flops 8053063680 | bytes 5505024 | tf_op jit(solution)/shard_map/pallas_call | solution.py:197
  426.7 9.9 %maximum_bitcast_fusion = bf16[1,4608,384]{2,1,0:T(8,128)(2,1)S(1)} fusion(bf16[1536,384]{1,0:T(8,128)(2,1)S(1)} %convolution_convert_fusion.9, bf16[1536,384]{1,0:T(8,128)(2,1)S(1)} %convolution_convert_fusion.10, bf16[1536,384]{1,0:T(8,128)(2,1)S(1)} %copy-done.34), kind=kLoop, calls=%fused_computation.57 | loop fusion | flops 10616832 | bytes 7077888 | tf_op jit(solution)/shard_map/stack | solution.py:394
  436.6 10.2 %maximum_bitcast_fusion.1 = bf16[1,4608,384]{2,1,0:T(8,128)(2,1)S(1)} fusion(bf16[1536,384]{1,0:T(8,128)(2,1)S(1)} %convolution_convert_fusion.6, bf16[1536,384]{1,0:T(8,128)(2,1)S(1)} %convolution_convert_fusion.7, bf16[1536,384]{1,0:T(8,128)(2,1)S(1)} %convolution_convert_fusion.8), kind=kLoop, calls=%fused_computation.58 | loop fusion | flops 10616832 | bytes 7077888 | tf_op jit(solution)/shard_map/stack | solution.py:394
  473.2 11.1 %collective-permute-done.22 = bf16[2,96,1536]{2,1,0:T(8,128)(2,1)} collective-permute-done((bf16[2,96,1536]{2,1,0:T(8,128)(2,1)S(1)}, bf16[2,96,1536]{2,1,0:T(8,128)(2,1)}, u32[]{:S(2)}, u32[]{:S(2)}) %collective-permute-start.22) | collective-permute-done | bytes 589856 | tf_op jit(solution)/shard_map/ppermute | solution.py:29
  493.1 28.3 %collective-permute-done.18 = bf16[2,1152,384]{2,1,0:T(8,128)(2,1)} collective-permute-done((bf16[2,1152,384]{2,1,0:T(8,128)(2,1)S(1)}, bf16[2,1152,384]{2,1,0:T(8,128)(2,1)}, u32[]{:S(2)}, u32[]{:S(2)}) %collective-permute-start.18) | collective-permute-done | bytes 1769504 | tf_op jit(solution)/shard_map/ppermute | solution.py:29
  535.6 9.4 %collective-permute-done.19 = bf16[2,576,384]{2,1,0:T(8,128)(2,1)} collective-permute-done((bf16[2,576,384]{2,1,0:T(8,128)(2,1)S(1)}, bf16[2,576,384]{2,1,0:T(8,128)(2,1)}, u32[]{:S(2)}, u32[]{:S(2)}) %collective-permute-start.19) | collective-permute-done | bytes 884768 | tf_op jit(solution)/shard_map/ppermute | solution.py:29
  558.7 9.4 collective-permute-done.20
  586.2 37.3 %collective-permute-done.26 = bf16[2,384,1536]{2,1,0:T(8,128)(2,1)} collective-permute-done((bf16[2,384,1536]{2,1,0:T(8,128)(2,1)S(1)}, bf16[2,384,1536]{2,1,0:T(8,128)(2,1)}, u32[]{:S(2)}, u32[]{:S(2)}) %collective-permute-start.26) | collective-permute-done | bytes 2359328 | tf_op jit(solution)/shard_map/ppermute | solution.py:29
  628.1 24.3 %collective-permute-done.27 = bf16[2,192,1536]{2,1,0:T(8,128)(2,1)} collective-permute-done((bf16[2,192,1536]{2,1,0:T(8,128)(2,1)S(1)}, bf16[2,192,1536]{2,1,0:T(8,128)(2,1)}, u32[]{:S(2)}, u32[]{:S(2)}) %collective-permute-start.27) | collective-permute-done | bytes 1179680 | tf_op jit(solution)/shard_map/ppermute | solution.py:29
  657.9 24.4 %collective-permute-done.28 = bf16[192,1536]{1,0:T(8,128)(2,1)S(1)} collective-permute-done((bf16[192,1536]{1,0:T(8,128)(2,1)S(1)}, bf16[192,1536]{1,0:T(8,128)(2,1)S(1)}, u32[]{:S(2)}, u32[]{:S(2)}) %collective-permute-start.28) | collective-permute-done | bytes 589856 | tf_op jit(solution)/shard_map/ppermute | solution.py:29
  706.0 53.9 %collective-permute-done.30 = bf16[2,384,1536]{2,1,0:T(8,128)(2,1)S(1)} collective-permute-done((bf16[2,384,1536]{2,1,0:T(8,128)(2,1)S(1)}, bf16[2,384,1536]{2,1,0:T(8,128)(2,1)S(1)}, u32[]{:S(2)}, u32[]{:S(2)}) %collective-permute-start.30) | collective-permute-done | bytes 2359328 | tf_op jit(solution)/shard_map/ppermute | solution.py:29
  766.7 19.9 %collective-permute-done.31 = bf16[2,192,1536]{2,1,0:T(8,128)(2,1)S(1)} collective-permute-done((bf16[2,192,1536]{2,1,0:T(8,128)(2,1)S(1)}, bf16[2,192,1536]{2,1,0:T(8,128)(2,1)S(1)}, u32[]{:S(2)}, u32[]{:S(2)}) %collective-permute-start.31) | collective-permute-done | bytes 1179680 | tf_op jit(solution)/shard_map/ppermute | solution.py:29
  792.1 20.8 %collective-permute-done.32 = bf16[192,1536]{1,0:T(8,128)(2,1)S(1)} collective-permute-done((bf16[192,1536]{1,0:T(8,128)(2,1)S(1)}, bf16[192,1536]{1,0:T(8,128)(2,1)S(1)}, u32[]{:S(2)}, u32[]{:S(2)}) %collective-permute-start.32) | collective-permute-done | bytes 589856 | tf_op jit(solution)/shard_map/ppermute | solution.py:29
  829.0 27.5 %collective-permute-done.16 = bf16[512,1536]{1,0:T(8,128)(2,1)S(1)} collective-permute-done((bf16[512,1536]{1,0:T(8,128)(2,1)S(1)}, bf16[512,1536]{1,0:T(8,128)(2,1)S(1)}, u32[]{:S(2)}, u32[]{:S(2)}) %collective-permute-start.16) | collective-permute-done | bytes 1572896 | tf_op jit(solution)/shard_map/ppermute | solution.py:29
  859.9 40.7 %psum.7 = f32[4,1536]{1,0:T(4,128)S(1)} all-reduce(f32[4,1536]{1,0:T(4,128)S(1)} %pad_maximum_fusion.3), channel_id=1, replica_groups=mesh['dp'=8,'tensor'=4] {'dp','tensor'}, use_global_device_ids=true, to_apply=%region_12.13 | all-reduce | flops 6144 | bytes 49152 | tf_op jit(solution)/shard_map/psum | solution.py:397
  (363 shorter events, 313.7 us)
Async XLA Ops:
  7.2 141.1 %all-gather.9.cloned.1.call-start = ((), (), s32[]{:S(2)}) async-start(), calls=%async_computation | async-start | bytes 3981312 | tf_op jit(solution)/shard_map/all_gather | solution.py:36
  8.5 23.7 %collective-permute-start.1 = (bf16[576,384]{1,0:T(8,128)(2,1)S(1)}, bf16[576,384]{1,0:T(8,128)(2,1)S(1)}, u32[]{:S(2)}, u32[]{:S(2)}) collective-permute-start(bf16[576,384]{1,0:T(8,128)(2,1)S(1)} %constant_dynamic-slice_fusion.11), channel_id=1, source_target_pairs={{0,2},{1,3},{2,0},{3,1},{4,6},{5,7},{6,4},{7,5},{8,10},{9,11},{10,... | collective-permute-start | bytes 1327112 | tf_op jit(solution)/shard_map/ppermute | solution.py:29
  33.0 133.2 %all-gather.11.cloned.1.call-start = ((), (), s32[]{:S(2)}) async-start(), calls=%async_computation.1 | async-start | bytes 1327104 | tf_op jit(solution)/shard_map/all_gather | solution.py:36
  43.0 222.5 %all-gather.13.cloned.1.call-start = ((), (), s32[]{:S(2)}) async-start(), calls=%async_computation.2 | async-start | bytes 5308416 | tf_op jit(solution)/shard_map/all_gather | solution.py:36
  44.2 23.9 %collective-permute-start.7 = (bf16[192,1536]{1,0:T(8,128)(2,1)S(1)}, bf16[192,1536]{1,0:T(8,128)(2,1)S(1)}, u32[]{:S(2)}, u32[]{:S(2)}) collective-permute-start(bf16[192,1536]{1,0:T(8,128)(2,1)S(1)} %constant_dynamic-slice_fusion.9), channel_id=1, source_target_pairs={{0,2},{1,3},{2,0},{3,1},{4,6},{5,7},{6,4},{7,5},{8,10},{9,11},{10,... | collective-permute-start | bytes 1769480 | tf_op jit(solution)/shard_map/ppermute | solution.py:29
  68.9 212.3 %all-gather.15.cloned.1.call-start = ((), (), s32[]{:S(2)}) async-start(), calls=%async_computation.3 | async-start | bytes 5308416 | tf_op jit(solution)/shard_map/all_gather | solution.py:36
  71.7 50.3 %collective-permute-start = (bf16[512,1536]{1,0:T(8,128)(2,1)}, bf16[512,1536]{1,0:T(8,128)(2,1)}, u32[]{:S(2)}, u32[]{:S(2)}) collective-permute-start(bf16[512,1536]{1,0:T(8,128)(2,1)} %fusion.32), channel_id=1, source_target_pairs={{0,1},{1,0},{2,3},{3,2},{4,5},{5,4},{6,7},{7,6},{8,9},{9,8},{10,11... | collective-permute-start | bytes 4718600 | tf_op jit(solution)/shard_map/ppermute | solution.py:29
  73.6 102.5 %collective-permute-start.8 = (bf16[192,1536]{1,0:T(8,128)(2,1)}, bf16[192,1536]{1,0:T(8,128)(2,1)S(1)}, u32[]{:S(2)}, u32[]{:S(2)}) collective-permute-start(bf16[192,1536]{1,0:T(8,128)(2,1)} %constant_dynamic-slice_fusion.8), channel_id=1, source_target_pairs={{0,2},{1,3},{2,0},{3,1},{4,6},{5,7},{6,4},{7,5},{8,10},{9,11},{10,... | collective-permute-start | bytes 1769480 | tf_op jit(solution)/shard_map/ppermute | solution.py:29
  77.0 135.4 %collective-permute-start.11 = (bf16[256,1536]{1,0:T(8,128)(2,1)}, bf16[256,1536]{1,0:T(8,128)(2,1)}, u32[]{:S(2)}, u32[]{:S(2)}) collective-permute-start(bf16[256,1536]{1,0:T(8,128)(2,1)} %get-tuple-element.33), channel_id=1, source_target_pairs={{0,1},{1,0},{2,3},{3,2},{4,5},{5,4},{6,7},{7,6},{8,9},{9,8},{10,11... | collective-permute-start | bytes 2359304 | tf_op jit(solution)/shard_map/ppermute | solution.py:29
  77.0 136.6 %collective-permute-start.12 = (bf16[256,1536]{1,0:T(8,128)(2,1)}, bf16[256,1536]{1,0:T(8,128)(2,1)}, u32[]{:S(2)}, u32[]{:S(2)}) collective-permute-start(bf16[256,1536]{1,0:T(8,128)(2,1)} %get-tuple-element.32), channel_id=1, source_target_pairs={{0,3},{1,2},{2,1},{3,0},{4,7},{5,6},{6,5},{7,4},{8,11},{9,10},{10,... | collective-permute-start | bytes 2359304 | tf_op jit(solution)/shard_map/ppermute | solution.py:29
  170.9 28.9 %collective-permute-start.3 = (bf16[256,1536]{1,0:T(8,128)(2,1)}, bf16[256,1536]{1,0:T(8,128)(2,1)}, u32[]{:S(2)}, u32[]{:S(2)}) collective-permute-start(bf16[256,1536]{1,0:T(8,128)(2,1)} %get-tuple-element.38), channel_id=1, source_target_pairs={{0,1},{1,0},{2,3},{3,2},{4,5},{5,4},{6,7},{7,6},{8,9},{9,8},{10,11... | collective-permute-start | bytes 2359304 | tf_op jit(solution)/shard_map/ppermute | solution.py:29
  177.0 729.9 %all-gather.19.cloned.1.call-start = ((), (), s32[]{:S(2)}) async-start(), calls=%async_computation.5 | async-start | bytes 1327104 | tf_op jit(solution)/shard_map/all_gather | solution.py:51
  204.4 26.5 %collective-permute-start.6 = (bf16[256,1536]{1,0:T(8,128)(2,1)S(1)}, bf16[256,1536]{1,0:T(8,128)(2,1)S(1)}, u32[]{:S(2)}, u32[]{:S(2)}) collective-permute-start(bf16[256,1536]{1,0:T(8,128)(2,1)S(1)} %get-tuple-element.37), channel_id=1, source_target_pairs={{0,3},{1,2},{2,1},{3,0},{4,7},{5,6},{6,5},{7,4},{8,11},{9,10},{10,... | collective-permute-start | bytes 2359304 | tf_op jit(solution)/shard_map/ppermute | solution.py:29
  212.3 32.4 %collective-permute-start.5 = (bf16[256,1536]{1,0:T(8,128)(2,1)S(1)}, bf16[256,1536]{1,0:T(8,128)(2,1)S(1)}, u32[]{:S(2)}, u32[]{:S(2)}) collective-permute-start(bf16[256,1536]{1,0:T(8,128)(2,1)S(1)} %get-tuple-element.36), channel_id=1, source_target_pairs={{0,1},{1,0},{2,3},{3,2},{4,5},{5,4},{6,7},{7,6},{8,9},{9,8},{10,11... | collective-permute-start | bytes 2359304 | tf_op jit(solution)/shard_map/ppermute | solution.py:29
  296.3 22.3 %collective-permute-start.14 = (bf16[256,1536]{1,0:T(8,128)(2,1)S(1)}, bf16[256,1536]{1,0:T(8,128)(2,1)S(1)}, u32[]{:S(2)}, u32[]{:S(2)}) collective-permute-start(bf16[256,1536]{1,0:T(8,128)(2,1)S(1)} %get-tuple-element.31), channel_id=1, source_target_pairs={{0,3},{1,2},{2,1},{3,0},{4,7},{5,6},{6,5},{7,4},{8,11},{9,10},{10,... | collective-permute-start | bytes 2359304 | tf_op jit(solution)/shard_map/ppermute | solution.py:29
  298.0 34.7 %collective-permute-start.13 = (bf16[256,1536]{1,0:T(8,128)(2,1)S(1)}, bf16[256,1536]{1,0:T(8,128)(2,1)S(1)}, u32[]{:S(2)}, u32[]{:S(2)}) collective-permute-start(bf16[256,1536]{1,0:T(8,128)(2,1)S(1)} %get-tuple-element.30), channel_id=1, source_target_pairs={{0,1},{1,0},{2,3},{3,2},{4,5},{5,4},{6,7},{7,6},{8,9},{9,8},{10,11... | collective-permute-start | bytes 2359304 | tf_op jit(solution)/shard_map/ppermute | solution.py:29
  339.6 34.7 %collective-permute-start.15 = (bf16[512,1536]{1,0:T(8,128)(2,1)}, bf16[512,1536]{1,0:T(8,128)(2,1)S(1)}, u32[]{:S(2)}, u32[]{:S(2)}) collective-permute-start(bf16[512,1536]{1,0:T(8,128)(2,1)} %get-tuple-element.22), channel_id=1, source_target_pairs={{0,1},{1,0},{2,3},{3,2},{4,5},{5,4},{6,7},{7,6},{8,9},{9,8},{10,11... | collective-permute-start | bytes 4718600 | tf_op jit(solution)/shard_map/ppermute | solution.py:29
  467.2 82.6 %collective-permute-start.25 = (bf16[2,768,1536]{2,1,0:T(8,128)(2,1)}, bf16[2,768,1536]{2,1,0:T(8,128)(2,1)}, u32[]{:S(2)}, u32[]{:S(2)}) collective-permute-start(bf16[2,768,1536]{2,1,0:T(8,128)(2,1)} %fusion.12), channel_id=1, source_target_pairs={{0,4},{1,5},{2,6},{3,7},{4,0},{5,1},{6,2},{7,3},{8,12},{9,13},{10,... | collective-permute-start | bytes 14155784 | tf_op jit(solution)/shard_map/ppermute | solution.py:29
  472.2 49.2 %collective-permute-start.18 = (bf16[2,1152,384]{2,1,0:T(8,128)(2,1)S(1)}, bf16[2,1152,384]{2,1,0:T(8,128)(2,1)}, u32[]{:S(2)}, u32[]{:S(2)}) collective-permute-start(bf16[2,1152,384]{2,1,0:T(8,128)(2,1)S(1)} %constant_dynamic-slice_fusion.7), channel_id=1, source_target_pairs={{0,8},{1,9},{2,10},{3,11},{4,12},{5,13},{6,14},{7,15},{8,0},{9,1},... | collective-permute-start | bytes 5308424 | tf_op jit(solution)/shard_map/ppermute | solution.py:29
  535.6 374.5 %all-gather.17.cloned.1.call-start = ((), (), s32[]{:S(2)}) async-start(), calls=%async_computation.4 | async-start | bytes 3981312 | tf_op jit(solution)/shard_map/all_gather | solution.py:51
  557.3 66.2 %collective-permute-start.26 = (bf16[2,384,1536]{2,1,0:T(8,128)(2,1)S(1)}, bf16[2,384,1536]{2,1,0:T(8,128)(2,1)}, u32[]{:S(2)}, u32[]{:S(2)}) collective-permute-start(bf16[2,384,1536]{2,1,0:T(8,128)(2,1)S(1)} %constant_dynamic-slice_fusion.3), channel_id=1, source_target_pairs={{0,8},{1,9},{2,10},{3,11},{4,12},{5,13},{6,14},{7,15},{8,0},{9,1},... | collective-permute-start | bytes 7077896 | tf_op jit(solution)/shard_map/ppermute | solution.py:29
  569.0 347.0 %all-gather.21.cloned.1.call-start = ((), (), s32[]{:S(2)}) async-start(), calls=%async_computation.6 | async-start | bytes 5308416 | tf_op jit(solution)/shard_map/all_gather | solution.py:51
  586.2 97.1 %collective-permute-start.29 = (bf16[2,768,1536]{2,1,0:T(8,128)(2,1)}, bf16[2,768,1536]{2,1,0:T(8,128)(2,1)}, u32[]{:S(2)}, u32[]{:S(2)}) collective-permute-start(bf16[2,768,1536]{2,1,0:T(8,128)(2,1)} %fusion.10), channel_id=1, source_target_pairs={{0,4},{1,5},{2,6},{3,7},{4,0},{5,1},{6,2},{7,3},{8,12},{9,13},{10,... | collective-permute-start | bytes 14155784 | tf_op jit(solution)/shard_map/ppermute | solution.py:29
  626.6 25.8 %collective-permute-start.27 = (bf16[2,192,1536]{2,1,0:T(8,128)(2,1)S(1)}, bf16[2,192,1536]{2,1,0:T(8,128)(2,1)}, u32[]{:S(2)}, u32[]{:S(2)}) collective-permute-start(bf16[2,192,1536]{2,1,0:T(8,128)(2,1)S(1)} %constant_dynamic-slice_fusion.2), channel_id=1, source_target_pairs={{0,16},{1,17},{2,18},{3,19},{4,20},{5,21},{6,22},{7,23},{8,24},{9,... | collective-permute-start | bytes 3538952 | tf_op jit(solution)/shard_map/ppermute | solution.py:29
  654.0 28.3 %collective-permute-start.28 = (bf16[192,1536]{1,0:T(8,128)(2,1)S(1)}, bf16[192,1536]{1,0:T(8,128)(2,1)S(1)}, u32[]{:S(2)}, u32[]{:S(2)}) collective-permute-start(bf16[192,1536]{1,0:T(8,128)(2,1)S(1)} %slice_bitcast_fusion.2), channel_id=1, source_target_pairs={{0,2},{1,3},{2,0},{3,1},{4,6},{5,7},{6,4},{7,5},{8,10},{9,11},{10,... | collective-permute-start | bytes 1769480 | tf_op jit(solution)/shard_map/ppermute | solution.py:29
  683.2 241.0 %all-gather.23.cloned.1.call-start = ((), (), s32[]{:S(2)}) async-start(), calls=%async_computation.7 | async-start | bytes 5308416 | tf_op jit(solution)/shard_map/all_gather | solution.py:51
  688.7 71.2 %collective-permute-start.30 = (bf16[2,384,1536]{2,1,0:T(8,128)(2,1)S(1)}, bf16[2,384,1536]{2,1,0:T(8,128)(2,1)S(1)}, u32[]{:S(2)}, u32[]{:S(2)}) collective-permute-start(bf16[2,384,1536]{2,1,0:T(8,128)(2,1)S(1)} %constant_dynamic-slice_fusion.1), channel_id=1, source_target_pairs={{0,16},{1,17},{2,18},{3,19},{4,20},{5,21},{6,22},{7,23},{8,24},{9,... | collective-permute-start | bytes 7077896 | tf_op jit(solution)/shard_map/ppermute | solution.py:29
  698.0 63.0 %collective-permute-start.10 = (bf16[256,1536]{1,0:T(8,128)(2,1)S(1)}, bf16[256,1536]{1,0:T(8,128)(2,1)S(1)}, u32[]{:S(2)}, u32[]{:S(2)}) collective-permute-start(bf16[256,1536]{1,0:T(8,128)(2,1)S(1)} %get-tuple-element.35), channel_id=1, source_target_pairs={{0,3},{1,2},{2,1},{3,0},{4,7},{5,6},{6,5},{7,4},{8,11},{9,10},{10,... | collective-permute-start | bytes 2359304 | tf_op jit(solution)/shard_map/ppermute | solution.py:29
  701.6 59.3 %collective-permute-start.9 = (bf16[256,1536]{1,0:T(8,128)(2,1)S(1)}, bf16[256,1536]{1,0:T(8,128)(2,1)S(1)}, u32[]{:S(2)}, u32[]{:S(2)}) collective-permute-start(bf16[256,1536]{1,0:T(8,128)(2,1)S(1)} %get-tuple-element.34), channel_id=1, source_target_pairs={{0,1},{1,0},{2,3},{3,2},{4,5},{5,4},{6,7},{7,6},{8,9},{9,8},{10,11... | collective-permute-start | bytes 2359304 | tf_op jit(solution)/shard_map/ppermute | solution.py:29
  760.6 26.0 %collective-permute-start.31 = (bf16[2,192,1536]{2,1,0:T(8,128)(2,1)S(1)}, bf16[2,192,1536]{2,1,0:T(8,128)(2,1)S(1)}, u32[]{:S(2)}, u32[]{:S(2)}) collective-permute-start(bf16[2,192,1536]{2,1,0:T(8,128)(2,1)S(1)} %constant_dynamic-slice_fusion), channel_id=1, source_target_pairs={{0,8},{1,9},{2,10},{3,11},{4,12},{5,13},{6,14},{7,15},{8,0},{9,1},... | collective-permute-start | bytes 3538952 | tf_op jit(solution)/shard_map/ppermute | solution.py:29
  786.9 26.0 %collective-permute-start.32 = (bf16[192,1536]{1,0:T(8,128)(2,1)S(1)}, bf16[192,1536]{1,0:T(8,128)(2,1)S(1)}, u32[]{:S(2)}, u32[]{:S(2)}) collective-permute-start(bf16[192,1536]{1,0:T(8,128)(2,1)S(1)} %slice_bitcast_fusion), channel_id=1, source_target_pairs={{0,2},{1,3},{2,0},{3,1},{4,6},{5,7},{6,4},{7,5},{8,10},{9,11},{10,... | collective-permute-start | bytes 1769480 | tf_op jit(solution)/shard_map/ppermute | solution.py:29
  823.5 33.0 %collective-permute-start.16 = (bf16[512,1536]{1,0:T(8,128)(2,1)S(1)}, bf16[512,1536]{1,0:T(8,128)(2,1)S(1)}, u32[]{:S(2)}, u32[]{:S(2)}) collective-permute-start(bf16[512,1536]{1,0:T(8,128)(2,1)S(1)} %fusion.43), channel_id=1, source_target_pairs={{0,1},{1,0},{2,3},{3,2},{4,5},{5,4},{6,7},{7,6},{8,9},{9,8},{10,11... | collective-permute-start | bytes 4718600 | tf_op jit(solution)/shard_map/ppermute | solution.py:29
  (92 other events, 1397.5 us)
Sparse Core Ops, SparseCore 0:
  33.2 35.1 all-gather.8
  70.2 24.0 all-gather.10
  96.2 38.9 all-gather.12
  177.1 37.3 all-gather.14
  535.7 24.7 all-gather.18
  569.1 48.6 all-gather.16
  683.3 57.6 all-gather.20
  814.1 35.9 all-gather.22

commit v2 on v0

v2 whole, which is shorter than its diff:
```python
import functools
import math

import jax
import jax.numpy as jnp
import numpy as np
from jax import lax
from jax.experimental import pallas as pl
from jax.experimental.pallas import tpu as pltpu
from jax.sharding import PartitionSpec as P

HD = 128
FF = 6144
EPS = 1e-05
AXES = ("dp", "tensor")
BF = jnp.bfloat16
F32 = jnp.float32
LOG2E = 1.4426950408889634
LONG = 200_000_000_000
VMEM_LIMIT = 56 * 1024 * 1024

ODD, SIDE, LIMIT, NEAR_UNIT, FAR_UNIT = 0, 1, 4, 5, 6

NN = (((1,), (0,)), ((), ()))
NT = (((1,), (1,)), ((), ()))
TN = (((0,), (0,)), ((), ()))


def mm(a, b, dims=NN):
    return lax.dot_general(a, b, dims, preferred_element_type=F32)


def swap(value, dp_bits, tensor_bits):
    dp_size = lax.axis_size("dp")
    tensor_size = lax.axis_size("tensor")
    pairs = [
        (d * tensor_size + t, (d ^ dp_bits) * tensor_size + (t ^ tensor_bits))
        for d in range(dp_size)
        for t in range(tensor_size)
    ]
    return lax.ppermute(value, AXES, pairs)


class Chain:
    def __init__(self):
        self.last = None

    def __call__(self, call, *args):
        if self.last is not None:
            leaves, tree = jax.tree.flatten(args)
            leaves = lax.optimization_barrier(tuple(leaves) + (self.last,))[:-1]
            args = jax.tree.unflatten(tree, leaves)
        out = call(*args)
        self.last = jax.tree.leaves(out)[0]
        return out

    def wait(self, *args):
        return self(lambda *v: v[0] if len(v) == 1 else v, *args)


def dp_piece(weight):
    rows = weight.shape[0] // lax.axis_size("dp")
    return lax.dynamic_slice_in_dim(weight, lax.axis_index("dp") * rows, rows, 0)


def from_all(piece):
    return lax.all_gather(piece, "dp", axis=0, tiled=True)


def block(shape, index=None):
    if index is None:
        return pl.BlockSpec(shape, lambda *_: (0,) * len(shape))
    return pl.BlockSpec(shape, index)


def shape_of(shape, kind=BF):
    return jax.ShapeDtypeStruct(shape, kind)


def kernel(body, grid, ins, outs, shapes, scratch=(), aliases=None, cost=1):
    return pl.pallas_call(
        body,
        grid_spec=pltpu.PrefetchScalarGridSpec(
            num_scalar_prefetch=1,
            grid=grid,
            in_specs=ins,
            out_specs=outs,
            scratch_shapes=list(scratch),
        ),
        out_shape=shapes,
        input_output_aliases=aliases or {},
        compiler_params=pltpu.CompilerParams(vmem_limit_bytes=VMEM_LIMIT),
        cost_estimate=pl.CostEstimate(flops=cost, bytes_accessed=1, transcendentals=0),
    )


def rows_at(start, size):
    return pl.ds(pl.multiple_of(start, size), size)


def norm_stats(values):
    center = values - jnp.mean(values, axis=-1, keepdims=True)
    spread = jnp.mean(center * center, axis=-1, keepdims=True)
    inverse = lax.rsqrt(spread + EPS)
    return center * inverse, inverse


def norm_back(grads, normal, inverse, gain):
    scaled = grads * gain
    mean_one = jnp.mean(scaled, axis=-1, keepdims=True)
    mean_two = jnp.mean(scaled * normal, axis=-1, keepdims=True)
    return (
        inverse * (scaled - mean_one - normal * mean_two),
        jnp.sum(grads * normal, axis=0, keepdims=True),
        jnp.sum(grads, axis=0, keepdims=True),
    )


def first_norm(place, tokens, gain, shift):
    rows, depth = tokens.shape
    half = rows // 2

    def body(_, x, gain, shift, low, high):
        normal, _ = norm_stats(x[...].astype(F32))
        value = (normal * gain[...] + shift[...]).astype(BF)
        pl.when(pl.program_id(0) == 0)(lambda: low.__setitem__(..., value))
        pl.when(pl.program_id(0) == 1)(lambda: high.__setitem__(..., value))

    return kernel(
        body,
        (2,),
        [block((half, depth), lambda i, _: (i, 0))] + [block((1, depth))] * 2,
        [block((half, depth))] * 2,
        [shape_of((half, depth))] * 2,
    )(place, tokens, gain, shift)


def rope_tables(length):
    frequency = np.exp(
        np.arange(HD // 2, dtype=np.float32) * np.float32(-2.0 * math.log(10000.0) / HD)
    ).astype(np.float32)
    angles = (np.arange(length, dtype=np.float32)[:, None] * frequency[None, :]).astype(np.float64)
    cos_part, sin_part = np.cos(angles), np.sin(angles)
    return (
        np.concatenate([cos_part, cos_part], axis=1).astype(np.float32),
        np.concatenate([-sin_part, sin_part], axis=1).astype(np.float32),
    )


def project(place, own, other, weight, tables):
    part, depth = own[0].shape
    width = weight.shape[2]

    def body(p, ol, oh, tl, th, weight, cos, sin, out):
        def go(source):
            x = source[...]
            for c in range(3):
                result = mm(x, weight[c])
                if c == 2:
                    out[c] = result.astype(BF)
                    continue
                for h in range(width // HD):
                    one = result[:, h * HD : (h + 1) * HD]
                    turned = one * cos[...] + pltpu.roll(one, HD // 2, 1) * sin[...]
                    out[c, :, h * HD : (h + 1) * HD] = turned.astype(BF)

        step = pl.program_id(0)
        at = jnp.where(step // 2 == p[ODD], 0, 2) + step % 2
        for i, source in enumerate((ol, oh, tl, th)):
            pl.when(at == i)(functools.partial(go, source))

    table = block((part, HD), lambda i, _: (i, 0))
    return kernel(
        body,
        (4,),
        [block((part, depth))] * 4 + [block((3, depth, width)), table, table],
        block((3, part, width), lambda i, _: (0, i, 0)),
        shape_of((3, 4 * part, width)),
    )(place, *own, *other, weight, *tables)


QB = 256


def probs_t(q, k, first):
    scores = mm(k, q, NT)
    key_at = lax.broadcasted_iota(jnp.int32, scores.shape, 0)
    row_at = lax.broadcasted_iota(jnp.int32, scores.shape, 1) + first
    scores = jnp.where(key_at <= row_at, scores, -1e30)
    top = jnp.max(scores, axis=0, keepdims=True)
    weights = jnp.exp2((scores - top) * (HD ** (-0.5) * LOG2E))
    return weights, 1.0 / jnp.sum(weights, axis=0, keepdims=True)


def attend(place, qkv):
    _, length, width = qkv.shape

    def body(_, q_ref, k_ref, v_ref, out_ref):
        for first in range(0, length, QB):
            last = first + QB
            weights, inverse = probs_t(q_ref[0, first:last], k_ref[0, :last], first)
            blended = mm(v_ref[0, :last], (weights * inverse).astype(BF), TN)
            out_ref[first:last, :] = blended.T.astype(BF)

    spec = lambda c: block((1, length, HD), lambda h, _: (c, 0, h))
    return kernel(
        body,
        (width // HD,),
        [spec(0), spec(1), spec(2)],
        block((length, HD), lambda h, _: (0, h)),
        shape_of((length, width)),
    )(place, qkv, qkv, qkv)


def attend_back(place, cost, qkv, own, other, w_out, tables):
    _, length, width = qkv.shape
    depth = w_out.shape[1]
    part = length // 4

    def unturn(grads, cos, sin):
        return (grads * cos - pltpu.roll(grads, HD // 2, 1) * sin).astype(BF)

    def body(p, q_ref, k_ref, v_ref, ol, oh, tl, th, w_ref, cos, sin, out, g_ref, dk_ref, dv_ref):
        for base, low, high in ((p[ODD] * 2, ol, oh), ((1 - p[ODD]) * 2, tl, th)):
            g_ref[rows_at(base * part, part)] = mm(low[...], w_ref[...], NT).astype(BF)
            g_ref[rows_at((base + 1) * part, part)] = mm(high[...], w_ref[...], NT).astype(BF)
        for first in reversed(range(0, length, QB)):
            last = first + QB
            q = q_ref[0, first:last]
            g = g_ref[first:last]
            k = k_ref[0, :last]
            weights, inverse = probs_t(q, k, first)
            probs = weights * inverse
            grad_probs = mm(v_ref[0, :last], g, NT)
            inner = jnp.sum(probs * grad_probs, axis=0, keepdims=True)
            grad_scores = (probs * (grad_probs - inner) * HD ** (-0.5)).astype(BF)
            grad_v = mm(probs.astype(BF), g)
            grad_k = mm(grad_scores, q)
            if last == length:
                dv_ref[...] = grad_v
                dk_ref[...] = grad_k
            else:
                dv_ref[:last] += grad_v
                dk_ref[:last] += grad_k
            grad_q = mm(grad_scores, k, TN)
            out[0, first:last] = unturn(grad_q, cos[first:last], sin[first:last])
        out[1] = unturn(dk_ref[...], cos[...], sin[...])
        out[2] = dv_ref[...].astype(BF)

    spec = lambda c: block((1, length, HD), lambda h, _: (c, 0, h))
    piece = block((part, depth))
    table = block((length, HD))
    return kernel(
        body,
        (width // HD,),
        [spec(0), spec(1), spec(2)]
        + [piece] * 4
        + [block((HD, depth), lambda h, _: (h, 0)), table, table],
        block((3, length, HD), lambda h, _: (0, 0, h)),
        shape_of((3, length, width)),
        [pltpu.VMEM((length, HD), BF), pltpu.VMEM((length, HD), F32), pltpu.VMEM((length, HD), F32)],
        cost=cost,
    )(place, qkv, qkv, qkv, *own, *other, w_out, *tables)


def head_rows(place, leave, near, far, w_near, w_far):
    length, width = near.shape
    depth = w_near.shape[1]
    half = length // 4
    kind = BF if leave else F32
    cols = depth // 3

    def body(_, near, far, w_near, w_far, low, high):
        total = mm(near[...], w_near[...]) + mm(far[...], w_far[...])
        low[...] = total[:half].astype(kind)
        high[...] = total[half:].astype(kind)

    rows = block((2 * half, width), lambda i, p: (1 - p[ODD] if leave else p[ODD], 0))
    weight = block((width, cols), lambda i, p: (0, i))
    return kernel(
        body,
        (3,),
        [rows, rows, weight, weight],
        [block((half, cols), lambda i, p: (0, i))] * 2,
        [shape_of((half, depth), kind)] * 2,
    )(place, near, far, w_near, w_far)


def second_norm(place, which, stay, tokens, arrived, gain, shift):
    half, depth = stay.shape
    size = half // 2

    def body(_, stay, tokens, arrived, gain, shift, normed, resid):
        total = tokens[...].astype(F32) + stay[...] + arrived[...].astype(F32)
        resid[...] = total
        normal, _ = norm_stats(total)
        normed[...] = (normal * gain[...] + shift[...]).astype(BF)

    piece = block((size, depth), lambda i, _: (i, 0))
    return kernel(
        body,
        (2,),
        [piece, block((size, depth), lambda i, _: (2 * which + i, 0)), piece]
        + [block((1, depth))] * 2,
        [piece] * 2,
        [shape_of((half, depth)), shape_of((half, depth), F32)],
    )(place, stay, tokens, arrived, gain, shift)


def gelu_pair(v):
    c = math.sqrt(2.0 / math.pi)
    square = v * v
    t = jnp.tanh(v * (c + (c * 0.044715) * square))
    half = 0.5 + 0.5 * t
    slope = half + v * (0.5 - 0.5 * t * t) * (c + (3.0 * 0.044715 * c) * square)
    return v * half, slope


UB = 768
SB = 256


def feed(group, place, normed, normed_far, cot, cot_far, weights, kept=()):
    half, depth = normed.shape
    size = 2 * half
    units = weights[0].shape[1]
    near_steps = units // UB

    def body(p, own, other, g_own, g_other, un, dn, uf, df, *refs):
        hn, pn, hf, pf, rows, grads, stay, leave, total = refs[-9:]
        step = pl.program_id(0)

        @pl.when(step == 0)
        def _():
            total[...] = jnp.zeros_like(total)
            rows[:half] = own[...]
            rows[half:] = other[...]
            grads[:half] = g_own[...]
            grads[half:] = g_other[...]

        def work(up, down, hidden, pre):
            for at in range(0, UB, SB):
                there = slice(at, at + SB)
                value, slope = gelu_pair(mm(rows[...], up[:, there]))
                hidden[:, there] = value.astype(BF)
                grad = mm(grads[...], down[there], NT)
                pre[:, there] = (grad * slope).astype(BF)
            total[...] += mm(pre[...], up[...], NT)

        def part(first_unit, up, down, hidden, pre):
            live = first_unit < p[LIMIT]

            @pl.when(live)
            def _():
                work(up, down, hidden, pre)

            @pl.when(jnp.logical_not(live))
            def _():
                hidden[...] = jnp.zeros((size, UB), BF)
                pre[...] = jnp.zeros((size, UB), BF)

        @pl.when(step < near_steps)
        def _():
            part(p[NEAR_UNIT] + step * UB, un, dn, hn, pn)

        @pl.when(step >= near_steps)
        def _():
            part(p[FAR_UNIT] + (step - near_steps) * UB, uf, df, hf, pf)

        @pl.when(step == 2 * near_steps - 1)
        def _():
            stay[...] = total[:half]
            leave[...] = total[half:].astype(BF)

    near = lambda j: jnp.minimum(j, near_steps - 1)
    far = lambda j: jnp.maximum(j - near_steps, 0)
    ups = [block((depth, UB), lambda j, _, at=at: (0, at(j))) for at in (near, far)]
    downs = [block((UB, depth), lambda j, _, at=at: (at(j), 0)) for at in (near, far)]
    wide = [block((size, UB), lambda j, _, at=at: (group, at(j))) for at in (near, far)]
    piece = block((half, depth))
    rows = block((size, depth), lambda j, _: (group, 0))
    return kernel(
        body,
        (2 * near_steps,),
        [piece, piece, block((half, depth), lambda j, _: (1 - group, 0)), piece]
        + [ups[0], downs[0], ups[1], downs[1]]
        + [pl.BlockSpec(memory_space=pl.ANY)] * len(kept),
        [wide[0], wide[0], wide[1], wide[1], rows, rows, piece, piece],
        [shape_of((2 * size, units))] * 4
        + [shape_of((2 * size, depth))] * 2
        + [shape_of((half, depth), F32), shape_of((half, depth))],
        [pltpu.VMEM((size, depth), F32)],
        {9 + i: i for i in range(len(kept))},
    )(place, normed, normed_far, cot, cot_far, *weights, *kept)


def second_back(place, which, resid, stay, arrived, cot, gain):
    half, depth = resid.shape
    size = half // 2

    def body(_, resid, stay, arrived, cot, gain, low, wide, gain_sum, shift_sum):
        normal, inverse = norm_stats(resid[...])
        grad, gains, shifts = norm_back(
            stay[...] + arrived[...].astype(F32), normal, inverse, gain[...]
        )
        grad = grad + cot[...].astype(F32)
        wide[...] = grad
        low[...] = grad.astype(BF)

        @pl.when(pl.program_id(0) == 0)
        def _():
            gain_sum[...] = gains
            shift_sum[...] = shifts

        @pl.when(pl.program_id(0) > 0)
        def _():
            gain_sum[...] += gains
            shift_sum[...] += shifts

    piece = block((size, depth), lambda i, _: (i, 0))
    vector = block((1, depth))
    return kernel(
        body,
        (2,),
        [piece] * 3 + [block((size, depth), lambda i, _: (2 * which + i, 0)), vector],
        [piece, piece, vector, vector],
        [shape_of((half, depth)), shape_of((half, depth), F32)] + [shape_of((1, depth), F32)] * 2,
    )(place, resid, stay, arrived, cot, gain)


def down_rows(place, near, far, w_near, w_far, resid_high, resid_low):
    rows, units = near.shape
    depth = w_near.shape[1]
    half = rows // 4
    cols = depth // 3

    def body(_, near, far, w_near, w_far, resid_high, resid_low, high, low, out_high, out_low):
        for i, (stay, resid, leave) in enumerate(
            ((out_high, resid_high, high), (out_low, resid_low, low))
        ):
            here = slice(2 * i * half, 2 * (i + 1) * half)
            total = mm(near[here], w_near[...]) + mm(far[here], w_far[...])
            stay[...] = total[:half] + resid[...]
            leave[...] = total[half:].astype(BF)

    hidden = block((rows, units))
    weight = block((units, cols), lambda j, _: (0, j))
    piece = block((half, cols), lambda j, _: (0, j))
    return kernel(
        body,
        (3,),
        [hidden, hidden, weight, weight, piece, piece],
        [piece] * 4,
        [shape_of((half, depth))] * 2 + [shape_of((half, depth), F32)] * 2,
    )(place, near, far, w_near, w_far, resid_high, resid_low)


def layer_rows(place, out_low, out_high, low, high):
    half, depth = low.shape

    def body(_, out_low, out_high, low, high, out):
        out[:half] = (out_low[...] + low[...].astype(F32)).astype(BF)
        out[half:] = (out_high[...] + high[...].astype(F32)).astype(BF)

    piece = block((half, depth))
    return kernel(body, (1,), [piece] * 4, block((2 * half, depth)), shape_of((2 * half, depth)))(
        place, out_low, out_high, low, high
    )


def wide_grad(place, bit, lefts, rights, arrived=None):
    rows, width = lefts[0].shape
    depth = rights[0].shape[1]
    half = width // 2
    cols = depth // 3
    last = arrived is not None

    def body(p, l0, l1, r0, r1, *refs):
        turned = refs[-1]
        shard = pl.program_id(0)

        @pl.when(pl.program_id(1) == 0)
        def _():
            pl.when(shard == 0)(lambda: turned.__setitem__(..., l0[...].T))
            pl.when(shard == 1)(lambda: turned.__setitem__(..., l1[...].T))

        def go(right):
            if not last:
                refs[0][0, 0] = mm(turned[...], right[...]).astype(BF)
                return
            for out, side in ((refs[1], p[SIDE + bit]), (refs[2], 1 - p[SIDE + bit])):
                here = rows_at(side * (half // 2), half // 2)
                value = mm(turned[here], right[...]) + refs[0][0, 0, here].astype(F32)
                out[0, 0] = value.astype(BF)

        pl.when(shard == 0)(lambda: go(r0))
        pl.when(shard == 1)(lambda: go(r1))

    side = lambda p: p[SIDE] if last else 1 - p[SIDE]
    left = block((rows, half), lambda s, j, p: (0, side(p)))
    right = lambda shard: block(
        (rows, cols), lambda s, j, p: (0, jnp.where(s == shard, j, 2 * (1 - shard)))
    )
    tall = lambda size: block((1, 1, size, cols), lambda s, j, p: (s, 0, 0, j))
    if last:
        outs = [tall(half // 2)] * 2
        shapes = [shape_of((2, 1, half // 2, depth))] * 2
    else:
        outs, shapes = tall(half), shape_of((2, 1, half, depth))
    return kernel(
        body,
        (2, 3),
        [left, left, right(0), right(1)] + [tall(half)] * last,
        outs,
        shapes,
        [pltpu.VMEM((half, rows), BF)],
    )(place, *lefts, *rights, *([arrived] if last else []))


def narrow_grad(place, bit, first, total, own, other, nears, fars, arrived=None, kept=()):
    rows, depth = own[0].shape
    parts = len(own)
    count, length, width = nears.shape
    half = depth // 2
    last = arrived is not None
    n_out = 2 if last else 1

    def body(p, *refs):
        own, other = refs[:parts], refs[parts : 2 * parts]
        near, far = refs[2 * parts : 2 * parts + 2]
        arrived, outs, turned = refs[2 * parts + 2], refs[-1 - n_out : -1], refs[-1]
        shard = pl.program_id(0)

        @pl.when((shard == 0) & (pl.program_id(1) == 0))
        def _():
            for lefts, base in ((own, p[ODD]), (other, 1 - p[ODD])):
                for i, left in enumerate(lefts):
                    turned[:, rows_at((base * parts + i) * rows, rows)] = left[...].T

        def go(right):
            if not last:
                outs[0][0, 0] = mm(turned[...], right[0]).astype(BF)
                return
            for out, side in ((outs[0], p[SIDE + bit]), (outs[1], 1 - p[SIDE + bit])):
                here = rows_at(side * (half // 2), half // 2)
                value = mm(turned[here], right[0]) + arrived[0, 0, here].astype(F32)
                out[0, 0] = value.astype(BF)

        pl.when(shard == 0)(lambda: go(near))
        pl.when(shard == 1)(lambda: go(far))

    side = lambda p: p[SIDE] if last else 1 - p[SIDE]
    left = block((rows, half), lambda s, c, p: (0, side(p)))
    right = lambda shard: block(
        (1, length, width),
        lambda s, c, p: (jnp.where(s == shard, c, (count - 1) * (1 - shard)), 0, 0),
    )
    tall = lambda size: block((1, 1, size, width), lambda s, c, p: (s, first + c, 0, 0))
    size = half // 2 if last else half
    ins = [left] * (2 * parts) + [right(0), right(1)] + [tall(half)] * last
    return kernel(
        body,
        (2, count),
        ins + [pl.BlockSpec(memory_space=pl.ANY)] * len(kept),
        [tall(size)] * n_out,
        [shape_of((2, total, size, width))] * n_out,
        [pltpu.VMEM((half, length), BF)],
        {1 + len(ins) + i: i for i in range(len(kept))},
    )(place, *own, *other, nears, fars, *([arrived] if last else []), *kept)


def add_split(place, bit, keep, arrived):
    _, count, rows, width = keep.shape
    half = rows // 2

    def body(p, mine, theirs, keep, send):
        here = rows_at(p[SIDE + bit] * half, half)
        there = rows_at((1 - p[SIDE + bit]) * half, half)
        keep[0, 0] = (mine[0, 0, here].astype(F32) + theirs[0, 0, here].astype(F32)).astype(BF)
        send[0, 0] = (mine[0, 0, there].astype(F32) + theirs[0, 0, there].astype(F32)).astype(BF)

    full = block((1, 1, rows, width), lambda s, c, p: (s, c, 0, 0))
    out = block((1, 1, half, width), lambda s, c, p: (s, c, 0, 0))
    return kernel(
        body, (2, count), [full, full], [out, out], [shape_of((2, count, half, width))] * 2
    )(place, keep, arrived)


def add_last(place, keep, arrived):
    _, count, rows, width = keep.shape

    def body(_, mine, theirs, near, far):
        near[...] = (mine[0].astype(F32) + theirs[0].astype(F32)).astype(BF)
        far[...] = (mine[1].astype(F32) + theirs[1].astype(F32)).astype(BF)

    full = block((2, 1, rows, width), lambda c, p: (0, c, 0, 0))
    out = block((1, rows, width), lambda c, p: (c, 0, 0))
    return kernel(
        body, (count,), [full, full], [out, out], [shape_of((count, rows, width))] * 2
    )(place, keep, arrived)


def add_pair(place, near, arrived):
    count, rows, width = near.shape

    def body(_, mine, theirs, out):
        out[...] = (mine[...].astype(F32) + theirs[...].astype(F32)).astype(BF)

    full = block((1, rows, width), lambda c, p: (c, 0, 0))
    return kernel(body, (count,), [full, full], full, shape_of((count, rows, width)))(
        place, near, arrived
    )


def assemble(table, whole):
    size, count, rows, width = whole.shape

    def body(_, piece, out):
        out[...] = piece[0].astype(F32)

    return kernel(
        body,
        (size,),
        [block((1, count, rows, width), lambda j, t: (t[j], 0, 0, 0))],
        block((count, rows, width), lambda j, t: (0, j, 0)),
        shape_of((count, rows * size, width), F32),
    )(table, whole)


def assemble_heads(table, whole):
    size, count, rows, width = whole.shape

    def body(_, piece, out, last):
        out[...] = piece[0, : count - 1].astype(F32)
        last[pl.program_id(0)] = piece[0, count - 1].astype(F32).T

    out, last = kernel(
        body,
        (size,),
        [block((1, count, rows, width), lambda j, t: (t[j], 0, 0, 0))],
        [
            block((count - 1, rows, width), lambda j, t: (0, j, 0)),
            block((size, width, rows)),
        ],
        [shape_of((count - 1, rows * size, width), F32), shape_of((size, width, rows), F32)],
    )(table, whole)
    return out, last.transpose(1, 0, 2).reshape(width, rows * size)


def back_rows(place, leave, near, far, w_near, w_far):
    count, length, width = near.shape
    depth = w_near.shape[1]
    rows = length // 2
    cols = depth // 3
    kind = BF if leave else F32

    def body(_, near, far, w_near, w_far, out):
        for lo in range(0, rows, rows // 2):
            here = slice(lo, lo + rows // 2)
            total = mm(near[0, here], w_near[0], NT)
            for proj, weight, c in [(near, w_near, c) for c in range(1, count)] + [
                (far, w_far, c) for c in range(count)
            ]:
                total = total + mm(proj[c, here], weight[c], NT)
            out[here] = total.astype(kind)

    at = lambda p: 1 - p[ODD] if leave else p[ODD]
    proj = block((count, rows, width), lambda j, p: (0, at(p), 0))
    weight = block((count, cols, width), lambda j, p: (0, j, 0))
    return kernel(
        body,
        (3,),
        [proj, proj, weight, weight],
        block((rows, cols), lambda j, p: (0, j)),
        shape_of((rows, depth), kind),
        cost=1 if leave else LONG,
    )(place, near, far, w_near, w_far)


def first_back(place, tokens, stay, arrived, resid_low, resid_high, gain):
    rows, depth = tokens.shape
    half = rows // 2

    def body(_, tokens, stay, arrived, resid_low, resid_high, gain, out, gain_sum, shift_sum):
        normal, inverse = norm_stats(tokens[...].astype(F32))
        grad, gains, shifts = norm_back(
            stay[...] + arrived[...].astype(F32), normal, inverse, gain[...]
        )

        @pl.when(pl.program_id(0) == 0)
        def _():
            out[...] = grad + resid_low[...]
            gain_sum[...] = gains
            shift_sum[...] = shifts

        @pl.when(pl.program_id(0) == 1)
        def _():
            out[...] = grad + resid_high[...]
            gain_sum[...] += gains
            shift_sum[...] += shifts

    tile = block((half, depth), lambda i, _: (i, 0))
    piece = block((half, depth))
    vector = block((1, depth))
    return kernel(
        body,
        (2,),
        [tile, tile, tile, piece, piece, vector],
        [tile, vector, vector],
        [shape_of((rows, depth), F32)] + [shape_of((1, depth), F32)] * 2,
        cost=LONG,
    )(place, tokens, stay, arrived, resid_low, resid_high, gain)


def shards(
    tokens,
    granularity,
    gain_one,
    shift_one,
    w_qkv,
    w_out,
    gain_two,
    shift_two,
    w_up,
    w_down,
    cotangent,
):
    tensor_size = lax.axis_size("tensor")
    dp_size = lax.axis_size("dp")
    rank = lax.axis_index("tensor")
    dp_at = lax.axis_index("dp")
    local_rows, depth = tokens.shape
    seq_len = local_rows * tensor_size // granularity.shape[0]
    assert tensor_size == 4 and seq_len == 2 * local_rows and dp_size % 8 == 0
    half = local_rows // 2
    hidden_here = w_up.shape[1]
    head_width = w_qkv.shape[2]
    bits = dp_size.bit_length() - 1
    tables = [jnp.asarray(t) for t in rope_tables(seq_len)]
    gain_one, shift_one, gain_two, shift_two = (
        v[None, :] for v in (gain_one, shift_one, gain_two, shift_two)
    )
    limits = jnp.left_shift(jnp.ones_like(granularity), granularity) * (FF // 8)
    upper = rank // 2
    place = jnp.stack(
        [
            rank % 2,
            dp_at & 1,
            (dp_at >> 1) & 1,
            (dp_at >> 2) & 1,
            jnp.where(upper == 0, limits[0], limits[1]),
            rank * hidden_here,
            (rank ^ 2) * hidden_here,
        ]
    ).astype(jnp.int32)
    chain = Chain()
    run = lambda call, *args: chain(functools.partial(call, place), *args)

    piece_qkv = swap(chain(dp_piece, w_qkv.reshape(3 * depth, head_width)), 0, 2)
    normed = run(first_norm, tokens, gain_one, shift_one)
    normed_far = [swap(v, 0, 1) for v in normed]
    normed_far[0], piece_qkv = chain.wait(normed_far[0], piece_qkv)
    w_qkv_far = from_all(piece_qkv).reshape(w_qkv.shape)
    piece_out, piece_up = chain(lambda a, b: (dp_piece(a), dp_piece(b)), w_out, w_up)
    piece_out, piece_up = swap(piece_out, 0, 2), swap(piece_up, 0, 2)
    normed_far[1], piece_out = chain.wait(normed_far[1], piece_out)
    w_out_far = from_all(piece_out)
    qkv_near = run(project, normed, normed_far, w_qkv, tables)
    att_near = run(attend, qkv_near)
    w_up_far = from_all(chain.wait(piece_up))
    piece_down, cot_low, cot_high = chain(
        lambda w, c: (dp_piece(w), c[:half], c[half:]), w_down, cotangent
    )
    piece_down = swap(piece_down, 0, 2)
    cot_high, cot_low = swap(cot_high, 0, 1), swap(cot_low, 0, 1)
    qkv_far = run(project, normed, normed_far, w_qkv_far, tables)
    att_far = run(attend, qkv_far)
    piece_down, cot_high, cot_low = chain.wait(piece_down, cot_high, cot_low)
    w_down_far = from_all(piece_down)
    heads = (att_near, att_far, w_out, w_out_far)
    low, high = chain(lambda *a: head_rows(place, True, *a), *heads)
    high, low = swap(high, 0, 1), swap(low, 0, 1)
    stay_low, stay_high = chain(lambda *a: head_rows(place, False, *a), *heads)
    norm_args = (gain_two, shift_two)
    normed_high, resid_high = chain(
        lambda *a: second_norm(place, 1, *a), stay_high, tokens, high, *norm_args
    )
    normed_high_far = swap(normed_high, 0, 1)
    normed_low, resid_low = chain(
        lambda *a: second_norm(place, 0, *a), stay_low, tokens, low, *norm_args
    )
    normed_low_far = swap(normed_low, 0, 1)

    weights = (w_up, w_down, w_up_far, w_down_far)
    *kept, stay_high, leave_high = chain(
        lambda *a: feed(0, place, *a), normed_high, normed_high_far, cotangent, cot_high, weights
    )
    back_high = swap(leave_high, 0, 1)
    *kept, stay_low, leave_low = chain(
        lambda *a: feed(1, place, *a), normed_low, normed_low_far, cotangent, cot_low, weights, kept
    )
    back_low = swap(leave_low, 0, 1)
    hidden_near, pre_near, hidden_far, pre_far, rows_two, grad_rows = kept
    ups = ((rows_two, rows_two), (pre_near, pre_far))
    downs = ((hidden_near, hidden_far), (grad_rows, grad_rows))
    grad_high, wide_high, gain_high, shift_high = chain(
        lambda *a: second_back(place, 1, *a), resid_high, stay_high, back_high, cotangent, gain_two
    )
    up = chain(lambda *a: wide_grad(place, None, *a), *ups)
    grad_low, wide_low, gain_low, shift_low = chain(
        lambda *a: second_back(place, 0, *a), resid_low, stay_low, back_low, cotangent, gain_two
    )
    grad_high_far, grad_low_far = swap(grad_high, 0, 1), swap(grad_low, 0, 1)
    down = chain(lambda *a: wide_grad(place, None, *a), *downs)
    out_high_leave, out_low_leave, out_high, out_low = run(
        down_rows, hidden_near, hidden_far, w_down, w_down_far, resid_high, resid_low
    )
    grad_high_far, grad_low_far = chain.wait(grad_high_far, grad_low_far)

    up, down = swap(up, 1, 0), swap(down, 1, 0)
    own, other = (grad_low, grad_high), (grad_low_far, grad_high_far)
    proj_far = chain(
        lambda *a: attend_back(place, LONG, *a), qkv_far, own, other, w_out_far, tables
    )
    up, down = chain.wait(up, down)
    up_keep, up = chain(lambda *a: wide_grad(place, 1, *a), *ups, up)
    down_keep, down = chain(lambda *a: wide_grad(place, 2, *a), *downs, down)
    up, down = swap(up, 2, 0), swap(down, 4, 0)
    proj_near = chain(lambda *a: attend_back(place, 1, *a), qkv_near, own, other, w_out, tables)
    leave_one = chain(
        lambda *a: back_rows(place, True, *a), proj_near, proj_far, w_qkv, w_qkv_far
    )
    attended = (att_near[None], att_far[None])
    kept = chain(
        lambda *a: narrow_grad(place, None, 0, 4, *a), normed, normed_far, proj_near, proj_far
    )
    kept = chain(
        lambda *a: narrow_grad(place, None, 3, 4, *a[:4], kept=a[4]), own, other, *attended, kept
    )
    up, down = chain.wait(up, down)
    up_keep, up = chain(lambda *a: add_split(place, 2, *a), up_keep, up)
    down_keep, down = chain(lambda *a: add_split(place, 1, *a), down_keep, down)
    up, down = swap(up, 4, 0), swap(down, 2, 0)
    heads_grad, back_one = swap(kept[0], 1, 0), swap(leave_one, 0, 1)
    stay_one = chain(
        lambda *a: back_rows(place, False, *a), proj_near, proj_far, w_qkv, w_qkv_far
    )
    heads_grad = chain.wait(heads_grad)
    kept = chain(
        lambda *a: narrow_grad(place, 1, 0, 4, *a),
        normed,
        normed_far,
        proj_near,
        proj_far,
        heads_grad,
    )
    heads_keep, heads_grad = chain(
        lambda *a: narrow_grad(place, 1, 3, 4, *a[:5], kept=a[5]),
        own,
        other,
        *attended,
        heads_grad,
        kept,
    )
    heads_grad = swap(heads_grad, 2, 0)
    up, down, back_one = chain.wait(up, down, back_one)

    def last_step(keep, arrived, hops):
        near, far = run(add_last, keep, arrived)
        return near, swap(far, 0, hops)

    def gather(near, arrived):
        piece = run(add_pair, near, arrived)
        for bit in range(3, bits):
            size = piece.shape[1] // 2
            side = (dp_at >> bit) & 1
            mine = lax.dynamic_slice_in_dim(piece, side * size, size, 1)
            theirs = lax.dynamic_slice_in_dim(piece, (1 - side) * size, size, 1)
            piece = add_pair(place, mine, swap(theirs, 1 << bit, 0))
        return lax.all_gather(piece, "dp", axis=0, tiled=False)

    def order_table(order):
        order = order + list(range(3, bits))
        return jnp.asarray(
            [
                sum(((j >> (bits - 1 - i)) & 1) << bit for i, bit in enumerate(order))
                for j in range(dp_size)
            ],
            jnp.int32,
        )

    up_near, up_far = last_step(up_keep, up, 2)
    down_near, down_far = last_step(down_keep, down, 2)
    out_high_far, out_low_far = swap(out_high_leave, 0, 1), swap(out_low_leave, 0, 1)
    grad_tokens, gain_sum, shift_sum = run(
        first_back, tokens, stay_one, back_one, wide_low, wide_high, gain_one
    )
    sums = chain(
        lambda *a: jnp.concatenate(a, axis=0),
        gain_sum,
        shift_sum,
        gain_low + gain_high,
        shift_low + shift_high,
    )
    steps = [(1 << b, 0) for b in range(bits)] + [(0, 1), (0, 2)]

    def sum_step(sums):
        return chain(lambda a, b: a + b, sums, swap(sums, *steps.pop()))

    heads_keep, heads_grad = chain(lambda *a: add_split(place, 2, *a), heads_keep, heads_grad)
    heads_grad = swap(heads_grad, 4, 0)
    sums = sum_step(sums)
    up_all = gather(up_near, up_far)
    sums = sum_step(sums)
    heads_near, heads_far = last_step(heads_keep, heads_grad, 2)
    down_all = gather(down_near, down_far)
    sums = sum_step(sums)
    heads_all = gather(heads_near, heads_far)
    while steps:
        sums = sum_step(sums)
    layer_out = run(layer_rows, out_low, out_high, out_low_far, out_high_far)

    xy, yx = order_table([0, 1, 2]), order_table([0, 2, 1])
    grad_up = chain(lambda v: assemble(xy, v), up_all)[0]
    grad_down = chain(lambda v: assemble(yx, v), down_all)[0]
    grad_qkv, grad_out = chain(lambda v: assemble_heads(xy, v), heads_all)
    return (
        layer_out,
        grad_tokens,
        sums[0],
        sums[1],
        grad_qkv,
        grad_out,
        sums[2],
        sums[3],
        grad_up,
        grad_down,
    )


def solution(mesh):
    rows = P(AXES, None)
    params = (P(), P(), P(None, None, "tensor"), P("tensor", None))
    wide = (P(None, "tensor"), P("tensor", None))
    return jax.shard_map(
        shards,
        mesh=mesh,
        in_specs=(rows, P("dp")) + params + (P(), P()) + wide + (rows,),
        out_specs=(rows, rows) + params + (P(), P()) + wide,
        check_vma=False,
    )
```

time: 1790 us -> 691 us (0.39)
  waiting for transfers between devices: 1160 us -> 240 us
  Pallas kernels: 0 us -> 344 us
  matrix products: 309 us -> 0 us
  local copies, waits for them, and re-layouts: 157 us -> 28 us
  other arithmetic: 87.7 us -> 2.64 us
  starting transfers between devices: 0.66 us -> 47.5 us
  blocking collectives: 42 us -> 0 us
    reduce_scatter x7 -> x0, waiting for transfers between devices: 624 us -> none  [the longest x1 210 us: shards(): lax.psum_scatter(jnp.dot(attn_flat, w_out, preferred_element_type=jnp.flo...]
    all_gather x8 -> x7, waiting for transfers between devices: 495 us -> 0.24 us  [the longest x3 0.22 us: gather(): return lax.all_gather(piece, 'dp', axis=0, tiled=False)]
    pallas_call x0 -> x40, Pallas kernels: none -> 344 us  [the longest x4 50.7 us: wide_grad(): kernel(body, (2, 3), [left, left, right(0), right(1)] + [tall(half)] * la...]
    dot_general x26 -> x0, matrix products: 309 us -> none  [the longest x2 44.4 us: back_one(): jnp.einsum('hqk,khd->qhd', grad_scores, key_one, preferred_element_type=j...]
    ppermute x0 -> x36, waiting for transfers between devices: none -> 240 us  [swap(): return lax.ppermute(value, AXES, pairs)]
    ppermute x0 -> x36, starting transfers between devices: none -> 46.4 us  [swap(): return lax.ppermute(value, AXES, pairs)]
    unnamed x69 -> x75, local copies, waits for them, and re-layouts: 60.4 us -> 14.9 us
    unnamed x17 -> x7, waiting for transfers between devices: 45.4 us -> 0.11 us
  transfers between devices with their start and end apart: 16 -> 43, of which waited for: 12 -> 22; matrix products, arithmetic and copies ran while one was open for 20% -> 1% of each run, Pallas kernels for 0% -> 43%
where the time goes in v2:
time: 691 us; the launch traced here: 679 us
  Pallas kernels  344 us (50%)
  waiting for transfers between devices  240 us (35%)
  starting transfers between devices  47.5 us (7%)
  local copies, waits for them, and re-layouts  28 us (4%)
  between operations  16 us (2%)
    ppermute x36, waiting for transfers between devices, swap(): return lax.ppermute(value, AXES, pairs)  240 us
    pallas_call x4, Pallas kernels, wide_grad(): kernel(body, (2, 3), [left, left, right(0), right(1)] + [tall(half)] * la...  50.7 us
    ppermute x36, starting transfers between devices, swap(): return lax.ppermute(value, AXES, pairs)  46.4 us
    pallas_call x2, Pallas kernels, feed(): kernel(body, (2 * near_steps,), [piece, piece, block((half, depth), lambd...  42.7 us
    pallas_call x2, Pallas kernels, attend_back(): kernel(body, (width // HD,), [spec(0), spec(1), spec(2)] + [piece] * 4 +...  34 us
    pallas_call x4, Pallas kernels, narrow_grad(): kernel(body, (2, count), ins + [pl.BlockSpec(memory_space=pl.ANY)] * len(...  34 us
    pallas_call x2, Pallas kernels, project(): kernel(body, (4,), [block((part, depth))] * 4 + [block((3, depth, width))...  20.9 us
    pallas_call x2, Pallas kernels, back_rows(): kernel(body, (3,), [proj, proj, weight, weight], block((rows, cols), lamb...  19.1 us
  transfers between devices with their start and end apart: 43, of which 22 were waited for; matrix products, arithmetic and copies ran while one was open for 1% of the time, Pallas kernels for 43%

profile of v2, /device:TPU:0, one launch (start us, length us, event | category | flops | bytes accessed | tf_op | source)
XLA Modules:
  0.0 678.6 jit_solution(9382097212012436132)
XLA Ops:
  23.9 23.9 %collective-permute-done.1 = bf16[576,384]{1,0:T(8,128)(2,1)S(1)} collective-permute-done((bf16[576,384]{1,0:T(8,128)(2,1)S(1)}, bf16[576,384]{1,0:T(8,128)(2,1)S(1)}, u32[]{:S(2)}, u32[]{:S(2)}) %collective-permute-start.1) | collective-permute-done | bytes 442400 | tf_op jit(solution)/shard_map/ppermute | solution.py:41
  54.0 18.2 %collective-permute-done.2.th.refs_3_ = bf16[256,1536]{1,0:T(8,128)(2,1)S(1)} collective-permute-done((bf16[256,1536]{1,0:T(8,128)(2,1)}, bf16[256,1536]{1,0:T(8,128)(2,1)S(1)}, u32[]{:S(2)}, u32[]{:S(2)}) %collective-permute-start.2) | collective-permute-done | bytes 786464 | tf_op jit(solution)/shard_map/ppermute | solution.py:41
  76.8 10.4 %shard_map.223.q_ref.k_ref.v_ref = bf16[3,1024,384]{2,1,0:T(8,128)(2,1)} custom-call(s32[7]{0:T(128)} %stack.31._.p, bf16[256,1536]{1,0:T(8,128)(2,1)} %get-tuple-element.479.ol.refs_0_, bf16[256,1536]{1,0:T(8,128)(2,1)} %get-tuple-element.480.oh.refs_1_, bf16[256,1536]{1,0:T(8,128)(2,1)} %copy-done.1, bf16[256,1536]{1,0:T(8,128)(2,1)} %copy-done.2, ...), custom_call_target="tpu_custom_call" | custom-call | flops 1 | bytes 1 | tf_op jit(solution)/shard_map/pallas_call | solution.py:173
  87.3 9.0 %shard_map.224.near = bf16[1024,384]{1,0:T(8,128)(2,1)} custom-call(s32[7]{0:T(128)} %stack.31._.p, bf16[3,1024,384]{2,1,0:T(8,128)(2,1)} %shard_map.223.q_ref.k_ref.v_ref, bf16[3,1024,384]{2,1,0:T(8,128)(2,1)} %shard_map.223.q_ref.k_ref.v_ref, bf16[3,1024,384]{2,1,0:T(8,128)(2,1)} %shard_map.223.q_ref.k_ref.v_ref), custom_call_target="tpu_custom_call" | custom-call | flops 1 | bytes 1 | tf_op jit(solution)/shard_map/pallas_call | solution.py:206
  107.3 10.5 %shard_map.225.q_ref.k_ref.v_ref = bf16[3,1024,384]{2,1,0:T(8,128)(2,1)} custom-call(s32[7]{0:T(128)} %stack.31._.p, bf16[256,1536]{1,0:T(8,128)(2,1)} %get-tuple-element.479.ol.refs_0_, bf16[256,1536]{1,0:T(8,128)(2,1)} %get-tuple-element.480.oh.refs_1_, bf16[256,1536]{1,0:T(8,128)(2,1)} %copy-done.1, bf16[256,1536]{1,0:T(8,128)(2,1)} %copy-done.2, ...), custom_call_target="tpu_custom_call" | custom-call | flops 1 | bytes 1 | tf_op jit(solution)/shard_map/pallas_call | solution.py:173
  117.8 8.9 %shard_map.226.far = bf16[1024,384]{1,0:T(8,128)(2,1)} custom-call(s32[7]{0:T(128)} %stack.31._.p, bf16[3,1024,384]{2,1,0:T(8,128)(2,1)} %shard_map.225.q_ref.k_ref.v_ref, bf16[3,1024,384]{2,1,0:T(8,128)(2,1)} %shard_map.225.q_ref.k_ref.v_ref, bf16[3,1024,384]{2,1,0:T(8,128)(2,1)} %shard_map.225.q_ref.k_ref.v_ref), custom_call_target="tpu_custom_call" | custom-call | flops 1 | bytes 1 | tf_op jit(solution)/shard_map/pallas_call | solution.py:206
  126.7 22.2 %collective-permute-done.5 = bf16[192,1536]{1,0:T(8,128)(2,1)} collective-permute-done((bf16[192,1536]{1,0:T(8,128)(2,1)}, bf16[192,1536]{1,0:T(8,128)(2,1)}, u32[]{:S(2)}, u32[]{:S(2)}) %collective-permute-start.5) | collective-permute-done | bytes 589856 | tf_op jit(solution)/shard_map/ppermute | solution.py:41
  166.1 11.6 %collective-permute-done.9.arrived = bf16[256,1536]{1,0:T(8,128)(2,1)S(1)} collective-permute-done((bf16[256,1536]{1,0:T(8,128)(2,1)}, bf16[256,1536]{1,0:T(8,128)(2,1)S(1)}, u32[]{:S(2)}, u32[]{:S(2)}) %collective-permute-start.9) | collective-permute-done | bytes 786464 | tf_op jit(solution)/shard_map/ppermute | solution.py:41
  182.9 11.7 %collective-permute-done.8.arrived = bf16[256,1536]{1,0:T(8,128)(2,1)S(1)} collective-permute-done((bf16[256,1536]{1,0:T(8,128)(2,1)}, bf16[256,1536]{1,0:T(8,128)(2,1)S(1)}, u32[]{:S(2)}, u32[]{:S(2)}) %collective-permute-start.8) | collective-permute-done | bytes 786464 | tf_op jit(solution)/shard_map/ppermute | solution.py:41
  199.7 11.7 %collective-permute-done.11.other = bf16[256,1536]{1,0:T(8,128)(2,1)S(1)} collective-permute-done((bf16[256,1536]{1,0:T(8,128)(2,1)}, bf16[256,1536]{1,0:T(8,128)(2,1)S(1)}, u32[]{:S(2)}, u32[]{:S(2)}) %collective-permute-start.11) | collective-permute-done | bytes 786464 | tf_op jit(solution)/shard_map/ppermute | solution.py:41
  212.3 21.3 %shard_map.231 = (bf16[1024,1536]{1,0:T(8,128)(2,1)}, bf16[1024,1536]{1,0:T(8,128)(2,1)}, bf16[1024,1536]{1,0:T(8,128)(2,1)}, bf16[1024,1536]{1,0:T(8,128)(2,1)}...) custom-call(s32[7]{0:T(128)} %stack.31._.p, ...), custom_call_target="tpu_custom_call" | custom-call | flops 1 | bytes 1 | tf_op jit(solution)/shard_map/pallas_call | solution.py:382
  235.2 21.4 %shard_map.232 = (bf16[1024,1536]{1,0:T(8,128)(2,1)}, bf16[1024,1536]{1,0:T(8,128)(2,1)}, bf16[1024,1536]{1,0:T(8,128)(2,1)}, bf16[1024,1536]{1,0:T(8,128)(2,1)}...) custom-call(s32[7]{0:T(128)} %stack.31._.p, ...), custom_call_target="tpu_custom_call", output_to_operand_aliasing={{0}: (9, {}), {1}: (10, {}), {2}: (11, {}), {3}: (12, {}), ... | custom-call | flops 1 | bytes 1 | tf_op jit(solution)/shard_map/pallas_call | solution.py:382
  264.4 12.2 %shard_map.234 = bf16[2,1,768,1536]{3,2,1,0:T(8,128)(2,1)} custom-call(s32[7]{0:T(128)} %stack.31._.p, bf16[1024,1536]{1,0:T(8,128)(2,1)} %get-tuple-element.426.l0.l1, bf16[1024,1536]{1,0:T(8,128)(2,1)} %get-tuple-element.426.l0.l1, bf16[1024,1536]{1,0:T(8,128)(2,1)} %get-tuple-element.427.r0, bf16[1024,1536]{1,0:T(8,128)(2,1)} %get-tuple-element.428.r1), custom_call_target="tpu_custom_call" | custom-call | flops 1 | bytes 1 | tf_op jit(solution)/shard_map/pallas_call | solution.py:510
  284.5 12.4 %shard_map.236 = bf16[2,1,768,1536]{3,2,1,0:T(8,128)(2,1)} custom-call(s32[7]{0:T(128)} %stack.31._.p, bf16[1024,1536]{1,0:T(8,128)(2,1)} %get-tuple-element.431.l0.near, bf16[1024,1536]{1,0:T(8,128)(2,1)} %get-tuple-element.432.l1.far, bf16[1024,1536]{1,0:T(8,128)(2,1)} %get-tuple-element.434.r0.r1, bf16[1024,1536]{1,0:T(8,128)(2,1)} %get-tuple-element.434.r0.r1), custom_call_target="tpu_custom_call" | custom-call | flops 1 | bytes 1 | tf_op jit(solution)/shard_map/pallas_call | solution.py:510
  297.5 17.1 %shard_map.237 = (bf16[256,1536]{1,0:T(8,128)(2,1)}, bf16[256,1536]{1,0:T(8,128)(2,1)}, f32[256,1536]{1,0:T(8,128)}, f32[256,1536]{1,0:T(8,128)}) custom-call(s32[7]{0:T(128)} %stack.31._.p, bf16[1024,1536]{1,0:T(8,128)(2,1)} %get-tuple-element.431.l0.near, bf16[1024,1536]{1,0:T(8,128)(2,1)} %get-tuple-element.432.l1.far, bf16[1536,1536]{1,0:T(8,128)(2,1)} %w_near.2, ...), custom_call_target="tpu_custom_call" | custom-call | flops 1 | bytes 1 | tf_op jit(solution)/shard_map/pallas_call | solution.py:449
  315.8 16.8 %shard_map.238.far.refs_5_ = bf16[3,1024,384]{2,1,0:T(8,128)(2,1)} custom-call(s32[7]{0:T(128)} %stack.31._.p, bf16[3,1024,384]{2,1,0:T(8,128)(2,1)} %shard_map.225.q_ref.k_ref.v_ref, bf16[3,1024,384]{2,1,0:T(8,128)(2,1)} %shard_map.225.q_ref.k_ref.v_ref, bf16[3,1024,384]{2,1,0:T(8,128)(2,1)} %shard_map.225.q_ref.k_ref.v_ref, ...), custom_call_target="tpu_custom_call" | custom-call | flops 199999995904 | bytes 1 | tf_op jit(solution)/shard_map/pallas_call | solution.py:253
  332.6 12.9 %shard_map.239 = (bf16[2,1,384,1536]{3,2,1,0:T(8,128)(2,1)}, bf16[2,1,384,1536]{3,2,1,0:T(8,128)(2,1)}) custom-call(s32[7]{0:T(128)} %stack.31._.p, bf16[1024,1536]{1,0:T(8,128)(2,1)} %get-tuple-element.426.l0.l1, bf16[1024,1536]{1,0:T(8,128)(2,1)} %get-tuple-element.426.l0.l1, bf16[1024,1536]{1,0:T(8,128)(2,1)} %get-tuple-element.427.r0, ...), custom_call_target="tpu_custom_call" | custom-call | flops 1 | bytes 1 | tf_op jit(solution)/shard_map/pallas_call | solution.py:510
  345.6 13.1 %shard_map.240 = (bf16[2,1,384,1536]{3,2,1,0:T(8,128)(2,1)}, bf16[2,1,384,1536]{3,2,1,0:T(8,128)(2,1)}) custom-call(s32[7]{0:T(128)} %stack.31._.p, bf16[1024,1536]{1,0:T(8,128)(2,1)} %get-tuple-element.431.l0.near, bf16[1024,1536]{1,0:T(8,128)(2,1)} %get-tuple-element.432.l1.far, bf16[1024,1536]{1,0:T(8,128)(2,1)} %get-tuple-element.434.r0.r1, ...), custom_call_target="tpu_custom_call" | custom-call | flops 1 | bytes 1 | tf_op jit(solution)/shard_map/pallas_call | solution.py:510
  366.7 17.2 %shard_map.241.near.refs_4_ = bf16[3,1024,384]{2,1,0:T(8,128)(2,1)} custom-call(s32[7]{0:T(128)} %stack.31._.p, bf16[3,1024,384]{2,1,0:T(8,128)(2,1)} %shard_map.223.q_ref.k_ref.v_ref, bf16[3,1024,384]{2,1,0:T(8,128)(2,1)} %shard_map.223.q_ref.k_ref.v_ref, bf16[3,1024,384]{2,1,0:T(8,128)(2,1)} %shard_map.223.q_ref.k_ref.v_ref, ...), custom_call_target="tpu_custom_call" | custom-call | flops 1 | bytes 1 | tf_op jit(solution)/shard_map/pallas_call | solution.py:253
  383.9 9.4 %shard_map.242 = bf16[512,1536]{1,0:T(8,128)(2,1)} custom-call(s32[7]{0:T(128)} %stack.31._.p, bf16[3,1024,384]{2,1,0:T(8,128)(2,1)} %shard_map.241.near.refs_4_, bf16[3,1024,384]{2,1,0:T(8,128)(2,1)} %shard_map.238.far.refs_5_, bf16[3,1536,384]{2,1,0:T(8,128)(2,1)} %w_near.4, bf16[3,1536,384]{2,1,0:T(8,128)(2,1)} %bitcast.26), custom_call_target="tpu_custom_call" | custom-call | flops 1 | bytes 1 | tf_op jit(solution)/shard_map/pallas_call | solution.py:670
  393.7 10.7 %shard_map.243.refs_6_ = bf16[2,4,768,384]{3,2,1,0:T(8,128)(2,1)} custom-call(s32[7]{0:T(128)} %stack.31._.p, bf16[256,1536]{1,0:T(8,128)(2,1)} %get-tuple-element.479.ol.refs_0_, bf16[256,1536]{1,0:T(8,128)(2,1)} %get-tuple-element.480.oh.refs_1_, bf16[256,1536]{1,0:T(8,128)(2,1)} %copy-done.1, bf16[256,1536]{1,0:T(8,128)(2,1)} %copy-done.2, ...), custom_call_target="tpu_custom_call" | custom-call | flops 1 | bytes 1 | tf_op jit(solution)/shard_map/pallas_call | solution.py:561
  429.3 9.7 %shard_map.247.stay = f32[512,1536]{1,0:T(8,128)} custom-call(s32[7]{0:T(128)} %stack.31._.p, bf16[3,1024,384]{2,1,0:T(8,128)(2,1)} %shard_map.241.near.refs_4_, bf16[3,1024,384]{2,1,0:T(8,128)(2,1)} %shard_map.238.far.refs_5_, bf16[3,1536,384]{2,1,0:T(8,128)(2,1)} %w_near.4, bf16[3,1536,384]{2,1,0:T(8,128)(2,1)} %bitcast.27), custom_call_target="tpu_custom_call" | custom-call | flops 199999995904 | bytes 1 | tf_op jit(solution)/shard_map/pallas_call | solution.py:670
  439.0 11.2 %shard_map.248 = (bf16[2,4,384,384]{3,2,1,0:T(8,128)(2,1)}, bf16[2,4,384,384]{3,2,1,0:T(8,128)(2,1)}) custom-call(s32[7]{0:T(128)} %stack.31._.p, bf16[256,1536]{1,0:T(8,128)(2,1)} %get-tuple-element.479.ol.refs_0_, bf16[256,1536]{1,0:T(8,128)(2,1)} %get-tuple-element.480.oh.refs_1_, bf16[256,1536]{1,0:T(8,128)(2,1)} %copy-done.1, ...), custom_call_target="tpu_custom_call" | custom-call | flops 1 | bytes 1 | tf_op jit(solution)/shard_map/pallas_call | solution.py:561
  479.5 42.8 %collective-permute-done.27.theirs = bf16[2,4,384,384]{3,2,1,0:T(8,128)(2,1)} collective-permute-done((bf16[2,4,384,384]{3,2,1,0:T(8,128)(2,1)}, bf16[2,4,384,384]{3,2,1,0:T(8,128)(2,1)}, u32[]{:S(2)}, u32[]{:S(2)}) %collective-permute-start.27) | collective-permute-done | bytes 2359328 | tf_op jit(solution)/shard_map/ppermute | solution.py:41
  534.1 10.1 %collective-permute-done.28 = f32[4,1536]{1,0:T(4,128)S(1)} collective-permute-done((f32[4,1536]{1,0:T(4,128)S(1)}, f32[4,1536]{1,0:T(4,128)S(1)}, u32[]{:S(2)}, u32[]{:S(2)}) %collective-permute-start.28) | collective-permute-done | bytes 24608 | tf_op jit(solution)/shard_map/ppermute | solution.py:41
  544.2 27.2 %collective-permute-done.32.theirs = bf16[2,4,192,384]{3,2,1,0:T(8,128)(2,1)S(1)} collective-permute-done((bf16[2,4,192,384]{3,2,1,0:T(8,128)(2,1)S(1)}, bf16[2,4,192,384]{3,2,1,0:T(8,128)(2,1)S(1)}, u32[]{:S(2)}, u32[]{:S(2)}) %collective-permute-start.32) | collective-permute-done | bytes 1179680 | tf_op jit(solution)/shard_map/ppermute | solution.py:41
  584.6 13.8 %collective-permute-done.34.theirs = bf16[4,192,384]{2,1,0:T(8,128)(2,1)S(1)} collective-permute-done((bf16[4,192,384]{2,1,0:T(8,128)(2,1)S(1)}, bf16[4,192,384]{2,1,0:T(8,128)(2,1)S(1)}, u32[]{:S(2)}, u32[]{:S(2)}) %collective-permute-start.34) | collective-permute-done | bytes 589856 | tf_op jit(solution)/shard_map/ppermute | solution.py:41
  611.2 12.8 %collective-permute-done.14.low = bf16[256,1536]{1,0:T(8,128)(2,1)S(1)} collective-permute-done((bf16[256,1536]{1,0:T(8,128)(2,1)S(1)}, bf16[256,1536]{1,0:T(8,128)(2,1)S(1)}, u32[]{:S(2)}, u32[]{:S(2)}) %collective-permute-start.14) | collective-permute-done | bytes 786464 | tf_op jit(solution)/shard_map/ppermute | solution.py:41
  624.0 11.0 %collective-permute-done.15.high = bf16[256,1536]{1,0:T(8,128)(2,1)S(1)} collective-permute-done((bf16[256,1536]{1,0:T(8,128)(2,1)S(1)}, bf16[256,1536]{1,0:T(8,128)(2,1)S(1)}, u32[]{:S(2)}, u32[]{:S(2)}) %collective-permute-start.15) | collective-permute-done | bytes 786464 | tf_op jit(solution)/shard_map/ppermute | solution.py:41
  640.9 8.3 %shard_map.259 = f32[1,1536,1536]{2,1,0:T(8,128)} custom-call(s32[8]{0:T(128)} %constant.60.clone._, bf16[8,1,192,1536]{3,2,1,0:T(8,128)(2,1)} %bitcast.32), custom_call_target="tpu_custom_call" | custom-call | flops 1 | bytes 1 | tf_op jit(solution)/shard_map/pallas_call | solution.py:621
  649.2 8.4 %shard_map.260 = f32[1,1536,1536]{2,1,0:T(8,128)} custom-call(s32[8]{0:T(128)} %constant.61.clone._, bf16[8,1,192,1536]{3,2,1,0:T(8,128)(2,1)} %bitcast.33), custom_call_target="tpu_custom_call" | custom-call | flops 1 | bytes 1 | tf_op jit(solution)/shard_map/pallas_call | solution.py:621
  657.8 9.4 %shard_map.261 = (f32[3,1536,384]{2,1,0:T(8,128)}, f32[8,384,192]{2,1,0:T(8,128)}) custom-call(s32[8]{0:T(128)} %constant.60.clone._, bf16[8,4,192,384]{3,2,1,0:T(8,128)(2,1)} %bitcast.31), custom_call_target="tpu_custom_call" | custom-call | flops 1 | bytes 1 | tf_op jit(solution)/shard_map/pallas_call | solution.py:637
  (198 shorter events, 195.3 us)
Async XLA Ops:
  7.2 100.1 %all-gather.11.cloned.1.call-start = ((), (), s32[]{:S(2)}) async-start(), calls=%async_computation | async-start | bytes 3981312 | tf_op jit(solution)/shard_map/all_gather | solution.py:67
  18.3 30.3 %collective-permute-start = (bf16[256,1536]{1,0:T(8,128)(2,1)}, bf16[256,1536]{1,0:T(8,128)(2,1)S(1)}, u32[]{:S(2)}, u32[]{:S(2)}) collective-permute-start(bf16[256,1536]{1,0:T(8,128)(2,1)} %get-tuple-element.479.ol.refs_0_), channel_id=1, source_target_pairs={{0,1},{1,0},{2,3},{3,2},{4,5},{5,4},{6,7},{7,6},{8,9},{9,8},{10,11... | collective-permute-start | bytes 2359304 | tf_op jit(solution)/shard_map/ppermute | solution.py:41
  21.3 26.5 %collective-permute-start.1 = (bf16[576,384]{1,0:T(8,128)(2,1)S(1)}, bf16[576,384]{1,0:T(8,128)(2,1)S(1)}, u32[]{:S(2)}, u32[]{:S(2)}) collective-permute-start(bf16[576,384]{1,0:T(8,128)(2,1)S(1)} %constant_dynamic-slice_fusion.3), channel_id=1, source_target_pairs={{0,2},{1,3},{2,0},{3,1},{4,6},{5,7},{6,4},{7,5},{8,10},{9,11},{10,... | collective-permute-start | bytes 1327112 | tf_op jit(solution)/shard_map/ppermute | solution.py:41
  48.6 103.0 %all-gather.13.cloned.1.call-start = ((), (), s32[]{:S(2)}) async-start(), calls=%async_computation.1 | async-start | bytes 1327104 | tf_op jit(solution)/shard_map/all_gather | solution.py:67
  73.0 138.4 %all-gather.15.cloned.1.call-start = ((), (), s32[]{:S(2)}) async-start(), calls=%async_computation.2 | async-start | bytes 5308416 | tf_op jit(solution)/shard_map/all_gather | solution.py:67
  74.2 27.2 %collective-permute-start.4 = (bf16[192,1536]{1,0:T(8,128)(2,1)S(1)}, bf16[192,1536]{1,0:T(8,128)(2,1)S(1)}, u32[]{:S(2)}, u32[]{:S(2)}) collective-permute-start(bf16[192,1536]{1,0:T(8,128)(2,1)S(1)} %constant_dynamic-slice_fusion.1), channel_id=1, source_target_pairs={{0,2},{1,3},{2,0},{3,1},{4,6},{5,7},{6,4},{7,5},{8,10},{9,11},{10,... | collective-permute-start | bytes 1769480 | tf_op jit(solution)/shard_map/ppermute | solution.py:41
  102.2 109.3 %all-gather.17.cloned.1.call-start = ((), (), s32[]{:S(2)}) async-start(), calls=%async_computation.3 | async-start | bytes 5308416 | tf_op jit(solution)/shard_map/all_gather | solution.py:67
  102.6 46.2 %collective-permute-start.7 = (bf16[256,1536]{1,0:T(8,128)(2,1)S(1)}, bf16[256,1536]{1,0:T(8,128)(2,1)S(1)}, u32[]{:S(2)}, u32[]{:S(2)}) collective-permute-start(bf16[256,1536]{1,0:T(8,128)(2,1)S(1)} %get-tuple-element.586), channel_id=1, source_target_pairs={{0,1},{1,0},{2,3},{3,2},{4,5},{5,4},{6,7},{7,6},{8,9},{9,8},{10,11... | collective-permute-start | bytes 2359304 | tf_op jit(solution)/shard_map/ppermute | solution.py:41
  102.7 48.3 %collective-permute-start.6 = (bf16[256,1536]{1,0:T(8,128)(2,1)S(1)}, bf16[256,1536]{1,0:T(8,128)(2,1)S(1)}, u32[]{:S(2)}, u32[]{:S(2)}) collective-permute-start(bf16[256,1536]{1,0:T(8,128)(2,1)S(1)} %get-tuple-element.587), channel_id=1, source_target_pairs={{0,1},{1,0},{2,3},{3,2},{4,5},{5,4},{6,7},{7,6},{8,9},{9,8},{10,11... | collective-permute-start | bytes 2359304 | tf_op jit(solution)/shard_map/ppermute | solution.py:41
  106.6 42.2 %collective-permute-start.5 = (bf16[192,1536]{1,0:T(8,128)(2,1)}, bf16[192,1536]{1,0:T(8,128)(2,1)}, u32[]{:S(2)}, u32[]{:S(2)}) collective-permute-start(bf16[192,1536]{1,0:T(8,128)(2,1)} %constant_dynamic-slice_fusion), channel_id=1, source_target_pairs={{0,2},{1,3},{2,0},{3,1},{4,6},{5,7},{6,4},{7,5},{8,10},{9,11},{10,... | collective-permute-start | bytes 1769480 | tf_op jit(solution)/shard_map/ppermute | solution.py:41
  151.0 489.9 %all-gather.23.cloned.1.call-start = ((), (), s32[]{:S(2)}) async-start(), calls=%async_computation.6 | async-start | bytes 5308416 | tf_op jit(solution)/shard_map/all_gather | solution.py:880
  157.6 36.9 %collective-permute-start.8 = (bf16[256,1536]{1,0:T(8,128)(2,1)}, bf16[256,1536]{1,0:T(8,128)(2,1)S(1)}, u32[]{:S(2)}, u32[]{:S(2)}) collective-permute-start(bf16[256,1536]{1,0:T(8,128)(2,1)} %get-tuple-element.321), channel_id=1, source_target_pairs={{0,1},{1,0},{2,3},{3,2},{4,5},{5,4},{6,7},{7,6},{8,9},{9,8},{10,11... | collective-permute-start | bytes 2359304 | tf_op jit(solution)/shard_map/ppermute | solution.py:41
  182.3 29.1 %collective-permute-start.11 = (bf16[256,1536]{1,0:T(8,128)(2,1)}, bf16[256,1536]{1,0:T(8,128)(2,1)S(1)}, u32[]{:S(2)}, u32[]{:S(2)}) collective-permute-start(bf16[256,1536]{1,0:T(8,128)(2,1)} %get-tuple-element.343.own), channel_id=1, source_target_pairs={{0,1},{1,0},{2,3},{3,2},{4,5},{5,4},{6,7},{7,6},{8,9},{9,8},{10,11... | collective-permute-start | bytes 2359304 | tf_op jit(solution)/shard_map/ppermute | solution.py:41
  199.1 35.2 %collective-permute-start.10 = (bf16[256,1536]{1,0:T(8,128)(2,1)}, bf16[256,1536]{1,0:T(8,128)(2,1)S(1)}, u32[]{:S(2)}, u32[]{:S(2)}) collective-permute-start(bf16[256,1536]{1,0:T(8,128)(2,1)} %get-tuple-element.357.own), channel_id=1, source_target_pairs={{0,1},{1,0},{2,3},{3,2},{4,5},{5,4},{6,7},{7,6},{8,9},{9,8},{10,11... | collective-permute-start | bytes 2359304 | tf_op jit(solution)/shard_map/ppermute | solution.py:41
  263.8 50.8 %collective-permute-start.16 = (bf16[256,1536]{1,0:T(8,128)(2,1)}, bf16[256,1536]{1,0:T(8,128)(2,1)S(1)}, u32[]{:S(2)}, u32[]{:S(2)}) collective-permute-start(bf16[256,1536]{1,0:T(8,128)(2,1)} %get-tuple-element.489.oh.refs_1_), channel_id=1, source_target_pairs={{0,1},{1,0},{2,3},{3,2},{4,5},{5,4},{6,7},{7,6},{8,9},{9,8},{10,11... | collective-permute-start | bytes 2359304 | tf_op jit(solution)/shard_map/ppermute | solution.py:41
  283.0 31.6 %collective-permute-start.17 = (bf16[256,1536]{1,0:T(8,128)(2,1)}, bf16[256,1536]{1,0:T(8,128)(2,1)S(1)}, u32[]{:S(2)}, u32[]{:S(2)}) collective-permute-start(bf16[256,1536]{1,0:T(8,128)(2,1)} %get-tuple-element.488.ol.refs_0_), channel_id=1, source_target_pairs={{0,1},{1,0},{2,3},{3,2},{4,5},{5,4},{6,7},{7,6},{8,9},{9,8},{10,11... | collective-permute-start | bytes 2359304 | tf_op jit(solution)/shard_map/ppermute | solution.py:41
  284.5 48.1 %collective-permute-start.18 = (bf16[2,1,768,1536]{3,2,1,0:T(8,128)(2,1)}, bf16[2,1,768,1536]{3,2,1,0:T(8,128)(2,1)}, u32[]{:S(2)}, u32[]{:S(2)}) collective-permute-start(bf16[2,1,768,1536]{3,2,1,0:T(8,128)(2,1)} %shard_map.234), channel_id=1, source_target_pairs={{0,4},{1,5},{2,6},{3,7},{4,0},{5,1},{6,2},{7,3},{8,12},{9,13},{10,... | collective-permute-start | bytes 14155784 | tf_op jit(solution)/shard_map/ppermute | solution.py:41
  296.9 35.7 %collective-permute-start.19 = (bf16[2,1,768,1536]{3,2,1,0:T(8,128)(2,1)}, bf16[2,1,768,1536]{3,2,1,0:T(8,128)(2,1)}, u32[]{:S(2)}, u32[]{:S(2)}) collective-permute-start(bf16[2,1,768,1536]{3,2,1,0:T(8,128)(2,1)} %shard_map.236), channel_id=1, source_target_pairs={{0,4},{1,5},{2,6},{3,7},{4,0},{5,1},{6,2},{7,3},{8,12},{9,13},{10,... | collective-permute-start | bytes 14155784 | tf_op jit(solution)/shard_map/ppermute | solution.py:41
  358.7 57.3 %collective-permute-start.21 = (bf16[2,1,384,1536]{3,2,1,0:T(8,128)(2,1)}, bf16[2,1,384,1536]{3,2,1,0:T(8,128)(2,1)S(1)}, u32[]{:S(2)}, u32[]{:S(2)}) collective-permute-start(bf16[2,1,384,1536]{3,2,1,0:T(8,128)(2,1)} %get-tuple-element.446), channel_id=1, source_target_pairs={{0,16},{1,17},{2,18},{3,19},{4,20},{5,21},{6,22},{7,23},{8,24},{9,... | collective-permute-start | bytes 7077896 | tf_op jit(solution)/shard_map/ppermute | solution.py:41
  363.9 53.3 %collective-permute-start.20 = (bf16[2,1,384,1536]{3,2,1,0:T(8,128)(2,1)S(1)}, bf16[2,1,384,1536]{3,2,1,0:T(8,128)(2,1)S(1)}, u32[]{:S(2)}, u32[]{:S(2)}) collective-permute-start(bf16[2,1,384,1536]{3,2,1,0:T(8,128)(2,1)S(1)} %copy-done.31), channel_id=1, source_target_pairs={{0,8},{1,9},{2,10},{3,11},{4,12},{5,13},{6,14},{7,15},{8,0},{9,1},... | collective-permute-start | bytes 7077896 | tf_op jit(solution)/shard_map/ppermute | solution.py:41
  393.3 63.2 %collective-permute-start.24 = (bf16[512,1536]{1,0:T(8,128)(2,1)}, bf16[512,1536]{1,0:T(8,128)(2,1)}, u32[]{:S(2)}, u32[]{:S(2)}) collective-permute-start(bf16[512,1536]{1,0:T(8,128)(2,1)} %shard_map.242), channel_id=1, source_target_pairs={{0,1},{1,0},{2,3},{3,2},{4,5},{5,4},{6,7},{7,6},{8,9},{9,8},{10,11... | collective-permute-start | bytes 4718600 | tf_op jit(solution)/shard_map/ppermute | solution.py:41
  410.2 28.8 %collective-permute-start.25 = (bf16[2,4,768,384]{3,2,1,0:T(8,128)(2,1)}, bf16[2,4,768,384]{3,2,1,0:T(8,128)(2,1)}, u32[]{:S(2)}, u32[]{:S(2)}) collective-permute-start(bf16[2,4,768,384]{3,2,1,0:T(8,128)(2,1)} %shard_map.244), channel_id=1, source_target_pairs={{0,4},{1,5},{2,6},{3,7},{4,0},{5,1},{6,2},{7,3},{8,12},{9,13},{10,... | collective-permute-start | bytes 14155784 | tf_op jit(solution)/shard_map/ppermute | solution.py:41
  427.2 29.3 %collective-permute-start.23 = (bf16[2,1,192,1536]{3,2,1,0:T(8,128)(2,1)}, bf16[2,1,192,1536]{3,2,1,0:T(8,128)(2,1)}, u32[]{:S(2)}, u32[]{:S(2)}) collective-permute-start(bf16[2,1,192,1536]{3,2,1,0:T(8,128)(2,1)} %get-tuple-element.477), channel_id=1, source_target_pairs={{0,8},{1,9},{2,10},{3,11},{4,12},{5,13},{6,14},{7,15},{8,0},{9,1},... | collective-permute-start | bytes 3538952 | tf_op jit(solution)/shard_map/ppermute | solution.py:41
  428.8 27.7 %collective-permute-start.22 = (bf16[2,1,192,1536]{3,2,1,0:T(8,128)(2,1)}, bf16[2,1,192,1536]{3,2,1,0:T(8,128)(2,1)}, u32[]{:S(2)}, u32[]{:S(2)}) collective-permute-start(bf16[2,1,192,1536]{3,2,1,0:T(8,128)(2,1)} %get-tuple-element.476), channel_id=1, source_target_pairs={{0,16},{1,17},{2,18},{3,19},{4,20},{5,21},{6,22},{7,23},{8,24},{9,... | collective-permute-start | bytes 3538952 | tf_op jit(solution)/shard_map/ppermute | solution.py:41
  463.4 65.8 %collective-permute-start.29 = (bf16[1,192,1536]{2,1,0:T(8,128)(2,1)}, bf16[1,192,1536]{2,1,0:T(8,128)(2,1)}, u32[]{:S(2)}, u32[]{:S(2)}) collective-permute-start(bf16[1,192,1536]{2,1,0:T(8,128)(2,1)} %get-tuple-element.532), channel_id=1, source_target_pairs={{0,2},{1,3},{2,0},{3,1},{4,6},{5,7},{6,4},{7,5},{8,10},{9,11},{10,... | collective-permute-start | bytes 1769480 | tf_op jit(solution)/shard_map/ppermute | solution.py:41
  470.5 51.7 %collective-permute-start.27 = (bf16[2,4,384,384]{3,2,1,0:T(8,128)(2,1)}, bf16[2,4,384,384]{3,2,1,0:T(8,128)(2,1)}, u32[]{:S(2)}, u32[]{:S(2)}) collective-permute-start(bf16[2,4,384,384]{3,2,1,0:T(8,128)(2,1)} %get-tuple-element.526), channel_id=1, source_target_pairs={{0,8},{1,9},{2,10},{3,11},{4,12},{5,13},{6,14},{7,15},{8,0},{9,1},... | collective-permute-start | bytes 7077896 | tf_op jit(solution)/shard_map/ppermute | solution.py:41
  479.4 49.8 %collective-permute-start.26 = (f32[4,1536]{1,0:T(4,128)S(1)}, f32[4,1536]{1,0:T(4,128)S(1)}, u32[]{:S(2)}, u32[]{:S(2)}) collective-permute-start(f32[4,1536]{1,0:T(4,128)S(1)} %pad_maximum_fusion), channel_id=1, source_target_pairs={{0,2},{1,3},{2,0},{3,1},{4,6},{5,7},{6,4},{7,5},{8,10},{9,11},{10,... | collective-permute-start | bytes 73736 | tf_op jit(solution)/shard_map/ppermute | solution.py:41
  532.3 117.0 %all-gather.21.cloned.1.call-start = ((), (), s32[]{:S(2)}) async-start(), calls=%async_computation.5 | async-start | bytes 5308416 | tf_op jit(solution)/shard_map/all_gather | solution.py:880
  532.3 39.1 %collective-permute-start.32 = (bf16[2,4,192,384]{3,2,1,0:T(8,128)(2,1)S(1)}, bf16[2,4,192,384]{3,2,1,0:T(8,128)(2,1)S(1)}, u32[]{:S(2)}, u32[]{:S(2)}) collective-permute-start(bf16[2,4,192,384]{3,2,1,0:T(8,128)(2,1)S(1)} %copy-done.32), channel_id=1, source_target_pairs={{0,16},{1,17},{2,18},{3,19},{4,20},{5,21},{6,22},{7,23},{8,24},{9,... | collective-permute-start | bytes 3538952 | tf_op jit(solution)/shard_map/ppermute | solution.py:41
  533.1 43.7 %collective-permute-start.31 = (bf16[1,192,1536]{2,1,0:T(8,128)(2,1)S(1)}, bf16[1,192,1536]{2,1,0:T(8,128)(2,1)S(1)}, u32[]{:S(2)}, u32[]{:S(2)}) collective-permute-start(bf16[1,192,1536]{2,1,0:T(8,128)(2,1)S(1)} %copy-done.35), channel_id=1, source_target_pairs={{0,2},{1,3},{2,0},{3,1},{4,6},{5,7},{6,4},{7,5},{8,10},{9,11},{10,... | collective-permute-start | bytes 1769480 | tf_op jit(solution)/shard_map/ppermute | solution.py:41
  580.6 77.2 %all-gather.19.cloned.1.call-start = ((), (), s32[]{:S(2)}) async-start(), calls=%async_computation.4 | async-start | bytes 5308416 | tf_op jit(solution)/shard_map/all_gather | solution.py:880
  603.6 31.4 %collective-permute-start.15 = (bf16[256,1536]{1,0:T(8,128)(2,1)S(1)}, bf16[256,1536]{1,0:T(8,128)(2,1)S(1)}, u32[]{:S(2)}, u32[]{:S(2)}) collective-permute-start(bf16[256,1536]{1,0:T(8,128)(2,1)S(1)} %copy-done.33), channel_id=1, source_target_pairs={{0,1},{1,0},{2,3},{3,2},{4,5},{5,4},{6,7},{7,6},{8,9},{9,8},{10,11... | collective-permute-start | bytes 2359304 | tf_op jit(solution)/shard_map/ppermute | solution.py:41
  (48 other events, 523.5 us)
Sparse Core Ops, SparseCore 0:
  48.7 35.3 all-gather.10
  86.6 24.0 all-gather.12
  113.2 38.9 all-gather.14
  153.8 38.9 all-gather.16
  532.4 46.1 all-gather.22
  580.7 36.2 all-gather.20
  618.9 38.9 all-gather.18

commit v3 on v2

v3 whole, which is shorter than its diff:
```python
import functools
import math

import jax
import jax.numpy as jnp
import numpy as np
from jax import lax
from jax.experimental import pallas as pl
from jax.experimental.pallas import tpu as pltpu
from jax.sharding import PartitionSpec as P

HD = 128
FF = 6144
EPS = 1e-05
AXES = ("dp", "tensor")
BF = jnp.bfloat16
F32 = jnp.float32
LOG2E = 1.4426950408889634
LONG = 200_000_000_000
VMEM_LIMIT = 56 * 1024 * 1024
VMEM_SPARE = 10 * 1024 * 1024

ODD, SIDE, LIMIT, NEAR_UNIT, FAR_UNIT = 0, 1, 4, 5, 6

NN = (((1,), (0,)), ((), ()))
NT = (((1,), (1,)), ((), ()))
TN = (((0,), (0,)), ((), ()))


def mm(a, b, dims=NN):
    return lax.dot_general(a, b, dims, preferred_element_type=F32)


def swap(value, dp_bits, tensor_bits):
    dp_size = lax.axis_size("dp")
    tensor_size = lax.axis_size("tensor")
    pairs = [
        (d * tensor_size + t, (d ^ dp_bits) * tensor_size + (t ^ tensor_bits))
        for d in range(dp_size)
        for t in range(tensor_size)
    ]
    return lax.ppermute(value, AXES, pairs)


class Chain:
    def __init__(self):
        self.last = None

    def __call__(self, call, *args):
        if self.last is not None:
            leaves, tree = jax.tree.flatten(args)
            leaves = lax.optimization_barrier(tuple(leaves) + (self.last,))[:-1]
            args = jax.tree.unflatten(tree, leaves)
        out = call(*args)
        self.last = jax.tree.leaves(out)[0]
        return out

    def wait(self, *args):
        return self(lambda *v: v[0] if len(v) == 1 else v, *args)


def dp_piece(weight):
    rows = weight.shape[0] // lax.axis_size("dp")
    return lax.dynamic_slice_in_dim(weight, lax.axis_index("dp") * rows, rows, 0)


def from_all(piece):
    return lax.all_gather(piece, "dp", axis=0, tiled=True)


def stacked_from_all(piece):
    whole = lax.all_gather(piece, "dp", axis=0, tiled=False)
    if piece.shape[1] % 16 == 0:
        return whole
    return whole.transpose(1, 0, 2, 3).reshape(1, 2, -1, piece.shape[2])


def block(shape, index=None):
    if index is None:
        return pl.BlockSpec(shape, lambda *_: (0,) * len(shape))
    return pl.BlockSpec(shape, index)


def shape_of(shape, kind=BF):
    return jax.ShapeDtypeStruct(shape, kind)


def kernel(body, grid, ins, outs, shapes, scratch=(), aliases=None, cost=1):
    def call(place, *args):
        pairs = list(zip(ins, args)) + list(zip(jax.tree.leaves(outs), jax.tree.leaves(shapes)))
        blocks = [
            2 * math.prod(spec.block_shape) * array.dtype.itemsize
            for spec, array in pairs
            if spec.block_shape is not None
        ]
        blocks += [math.prod(one.shape) * jnp.dtype(one.dtype).itemsize for one in scratch]
        return pl.pallas_call(
            body,
            grid_spec=pltpu.PrefetchScalarGridSpec(
                num_scalar_prefetch=1,
                grid=grid,
                in_specs=ins,
                out_specs=outs,
                scratch_shapes=list(scratch),
            ),
            out_shape=shapes,
            input_output_aliases=aliases or {},
            compiler_params=pltpu.CompilerParams(
                vmem_limit_bytes=min(VMEM_LIMIT, sum(blocks) + VMEM_SPARE)
            ),
            cost_estimate=pl.CostEstimate(flops=cost, bytes_accessed=1, transcendentals=0),
        )(place, *args)

    return call


def rows_at(start, size):
    return pl.ds(pl.multiple_of(start, size), size)


def norm_stats(values):
    center = values - jnp.mean(values, axis=-1, keepdims=True)
    spread = jnp.mean(center * center, axis=-1, keepdims=True)
    inverse = lax.rsqrt(spread + EPS)
    return center * inverse, inverse


def norm_back(grads, normal, inverse, gain):
    scaled = grads * gain
    mean_one = jnp.mean(scaled, axis=-1, keepdims=True)
    mean_two = jnp.mean(scaled * normal, axis=-1, keepdims=True)
    return (
        inverse * (scaled - mean_one - normal * mean_two),
        jnp.sum(grads * normal, axis=0, keepdims=True),
        jnp.sum(grads, axis=0, keepdims=True),
    )


def first_norm(place, tokens, gain, shift):
    rows, depth = tokens.shape
    half = rows // 2

    def body(_, x, gain, shift, low, high):
        normal, _ = norm_stats(x[...].astype(F32))
        value = (normal * gain[...] + shift[...]).astype(BF)
        pl.when(pl.program_id(0) == 0)(lambda: low.__setitem__(..., value))
        pl.when(pl.program_id(0) == 1)(lambda: high.__setitem__(..., value))

    return kernel(
        body,
        (2,),
        [block((half, depth), lambda i, _: (i, 0))] + [block((1, depth))] * 2,
        [block((half, depth))] * 2,
        [shape_of((half, depth))] * 2,
    )(place, tokens, gain, shift)


def rope_tables(length):
    frequency = np.exp(
        np.arange(HD // 2, dtype=np.float32) * np.float32(-2.0 * math.log(10000.0) / HD)
    ).astype(np.float32)
    angles = (np.arange(length, dtype=np.float32)[:, None] * frequency[None, :]).astype(np.float64)
    cos_part, sin_part = np.cos(angles), np.sin(angles)
    return (
        np.concatenate([cos_part, cos_part], axis=1).astype(np.float32),
        np.concatenate([-sin_part, sin_part], axis=1).astype(np.float32),
    )


def project(place, own, other, weight, tables, through=None):
    part, depth = own[0].shape
    width = weight.shape[2]

    def body(p, ol, oh, tl, th, weight, cos, sin, *refs):
        out = refs[-1]
        if through is not None:
            out = refs[1]
            pl.when(pl.program_id(0) < 2)(lambda: refs[2].__setitem__(..., refs[0][...]))
            pl.when(pl.program_id(0) >= 2)(lambda: refs[3].__setitem__(..., refs[0][...]))

        def go(source):
            x = source[...]
            for c in range(3):
                result = mm(x, weight[c])
                if c == 2:
                    out[c] = result.astype(BF)
                    continue
                for h in range(width // HD):
                    one = result[:, h * HD : (h + 1) * HD]
                    turned = one * cos[...] + pltpu.roll(one, HD // 2, 1) * sin[...]
                    out[c, :, h * HD : (h + 1) * HD] = turned.astype(BF)

        step = pl.program_id(0)
        at = jnp.where(step // 2 == p[ODD], 0, 2) + step % 2
        for i, source in enumerate((ol, oh, tl, th)):
            pl.when(at == i)(functools.partial(go, source))

    table = block((part, HD), lambda i, _: (i, 0))
    size = part // 2
    ins, outs = [], []
    if through is not None:
        ins = [block((size, depth), lambda i, _: (i, 0))]
        outs = [
            block((size, depth), lambda i, _: (jnp.minimum(i, 1), 0)),
            block((size, depth), lambda i, _: (jnp.maximum(i - 2, 0), 0)),
        ]
    return kernel(
        body,
        (4,),
        [block((part, depth))] * 4 + [block((3, depth, width)), table, table] + ins,
        [block((3, part, width), lambda i, _: (0, i, 0))] + outs,
        [shape_of((3, 4 * part, width))] + [shape_of((part, depth))] * len(outs),
    )(place, *own, *other, weight, *tables, *([through] if ins else []))


QB = 256


EXP_SCALE = HD ** (-0.5) * LOG2E


def masked(scores):
    key_at = lax.broadcasted_iota(jnp.int32, scores.shape, 0)
    row_at = lax.broadcasted_iota(jnp.int32, scores.shape, 1)
    return jnp.where(key_at <= row_at, scores, -1e30)


def probs_t(q, k_ref, first):
    diagonal = masked(mm(k_ref[0, first : first + QB], q, NT))
    top = jnp.max(diagonal, axis=0, keepdims=True)
    before = None
    if first:
        before = mm(k_ref[0, :first], q, NT)
        top = jnp.maximum(top, jnp.max(before, axis=0, keepdims=True))
    diagonal = jnp.exp2((diagonal - top) * EXP_SCALE)
    total = jnp.sum(diagonal, axis=0, keepdims=True)
    if first:
        before = jnp.exp2((before - top) * EXP_SCALE)
        total = total + jnp.sum(before, axis=0, keepdims=True)
    return before, diagonal, 1.0 / total


def attend(place, far, qkv, kept=()):
    _, length, width = qkv.shape
    heads = width // HD

    def body(_, q_ref, k_ref, v_ref, *refs):
        out_ref = refs[-1]
        for first in range(0, length, QB):
            last = first + QB
            before, diagonal, inverse = probs_t(q_ref[0, first:last], k_ref, first)
            blended = mm(v_ref[0, first:last], diagonal.astype(BF), TN)
            if first:
                blended = blended + mm(v_ref[0, :first], before.astype(BF), TN)
            out_ref[first:last, :] = (blended * inverse).T.astype(BF)

    spec = lambda c: block((1, length, HD), lambda h, _: (c, 0, h))
    return kernel(
        body,
        (heads,),
        [spec(0), spec(1), spec(2)] + [pl.BlockSpec(memory_space=pl.ANY)] * len(kept),
        [block((length, HD), lambda h, _: (0, h + heads * far))],
        [shape_of((length, 2 * width))],
        aliases={4 + i: i for i in range(len(kept))},
    )(place, qkv, qkv, qkv, *kept)


def attend_back(place, far, cost, qkv, own, other, w_out, tables, kept=()):
    _, length, width = qkv.shape
    heads = width // HD
    depth = w_out.shape[1]
    part = length // 4

    def unturn(grads, cos, sin):
        return (grads * cos - pltpu.roll(grads, HD // 2, 1) * sin).astype(BF)

    def body(p, q_ref, k_ref, v_ref, ol, oh, tl, th, w_ref, cos, sin, *refs):
        out, g_ref, dk_ref, dv_ref = refs[-4:]
        for base, low, high in ((p[ODD] * 2, ol, oh), ((1 - p[ODD]) * 2, tl, th)):
            g_ref[rows_at(base * part, part)] = mm(low[...], w_ref[...], NT).astype(BF)
            g_ref[rows_at((base + 1) * part, part)] = mm(high[...], w_ref[...], NT).astype(BF)
        for first in reversed(range(0, length, QB)):
            last = first + QB
            q = q_ref[0, first:last]
            g = g_ref[first:last]
            *weights, inverse = probs_t(q, k_ref, first)
            parts = []
            inner = 0.0
            for weight, here in zip(weights, (slice(0, first), slice(first, last))):
                if weight is None:
                    continue
                grad_probs = mm(v_ref[0, here], g, NT)
                inner = inner + jnp.sum(weight * grad_probs, axis=0, keepdims=True)
                parts.append((here, weight, grad_probs))
            inner = inner * inverse
            scaled = inverse * HD ** (-0.5)
            grad_q = 0.0
            for here, weight, grad_probs in parts:
                grad_scores = (weight * ((grad_probs - inner) * scaled)).astype(BF)
                grad_v = mm((weight * inverse).astype(BF), g)
                grad_k = mm(grad_scores, q)
                if last == length:
                    dv_ref[here] = grad_v
                    dk_ref[here] = grad_k
                else:
                    dv_ref[here] += grad_v
                    dk_ref[here] += grad_k
                grad_q = grad_q + mm(grad_scores, k_ref[0, here], TN)
            out[0, first:last] = unturn(grad_q, cos[first:last], sin[first:last])
        out[1] = unturn(dk_ref[...], cos[...], sin[...])
        out[2] = dv_ref[...].astype(BF)

    spec = lambda c: block((1, length, HD), lambda h, _: (c, 0, h))
    piece = block((part, depth))
    table = block((length, HD))
    return kernel(
        body,
        (heads,),
        [spec(0), spec(1), spec(2)]
        + [piece] * 4
        + [block((HD, depth), lambda h, _: (h, 0)), table, table]
        + [pl.BlockSpec(memory_space=pl.ANY)] * len(kept),
        [block((3, length, HD), lambda h, _: (0, 0, h + heads * far))],
        [shape_of((3, length, 2 * width))],
        [pltpu.VMEM((length, HD), BF), pltpu.VMEM((length, HD), F32), pltpu.VMEM((length, HD), F32)],
        {11 + i: i for i in range(len(kept))},
        cost,
    )(place, qkv, qkv, qkv, *own, *other, w_out, *tables, *kept)


def head_rows(place, leave, heads, w_near, w_far):
    length, width = heads.shape
    depth = w_near.shape[1]
    half = length // 4
    kind = BF if leave else F32
    cols = depth // 2

    def body(_, heads, w_near, w_far, low, high):
        total = mm(heads[...], jnp.concatenate([w_near[...], w_far[...]], axis=0))
        low[...] = total[:half].astype(kind)
        high[...] = total[half:].astype(kind)

    weight = block((width // 2, cols), lambda i, p: (0, i))
    return kernel(
        body,
        (2,),
        [
            block((2 * half, width), lambda i, p: (1 - p[ODD] if leave else p[ODD], 0)),
            weight,
            weight,
        ],
        [block((half, cols), lambda i, p: (0, i))] * 2,
        [shape_of((half, depth), kind)] * 2,
    )(place, heads, w_near, w_far)


def second_norm(place, which, stay, tokens, arrived, gain, shift):
    half, depth = stay.shape
    size = half // 2

    def body(_, stay, tokens, arrived, gain, shift, normed, resid):
        total = tokens[...].astype(F32) + stay[...] + arrived[...].astype(F32)
        resid[...] = total
        normal, _ = norm_stats(total)
        normed[...] = (normal * gain[...] + shift[...]).astype(BF)

    piece = block((size, depth), lambda i, _: (i, 0))
    return kernel(
        body,
        (2,),
        [piece, block((size, depth), lambda i, _: (2 * which + i, 0)), piece]
        + [block((1, depth))] * 2,
        [piece] * 2,
        [shape_of((half, depth)), shape_of((half, depth), F32)],
    )(place, stay, tokens, arrived, gain, shift)


def gelu_pair(v):
    c = math.sqrt(2.0 / math.pi)
    square = v * v
    t = jnp.tanh(v * (c + (c * 0.044715) * square))
    half = 0.5 + 0.5 * t
    slope = half + v * (0.5 - 0.5 * t * t) * (c + (3.0 * 0.044715 * c) * square)
    return v * half, slope


UB = 768
SB = 256


def hidden_grads(place, cost, rows_in, weight):
    each, depth = rows_in[0].shape
    count = each * len(rows_in)
    parts, _, rows, _ = weight.shape
    units = parts * rows
    step = UB // rows if rows < UB else 1
    tile = (step, 1, min(rows, UB), depth)
    last = weight.shape[1] - 1

    def body(_, *refs):
        *sources, weight, out = refs
        w = weight[:, 0].reshape(UB, depth)
        for i, source in enumerate(sources):
            out[i * each : (i + 1) * each] = mm(source[...], w, NT).astype(BF)

    place_of = lambda j: (j, last, 0, 0) if rows <= UB else (0, last, j, 0)
    return kernel(
        body,
        (units // UB,),
        [block((each, depth))] * len(rows_in) + [block(tile, lambda j, _: place_of(j))],
        block((count, UB), lambda j, _: (0, j)),
        shape_of((count, units)),
        cost=cost,
    )(place, *rows_in, weight)


def feed(group, place, normed, normed_far, cot, cot_far, w_up, far_pair, hidden_grad, kept=()):
    half, depth = normed.shape
    size = 2 * half
    units = w_up.shape[1]
    near_steps = units // UB
    far_parts, _, far_rows, _ = far_pair.shape

    def body(p, own, other, g_own, g_other, un, uf, gno, gnt, gfo, gft, *refs):
        hn, pn, hf, pf, rows, grads, stay, leave, total = refs[-9:]
        step = pl.program_id(0)

        @pl.when(step == 0)
        def _():
            total[...] = jnp.zeros_like(total)
            rows[:half] = own[...]
            rows[half:] = other[...]
            grads[:half] = g_own[...]
            grads[half:] = g_other[...]

        def work(up, grad_own, grad_other, hidden, pre):
            for at in range(0, UB, SB):
                there = slice(at, at + SB)
                value, slope = gelu_pair(mm(rows[...], up[:, there]))
                hidden[:, there] = value.astype(BF)
                pre[:half, there] = (grad_own[:, there].astype(F32) * slope[:half]).astype(BF)
                pre[half:, there] = (grad_other[:, there].astype(F32) * slope[half:]).astype(BF)
            total[...] += mm(pre[...], up, NT)

        def part(first_unit, up, grad_own, grad_other, hidden, pre):
            live = first_unit < p[LIMIT]

            @pl.when(live)
            def _():
                work(up(), grad_own, grad_other, hidden, pre)

            @pl.when(jnp.logical_not(live))
            def _():
                hidden[...] = jnp.zeros((size, UB), BF)
                pre[...] = jnp.zeros((size, UB), BF)

        @pl.when(step < near_steps)
        def _():
            part(p[NEAR_UNIT] + step * UB, lambda: un[...], gno, gnt, hn, pn)

        @pl.when(step >= near_steps)
        def _():
            far_up = lambda: uf[:, 0].reshape(depth, UB)
            part(p[FAR_UNIT] + (step - near_steps) * UB, far_up, gfo, gft, hf, pf)

        @pl.when(step == 2 * near_steps - 1)
        def _():
            stay[...] = total[:half]
            leave[...] = total[half:].astype(BF)

    near = lambda j: jnp.minimum(j, near_steps - 1)
    far = lambda j: jnp.maximum(j - near_steps, 0)
    wide = [block((size, UB), lambda j, _, at=at: (group, at(j))) for at in (near, far)]
    slim = [block((half, UB), lambda j, _, at=at: (1 - group, at(j))) for at in (near, far)]
    piece = block((half, depth))
    rows = block((size, depth), lambda j, _: (group, 0))
    return kernel(
        body,
        (2 * near_steps,),
        [piece, piece, block((half, depth), lambda j, _: (1 - group, 0)), piece]
        + [block((depth, UB), lambda j, _: (0, near(j)))]
        + [block((far_parts, 1, far_rows, UB), lambda j, _: (0, 0, 0, far(j)))]
        + [slim[0], slim[0], slim[1], slim[1]]
        + [pl.BlockSpec(memory_space=pl.ANY)] * len(kept),
        [wide[0], wide[0], wide[1], wide[1], rows, rows, piece, piece],
        [shape_of((2 * size, units))] * 4
        + [shape_of((2 * size, depth))] * 2
        + [shape_of((half, depth), F32), shape_of((half, depth))],
        [pltpu.VMEM((size, depth), F32)],
        {11 + i: i for i in range(len(kept))},
    )(place, normed, normed_far, cot, cot_far, w_up, far_pair, *hidden_grad, *kept)


def second_back(place, which, resid, stay, arrived, cot, gain):
    half, depth = resid.shape
    size = half // 2

    def body(_, resid, stay, arrived, cot, gain, low, wide, gain_sum, shift_sum):
        normal, inverse = norm_stats(resid[...])
        grad, gains, shifts = norm_back(
            stay[...] + arrived[...].astype(F32), normal, inverse, gain[...]
        )
        grad = grad + cot[...].astype(F32)
        wide[...] = grad
        low[...] = grad.astype(BF)

        @pl.when(pl.program_id(0) == 0)
        def _():
            gain_sum[...] = gains
            shift_sum[...] = shifts

        @pl.when(pl.program_id(0) > 0)
        def _():
            gain_sum[...] += gains
            shift_sum[...] += shifts

    piece = block((size, depth), lambda i, _: (i, 0))
    vector = block((1, depth))
    return kernel(
        body,
        (2,),
        [piece] * 3 + [block((size, depth), lambda i, _: (2 * which + i, 0)), vector],
        [piece, piece, vector, vector],
        [shape_of((half, depth)), shape_of((half, depth), F32)] + [shape_of((1, depth), F32)] * 2,
    )(place, resid, stay, arrived, cot, gain)


def down_rows(place, near, far, w_near, far_pair, resid_high, resid_low):
    rows, units = near.shape
    depth = w_near.shape[1]
    half = rows // 4
    cols = depth // 3
    far_parts, _, far_rows, _ = far_pair.shape

    def body(_, near, far, w_near, w_far, resid_high, resid_low, high, low, out_high, out_low):
        w_second = w_far[:, 0].reshape(units, cols)
        for i, (stay, resid, leave) in enumerate(
            ((out_high, resid_high, high), (out_low, resid_low, low))
        ):
            here = slice(2 * i * half, 2 * (i + 1) * half)
            total = mm(near[here], w_near[...]) + mm(far[here], w_second)
            stay[...] = total[:half] + resid[...]
            leave[...] = total[half:].astype(BF)

    hidden = block((rows, units))
    piece = block((half, cols), lambda j, _: (0, j))
    return kernel(
        body,
        (3,),
        [
            hidden,
            hidden,
            block((units, cols), lambda j, _: (0, j)),
            block((far_parts, 1, far_rows, cols), lambda j, _: (0, 1, 0, j)),
            piece,
            piece,
        ],
        [piece] * 4,
        [shape_of((half, depth))] * 2 + [shape_of((half, depth), F32)] * 2,
        cost=LONG,
    )(place, near, far, w_near, far_pair, resid_high, resid_low)


def layer_rows(place, out_low, out_high, low, high):
    half, depth = low.shape

    def body(_, out_low, out_high, low, high, out):
        out[:half] = (out_low[...] + low[...].astype(F32)).astype(BF)
        out[half:] = (out_high[...] + high[...].astype(F32)).astype(BF)

    piece = block((half, depth))
    return kernel(body, (1,), [piece] * 4, block((2 * half, depth)), shape_of((2 * half, depth)))(
        place, out_low, out_high, low, high
    )


def wide_grad(place, bit, lefts, rights, arrived=None):
    rows, width = lefts[0].shape
    depth = rights[0].shape[1]
    half = width // 2
    cols = depth // 2
    last = arrived is not None

    def body(p, l0, l1, r0, r1, *refs):
        turned = refs[-1]
        shard = pl.program_id(0)

        @pl.when(pl.program_id(1) == 0)
        def _():
            pl.when(shard == 0)(lambda: turned.__setitem__(..., l0[...].T))
            pl.when(shard == 1)(lambda: turned.__setitem__(..., l1[...].T))

        def go(right):
            if not last:
                refs[0][0, 0] = mm(turned[...], right[...]).astype(BF)
                return
            for out, side in ((refs[1], p[SIDE + bit]), (refs[2], 1 - p[SIDE + bit])):
                here = rows_at(side * (half // 2), half // 2)
                value = mm(turned[here], right[...]) + refs[0][0, 0, here].astype(F32)
                out[0, 0] = value.astype(BF)

        pl.when(shard == 0)(lambda: go(r0))
        pl.when(shard == 1)(lambda: go(r1))

    side = lambda p: p[SIDE] if last else 1 - p[SIDE]
    left = block((rows, half), lambda s, j, p: (0, side(p)))
    right = lambda shard: block(
        (rows, cols), lambda s, j, p: (0, jnp.where(s == shard, j, 1 - shard))
    )
    tall = lambda size: block((1, 1, size, cols), lambda s, j, p: (s, 0, 0, j))
    if last:
        outs = [tall(half // 2)] * 2
        shapes = [shape_of((2, 1, half // 2, depth))] * 2
    else:
        outs, shapes = tall(half), shape_of((2, 1, half, depth))
    return kernel(
        body,
        (2, 2),
        [left, left, right(0), right(1)] + [tall(half)] * last,
        outs,
        shapes,
        [pltpu.VMEM((half, rows), BF)],
    )(place, *lefts, *rights, *([arrived] if last else []))


def narrow_grad(place, own, other, rights, dests, arrived=(), kept=()):
    rows, depth = own[0].shape
    parts = len(own)
    count, length, width = rights.shape
    half = depth // 2
    last = len(arrived) > 0
    n_out = 2 if last else 1
    size = half // 2 if last else half

    def body(p, *refs):
        own, other, right = refs[:parts], refs[parts : 2 * parts], refs[2 * parts]
        got = refs[2 * parts + 1 : 2 * parts + 1 + len(arrived)]
        outs, turned = refs[-1 - n_out * len(dests) : -1], refs[-1]
        c = pl.program_id(0)

        @pl.when(c == 0)
        def _():
            for lefts, base in ((own, p[ODD]), (other, 1 - p[ODD])):
                for i, left in enumerate(lefts):
                    turned[:, rows_at((base * parts + i) * rows, rows)] = left[...].T

        def go(i, bit):
            if not last:
                value = mm(turned[...], right[0]).astype(BF)
                outs[i][0, 0] = value[:, : width // 2]
                outs[i][1, 0] = value[:, width // 2 :]
                return
            for out, side in ((outs[2 * i], p[SIDE + bit]), (outs[2 * i + 1], 1 - p[SIDE + bit])):
                here = rows_at(side * size, size)
                value = mm(turned[here], right[0])
                for shard in range(2):
                    there = slice(shard * width // 2, (shard + 1) * width // 2)
                    out[shard, 0] = (value[:, there] + got[i][shard, 0, here].astype(F32)).astype(BF)

        for i, (first, many, _, _, bit) in enumerate(dests):
            pl.when((c >= first) & (c < first + many))(functools.partial(go, i, bit))

    side = lambda p: p[SIDE] if last else 1 - p[SIDE]
    left = block((rows, half), lambda c, p: (0, side(p)))

    def tall(dest, size):
        first, many, _, at, _ = dest
        return block(
            (2, 1, size, width // 2), lambda c, p: (0, at + jnp.clip(c - first, 0, many - 1), 0, 0)
        )

    ins = [left] * (2 * parts) + [block((1, length, width), lambda c, p: (c, 0, 0))]
    ins += [tall(dest, half) for dest in dests] * last
    return kernel(
        body,
        (count,),
        ins + [pl.BlockSpec(memory_space=pl.ANY)] * len(kept),
        [tall(dest, size) for dest in dests for _ in range(n_out)],
        [shape_of((2, dest[2], size, width // 2)) for dest in dests for _ in range(n_out)],
        [pltpu.VMEM((half, length), BF)],
        {1 + len(ins) + i: i for i in range(len(kept))},
    )(place, *own, *other, rights, *arrived, *kept)


def add_split(place, bits, *pairs):
    _, count, rows, width = pairs[0].shape
    half = rows // 2

    def body(p, *refs):
        for i, bit in enumerate(bits):
            mine, theirs = refs[2 * i : 2 * i + 2]
            outs = refs[2 * (len(bits) + i) : 2 * (len(bits) + i) + 2]
            for out, side in zip(outs, (p[SIDE + bit], 1 - p[SIDE + bit])):
                here = rows_at(side * half, half)
                out[0, 0] = (mine[0, 0, here].astype(F32) + theirs[0, 0, here].astype(F32)).astype(BF)

    full = block((1, 1, rows, width), lambda s, c, p: (s, c, 0, 0))
    out = block((1, 1, half, width), lambda s, c, p: (s, c, 0, 0))
    n = 2 * len(bits)
    return kernel(
        body, (2, count), [full] * n, [out] * n, [shape_of((2, count, half, width))] * n
    )(place, *pairs)


def add_last(place, *pairs):
    _, count, rows, width = pairs[0].shape
    n = len(pairs) // 2

    def body(_, *refs):
        near, far = refs[-2:]
        for i in range(n):
            for shard, out in ((0, near), (1, far)):
                for c in range(count):
                    mine, theirs = refs[2 * i][shard, c], refs[2 * i + 1][shard, c]
                    out[i * count + c] = (mine.astype(F32) + theirs.astype(F32)).astype(BF)

    full = block((2, count, rows, width))
    out = block((n * count, rows, width))
    return kernel(
        body, (1,), [full] * (2 * n), [out, out], [shape_of((n * count, rows, width))] * 2
    )(place, *pairs)


def add_pair(place, near, arrived):
    shape = near.shape

    def body(_, mine, theirs, out):
        out[...] = (mine[...].astype(F32) + theirs[...].astype(F32)).astype(BF)

    full = block(shape)
    return kernel(body, (1,), [full, full], full, shape_of(shape))(place, near, arrived)


def assemble(table, whole):
    size, _, rows, width = whole.shape

    def body(_, one, two, out_one, out_two):
        out_one[...] = one[0, 0].astype(F32)
        out_two[...] = two[0, 0].astype(F32)

    piece = lambda i: block((1, 1, rows, width), lambda j, t: (t[size * i + j], i, 0, 0))
    return kernel(
        body,
        (size,),
        [piece(0), piece(1)],
        [block((rows, width), lambda j, t: (j, 0))] * 2,
        [shape_of((rows * size, width), F32)] * 2,
    )(table, whole, whole)


def assemble_heads(table, whole):
    size, count, rows, width = whole.shape
    group = 2 if 2 * rows % 128 == 0 else size

    def body(_, *refs):
        pieces, (out, last) = refs[:-2], refs[-2:]
        for i in range(group):
            here = slice(i * rows, (i + 1) * rows)
            one, two = pieces[2 * i : 2 * i + 2]
            out[:2, here] = one[0].astype(F32)
            out[2, here] = two[0, 0].astype(F32)
        turned = jnp.concatenate([pieces[2 * i + 1][0, 1] for i in range(group)], axis=0)
        last[...] = turned.astype(F32).T

    piece = lambda i, k: block(
        (1, 2, rows, width), lambda j, t: (t[size * k + group * j + i], k, 0, 0)
    )
    return kernel(
        body,
        (size // group,),
        [piece(i, k) for i in range(group) for k in range(2)],
        [
            block((count - 1, group * rows, width), lambda j, t: (0, j, 0)),
            block((width, group * rows), lambda j, t: (0, j)),
        ],
        [shape_of((count - 1, rows * size, width), F32), shape_of((width, rows * size), F32)],
    )(table, *([whole] * (2 * group)))


def back_rows(place, leave, proj, w_near, w_far):
    count, length, width = proj.shape
    depth = w_near.shape[1]
    rows = length // 2
    cols = depth // 3
    kind = BF if leave else F32

    def body(_, proj, w_near, w_far, out):
        total = 0.0
        for c in range(count):
            weight = jnp.concatenate([w_near[c], w_far[c]], axis=1)
            total = total + mm(proj[c], weight, NT)
        out[...] = total.astype(kind)

    weight = block((count, cols, width // 2), lambda j, p: (0, j, 0))
    return kernel(
        body,
        (3,),
        [
            block((count, rows, width), lambda j, p: (0, 1 - p[ODD] if leave else p[ODD], 0)),
            weight,
            weight,
        ],
        block((rows, cols), lambda j, p: (0, j)),
        shape_of((rows, depth), kind),
        cost=LONG,
    )(place, proj, w_near, w_far)


def first_back(place, tokens, stay, arrived, resid_low, resid_high, gain):
    rows, depth = tokens.shape
    half = rows // 2

    def body(_, tokens, stay, arrived, resid_low, resid_high, gain, out, gain_sum, shift_sum):
        normal, inverse = norm_stats(tokens[...].astype(F32))
        grad, gains, shifts = norm_back(
            stay[...] + arrived[...].astype(F32), normal, inverse, gain[...]
        )

        @pl.when(pl.program_id(0) == 0)
        def _():
            out[...] = grad + resid_low[...]
            gain_sum[...] = gains
            shift_sum[...] = shifts

        @pl.when(pl.program_id(0) == 1)
        def _():
            out[...] = grad + resid_high[...]
            gain_sum[...] += gains
            shift_sum[...] += shifts

    tile = block((half, depth), lambda i, _: (i, 0))
    piece = block((half, depth))
    vector = block((1, depth))
    return kernel(
        body,
        (2,),
        [tile, tile, tile, piece, piece, vector],
        [tile, vector, vector],
        [shape_of((rows, depth), F32)] + [shape_of((1, depth), F32)] * 2,
        cost=LONG,
    )(place, tokens, stay, arrived, resid_low, resid_high, gain)


def shards(
    tokens,
    granularity,
    gain_one,
    shift_one,
    w_qkv,
    w_out,
    gain_two,
    shift_two,
    w_up,
    w_down,
    cotangent,
):
    tensor_size = lax.axis_size("tensor")
    dp_size = lax.axis_size("dp")
    rank = lax.axis_index("tensor")
    dp_at = lax.axis_index("dp")
    local_rows, depth = tokens.shape
    seq_len = local_rows * tensor_size // granularity.shape[0]
    assert tensor_size == 4 and seq_len == 2 * local_rows and dp_size % 8 == 0
    half = local_rows // 2
    hidden_here = w_up.shape[1]
    head_width = w_qkv.shape[2]
    bits = dp_size.bit_length() - 1
    tables = [jnp.asarray(t) for t in rope_tables(seq_len)]
    gain_one, shift_one, gain_two, shift_two = (
        v[None, :] for v in (gain_one, shift_one, gain_two, shift_two)
    )
    limits = jnp.left_shift(jnp.ones_like(granularity), granularity) * (FF // 8)
    upper = rank // 2
    place = jnp.stack(
        [
            rank % 2,
            dp_at & 1,
            (dp_at >> 1) & 1,
            (dp_at >> 2) & 1,
            jnp.where(upper == 0, limits[0], limits[1]),
            rank * hidden_here,
            (rank ^ 2) * hidden_here,
        ]
    ).astype(jnp.int32)
    chain = Chain()
    run = lambda call, *args: chain(functools.partial(call, place), *args)

    piece_qkv = swap(chain(dp_piece, w_qkv.reshape(3 * depth, head_width)), 0, 2)
    normed = run(first_norm, tokens, gain_one, shift_one)
    normed_far = [swap(v, 0, 1) for v in normed]
    w_down_own = w_down[None, None]
    own_near = chain(lambda *a: hidden_grads(place, LONG, *a), [cotangent], w_down_own)
    normed_far[0], piece_qkv = chain.wait(normed_far[0], piece_qkv)
    w_qkv_far = from_all(piece_qkv).reshape(w_qkv.shape)
    piece_out, piece_pair = chain(
        lambda a, b, c: (dp_piece(a), jnp.stack([dp_piece(b), dp_piece(c)])), w_out, w_up, w_down
    )
    piece_out, piece_pair = swap(piece_out, 0, 2), swap(piece_pair, 0, 2)
    normed_far[1], piece_out = chain.wait(normed_far[1], piece_out)
    w_out_far = from_all(piece_out)
    qkv_near, *cot_far = run(project, normed, normed_far, w_qkv, tables, cotangent)
    cot_far = [swap(v, 0, 1) for v in cot_far]
    heads = chain(lambda *a: attend(place, 0, *a), qkv_near)
    (qkv_far,) = run(project, normed, normed_far, w_qkv_far, tables)
    (heads,) = chain(lambda *a: attend(place, 1, *a), qkv_far, heads)
    cot_far[1], piece_pair = chain.wait(cot_far[1], piece_pair)
    far_pair = stacked_from_all(piece_pair)
    low, high = chain(lambda *a: head_rows(place, True, *a), heads, w_out, w_out_far)
    high, low = swap(high, 0, 1), swap(low, 0, 1)
    stay_low, stay_high = chain(lambda *a: head_rows(place, False, *a), heads, w_out, w_out_far)
    norm_args = (gain_two, shift_two)
    normed_high, resid_high = chain(
        lambda *a: second_norm(place, 1, *a), stay_high, tokens, high, *norm_args
    )
    normed_high_far = swap(normed_high, 0, 1)
    other_near = chain(lambda *a: hidden_grads(place, 1, *a), cot_far, w_down_own)
    normed_low, resid_low = chain(
        lambda *a: second_norm(place, 0, *a), stay_low, tokens, low, *norm_args
    )
    normed_low_far = swap(normed_low, 0, 1)
    other_far = chain(lambda *a: hidden_grads(place, 1, *a), cot_far, far_pair)
    own_far = chain(lambda *a: hidden_grads(place, 1, *a), [cotangent], far_pair)

    weights = (w_up, far_pair, (own_near, other_near, own_far, other_far))
    *kept, stay_high, leave_high = chain(
        lambda *a: feed(0, place, *a), normed_high, normed_high_far, cotangent, cot_far[1], *weights
    )
    back_high = swap(leave_high, 0, 1)
    *kept, stay_low, leave_low = chain(
        lambda *a: feed(1, place, *a),
        normed_low,
        normed_low_far,
        cotangent,
        cot_far[0],
        *weights,
        kept,
    )
    back_low = swap(leave_low, 0, 1)
    hidden_near, pre_near, hidden_far, pre_far, rows_two, grad_rows = kept
    ups = ((rows_two, rows_two), (pre_near, pre_far))
    downs = ((hidden_near, hidden_far), (grad_rows, grad_rows))
    grad_high, wide_high, gain_high, shift_high = chain(
        lambda *a: second_back(place, 1, *a), resid_high, stay_high, back_high, cotangent, gain_two
    )
    up = swap(chain(lambda *a: wide_grad(place, None, *a), *ups), 1, 0)
    down = swap(chain(lambda *a: wide_grad(place, None, *a), *downs), 1, 0)
    up_keep, up = chain(lambda *a: wide_grad(place, 1, *a), *ups, up)
    grad_low, wide_low, gain_low, shift_low = chain(
        lambda *a: second_back(place, 0, *a), resid_low, stay_low, back_low, cotangent, gain_two
    )
    grad_high_far, grad_low_far = swap(grad_high, 0, 1), swap(grad_low, 0, 1)
    down_keep, down = chain(lambda *a: wide_grad(place, 2, *a), *downs, down)
    up, down = swap(up, 2, 0), swap(down, 4, 0)
    grad_high_far, grad_low_far = chain.wait(grad_high_far, grad_low_far)

    own, other = (grad_low, grad_high), (grad_low_far, grad_high_far)
    proj = chain(
        lambda *a: attend_back(place, 1, 1, *a), qkv_far, own, other, w_out_far, tables
    )
    up, down = chain.wait(up, down)
    up_keep, up, down_keep, down = chain(
        lambda *a: add_split(place, (2, 1), *a), up_keep, up, down_keep, down
    )
    up, down = swap(up, 4, 0), swap(down, 2, 0)
    (proj,) = chain(
        lambda *a: attend_back(place, 0, 1, *a), qkv_near, own, other, w_out, tables, proj
    )
    first_dests, second_dests = [(0, 2, 2, 0, 1), (2, 1, 2, 0, 2)], [(0, 1, 2, 1, 2)]
    first, second = chain(
        lambda *a: narrow_grad(place, *a[:3], first_dests), normed, normed_far, proj
    )
    (second,) = chain(
        lambda *a: narrow_grad(place, *a[:3], second_dests, kept=a[3]),
        own,
        other,
        heads[None],
        [second],
    )
    first, second = swap(first, 1, 0), swap(second, 1, 0)
    up, down = chain.wait(up, down)
    wide_near, wide_far = run(add_last, up_keep, up, down_keep, down)
    wide_far = swap(wide_far, 0, 2)
    stay_one = chain(lambda *a: back_rows(place, False, *a), proj, w_qkv, w_qkv_far)
    first, second = chain.wait(first, second)
    first_keep, first, *kept = chain(
        lambda *a: narrow_grad(place, *a[:3], first_dests, a[3]),
        normed,
        normed_far,
        proj,
        [first, second],
    )
    second_keep, second = chain(
        lambda *a: narrow_grad(place, *a[:3], second_dests, a[3], a[4]),
        own,
        other,
        heads[None],
        [second],
        kept,
    )
    first, second = swap(first, 2, 0), swap(second, 4, 0)
    leave_one = chain(lambda *a: back_rows(place, True, *a), proj, w_qkv, w_qkv_far)
    back_one = swap(leave_one, 0, 1)
    out_high_leave, out_low_leave, out_high, out_low = run(
        down_rows, hidden_near, hidden_far, w_down, far_pair, resid_high, resid_low
    )
    out_high_far, out_low_far = swap(out_high_leave, 0, 1), swap(out_low_leave, 0, 1)

    def gather(near, arrived):
        piece = run(add_pair, near, arrived)
        for bit in range(3, bits):
            size = piece.shape[1] // 2
            side = (dp_at >> bit) & 1
            mine = lax.dynamic_slice_in_dim(piece, side * size, size, 1)
            theirs = lax.dynamic_slice_in_dim(piece, (1 - side) * size, size, 1)
            piece = add_pair(place, mine, swap(theirs, 1 << bit, 0))
        return lax.all_gather(piece, "dp", axis=0, tiled=False)

    def order_table(order):
        order = order + list(range(3, bits))
        return [
            sum(((j >> (bits - 1 - i)) & 1) << bit for i, bit in enumerate(order))
            for j in range(dp_size)
        ]

    first_keep, first, second_keep, second = chain(
        lambda *a: add_split(place, (2, 1), *a), first_keep, first, second_keep, second
    )
    first, second = swap(first, 4, 0), swap(second, 2, 0)
    wide_all = gather(wide_near, wide_far)
    heads_near, heads_far = run(add_last, first_keep, first, second_keep, second)
    heads_far = swap(heads_far, 0, 2)
    grad_tokens, gain_sum, shift_sum = run(
        first_back, tokens, stay_one, back_one, wide_low, wide_high, gain_one
    )
    sums = chain(
        lambda *a: jnp.concatenate(a, axis=0),
        gain_sum,
        shift_sum,
        gain_low + gain_high,
        shift_low + shift_high,
    )
    steps = [(0, 2), (0, 1)] + [(1 << b, 0) for b in range(bits)]
    sums = chain(lambda a, b: a + b, sums, swap(sums, *steps.pop()))
    heads_all = gather(heads_near, heads_far)
    while steps:
        sums = chain(lambda a, b: a + b, sums, swap(sums, *steps.pop()))
    layer_out = run(layer_rows, out_low, out_high, out_low_far, out_high_far)
    xy, yx = order_table([0, 1, 2]), order_table([0, 2, 1])
    table = jnp.asarray(xy + yx, jnp.int32)
    grad_up, grad_down = chain(lambda v: assemble(table, v), wide_all)
    grad_qkv, grad_out = chain(lambda v: assemble_heads(table, v), heads_all)
    return (
        layer_out,
        grad_tokens,
        sums[0],
        sums[1],
        grad_qkv,
        grad_out,
        sums[2],
        sums[3],
        grad_up,
        grad_down,
    )


def solution(mesh):
    rows = P(AXES, None)
    params = (P(), P(), P(None, None, "tensor"), P("tensor", None))
    wide = (P(None, "tensor"), P("tensor", None))
    return jax.shard_map(
        shards,
        mesh=mesh,
        in_specs=(rows, P("dp")) + params + (P(), P()) + wide + (rows,),
        out_specs=(rows, rows) + params + (P(), P()) + wide,
        check_vma=False,
    )
```

time: 691 us -> 591 us (0.86)
  Pallas kernels: 344 us -> 258 us
  waiting for transfers between devices: 240 us -> 201 us
  local copies, waits for them, and re-layouts: 28 us -> 66.5 us
  starting transfers between devices: 47.5 us -> 36.9 us
    pallas_call x40, Pallas kernels: 344 us -> 258 us  [call(): pl.pallas_call(body, grid_spec=pltpu.PrefetchScalarGridSpec(num_scalar_pr...]
    unnamed x75 -> x194, local copies, waits for them, and re-layouts: 14.9 us -> 59.4 us
    ppermute x36 -> x37, waiting for transfers between devices: 240 us -> 198 us  [swap(): return lax.ppermute(value, AXES, pairs)]
    ppermute x36 -> x37, starting transfers between devices: 46.4 us -> 36.5 us  [swap(): return lax.ppermute(value, AXES, pairs)]
  transfers between devices with their start and end apart: 43 -> 42, of which waited for: 22 -> 24; matrix products, arithmetic and copies ran while one was open for 1% -> 1% of each run, Pallas kernels for 43% -> 40%
where the time goes in v3:
time: 591 us; the launch traced here: 582 us
  Pallas kernels  258 us (44%)
  waiting for transfers between devices  201 us (34%)
  local copies, waits for them, and re-layouts  66.5 us (11%)
  starting transfers between devices  36.9 us (6%)
  between operations  16.2 us (3%)
    pallas_call x40, Pallas kernels, call(): pl.pallas_call(body, grid_spec=pltpu.PrefetchScalarGridSpec(num_scalar_pr...  258 us
    ppermute x37, waiting for transfers between devices, swap(): return lax.ppermute(value, AXES, pairs)  198 us
    unnamed x194, local copies, waits for them, and re-layouts  59.4 us
    ppermute x37, starting transfers between devices, swap(): return lax.ppermute(value, AXES, pairs)  36.5 us
  transfers between devices with their start and end apart: 42, of which 24 were waited for; matrix products, arithmetic and copies ran while one was open for 1% of the time, Pallas kernels for 40%

profile of v3, /device:TPU:0, one launch (start us, length us, event | category | flops | bytes accessed | tf_op | source)
XLA Modules:
  0.0 581.8 jit_solution(9913753957141053511)
XLA Ops:
  33.3 15.7 %collective-permute-done.tl.refs_2_ = bf16[256,1536]{1,0:T(8,128)(2,1)} collective-permute-done((bf16[256,1536]{1,0:T(8,128)(2,1)}, bf16[256,1536]{1,0:T(8,128)(2,1)}, u32[]{:S(2)}, u32[]{:S(2)}) %collective-permute-start) | collective-permute-done | bytes 786464 | tf_op jit(solution)/shard_map/ppermute | solution.py:42
  53.1 18.0 %collective-permute-done.2.th.refs_3_ = bf16[256,1536]{1,0:T(8,128)(2,1)S(1)} collective-permute-done((bf16[256,1536]{1,0:T(8,128)(2,1)S(1)}, bf16[256,1536]{1,0:T(8,128)(2,1)S(1)}, u32[]{:S(2)}, u32[]{:S(2)}) %collective-permute-start.2) | collective-permute-done | bytes 786464 | tf_op jit(solution)/shard_map/ppermute | solution.py:42
  75.7 8.8 %shard_map.215 = (bf16[3,1024,384]{2,1,0:T(8,128)(2,1)S(1)}, bf16[256,1536]{1,0:T(8,128)(2,1)S(1)}, bf16[256,1536]{1,0:T(8,128)(2,1)}) custom-call(s32[7]{0:T(128)S(1)} %stack.40._.p, bf16[256,1536]{1,0:T(8,128)(2,1)} %get-tuple-element.500.ol.refs_0_, bf16[256,1536]{1,0:T(8,128)(2,1)S(1)} %get-tuple-element.501.oh.refs_1_, ...), custom_call_target="tpu_custom_call" | custom-call | flops 1 | bytes 1 | tf_op jit(solution)/shard_map/pallas_call | solution.py:97
  86.6 6.4 %shard_map.216.refs_0_ = bf16[1024,768]{1,0:T(8,128)(2,1)S(1)} custom-call(s32[7]{0:T(128)S(1)} %stack.40._.p, bf16[3,1024,384]{2,1,0:T(8,128)(2,1)S(1)} %get-tuple-element.463.q_ref.k_ref.v_ref, bf16[3,1024,384]{2,1,0:T(8,128)(2,1)S(1)} %get-tuple-element.463.q_ref.k_ref.v_ref, bf16[3,1024,384]{2,1,0:T(8,128)(2,1)S(1)} %get-tuple-element.463.q_ref.k_ref.v_ref), custom_call_target="tpu_custom_call" | custom-call | flops 1 | bytes 1 | tf_op jit(solution)/shard_map/pallas_call | solution.py:97
  100.8 8.1 %shard_map.217.q_ref.k_ref.v_ref = bf16[3,1024,384]{2,1,0:T(8,128)(2,1)S(1)} custom-call(s32[7]{0:T(128)S(1)} %stack.40._.p, bf16[256,1536]{1,0:T(8,128)(2,1)} %get-tuple-element.500.ol.refs_0_, bf16[256,1536]{1,0:T(8,128)(2,1)S(1)} %get-tuple-element.501.oh.refs_1_, bf16[256,1536]{1,0:T(8,128)(2,1)} %collective-permute-done.tl.refs_2_, ...), custom_call_target="tpu_custom_call" | custom-call | flops 1 | bytes 1 | tf_op jit(solution)/shard_map/pallas_call | solution.py:97
  108.9 6.4 %shard_map.218.heads = bf16[1024,768]{1,0:T(8,128)(2,1)S(1)} custom-call(s32[7]{0:T(128)S(1)} %stack.40._.p, bf16[3,1024,384]{2,1,0:T(8,128)(2,1)S(1)} %shard_map.217.q_ref.k_ref.v_ref, bf16[3,1024,384]{2,1,0:T(8,128)(2,1)S(1)} %shard_map.217.q_ref.k_ref.v_ref, ...), custom_call_target="tpu_custom_call", output_to_operand_aliasing={{}: (4, {})} | custom-call | flops 1 | bytes 1 | tf_op jit(solution)/shard_map/pallas_call | solution.py:97
  116.5 12.5 %collective-permute-done.4.refs_1_.g_other = bf16[256,1536]{1,0:T(8,128)(2,1)} collective-permute-done((bf16[256,1536]{1,0:T(8,128)(2,1)}, bf16[256,1536]{1,0:T(8,128)(2,1)}, u32[]{:S(2)}, u32[]{:S(2)}) %collective-permute-start.4) | collective-permute-done | bytes 786464 | tf_op jit(solution)/shard_map/ppermute | solution.py:42
  140.4 15.8 %collective-permute-done.8.arrived = bf16[256,1536]{1,0:T(8,128)(2,1)S(1)} collective-permute-done((bf16[256,1536]{1,0:T(8,128)(2,1)S(1)}, bf16[256,1536]{1,0:T(8,128)(2,1)S(1)}, u32[]{:S(2)}, u32[]{:S(2)}) %collective-permute-start.8) | collective-permute-done | bytes 786464 | tf_op jit(solution)/shard_map/ppermute | solution.py:42
  159.4 13.6 %collective-permute-done.7.refs_0_.g_other = bf16[256,1536]{1,0:T(8,128)(2,1)S(1)} collective-permute-done((bf16[256,1536]{1,0:T(8,128)(2,1)}, bf16[256,1536]{1,0:T(8,128)(2,1)S(1)}, u32[]{:S(2)}, u32[]{:S(2)}) %collective-permute-start.7) | collective-permute-done | bytes 786464 | tf_op jit(solution)/shard_map/ppermute | solution.py:42
  180.0 9.9 %collective-permute-done.6.arrived = bf16[256,1536]{1,0:T(8,128)(2,1)S(1)} collective-permute-done((bf16[256,1536]{1,0:T(8,128)(2,1)S(1)}, bf16[256,1536]{1,0:T(8,128)(2,1)S(1)}, u32[]{:S(2)}, u32[]{:S(2)}) %collective-permute-start.6) | collective-permute-done | bytes 786464 | tf_op jit(solution)/shard_map/ppermute | solution.py:42
  198.0 4.8 shard_map.224.gft
  207.8 23.2 %shard_map.226 = (bf16[1024,1536]{1,0:T(8,128)(2,1)}, bf16[1024,1536]{1,0:T(8,128)(2,1)}, bf16[1024,1536]{1,0:T(8,128)(2,1)}, bf16[1024,1536]{1,0:T(8,128)(2,1)}...) custom-call(s32[7]{0:T(128)S(1)} %stack.40._.p, ...), custom_call_target="tpu_custom_call" | custom-call | flops 1 | bytes 1 | tf_op jit(solution)/shard_map/pallas_call | solution.py:97
  233.1 22.9 %shard_map.227 = (bf16[1024,1536]{1,0:T(8,128)(2,1)}, bf16[1024,1536]{1,0:T(8,128)(2,1)}, bf16[1024,1536]{1,0:T(8,128)(2,1)}, bf16[1024,1536]{1,0:T(8,128)(2,1)}...) custom-call(s32[7]{0:T(128)S(1)} %stack.40._.p, ...), custom_call_target="tpu_custom_call", output_to_operand_aliasing={{0}: (11, {}), {1}: (12, {}), {2}: (13, {}), {3}: (14, {}),... | custom-call | flops 1 | bytes 1 | tf_op jit(solution)/shard_map/pallas_call | solution.py:97
  263.1 8.3 %shard_map.229 = bf16[2,1,768,1536]{3,2,1,0:T(8,128)(2,1)S(1)} custom-call(s32[7]{0:T(128)S(1)} %stack.40._.p, bf16[1024,1536]{1,0:T(8,128)(2,1)S(1)} %copy-done.3, bf16[1024,1536]{1,0:T(8,128)(2,1)S(1)} %copy-done.3, bf16[1024,1536]{1,0:T(8,128)(2,1)S(1)} %copy-done.17, bf16[1024,1536]{1,0:T(8,128)(2,1)S(1)} %copy-done.22), custom_call_target="tpu_custom_call" | custom-call | flops 1 | bytes 1 | tf_op jit(solution)/shard_map/pallas_call | solution.py:97
  271.5 9.2 %shard_map.230 = bf16[2,1,768,1536]{3,2,1,0:T(8,128)(2,1)} custom-call(s32[7]{0:T(128)S(1)} %stack.40._.p, bf16[1024,1536]{1,0:T(8,128)(2,1)S(1)} %copy-done.16, bf16[1024,1536]{1,0:T(8,128)(2,1)S(1)} %copy-done.19, bf16[1024,1536]{1,0:T(8,128)(2,1)S(1)} %copy-done.4, bf16[1024,1536]{1,0:T(8,128)(2,1)S(1)} %copy-done.4), custom_call_target="tpu_custom_call" | custom-call | flops 1 | bytes 1 | tf_op jit(solution)/shard_map/pallas_call | solution.py:97
  289.6 8.7 %shard_map.231 = (bf16[2,1,384,1536]{3,2,1,0:T(8,128)(2,1)S(1)}, bf16[2,1,384,1536]{3,2,1,0:T(8,128)(2,1)S(1)}) custom-call(s32[7]{0:T(128)S(1)} %stack.40._.p, bf16[1024,1536]{1,0:T(8,128)(2,1)S(1)} %copy-done.3, bf16[1024,1536]{1,0:T(8,128)(2,1)S(1)} %copy-done.3, bf16[1024,1536]{1,0:T(8,128)(2,1)S(1)} %copy-done.18, bf16[1024,1536]{1,0:T(8,128)(2,1)S(1)} %copy-done.23, ...), custom_call_target="tpu_custom_call" | custom-call | flops 1 | bytes 1 | tf_op jit(solution)/shard_map/pallas_call | solution.py:97
  304.1 9.7 %shard_map.233 = (bf16[2,1,384,1536]{3,2,1,0:T(8,128)(2,1)S(1)}, bf16[2,1,384,1536]{3,2,1,0:T(8,128)(2,1)S(1)}) custom-call(s32[7]{0:T(128)S(1)} %stack.40._.p, bf16[1024,1536]{1,0:T(8,128)(2,1)S(1)} %copy-done.16, bf16[1024,1536]{1,0:T(8,128)(2,1)S(1)} %copy-done.20, bf16[1024,1536]{1,0:T(8,128)(2,1)S(1)} %copy-done.4, bf16[1024,1536]{1,0:T(8,128)(2,1)S(1)} %copy-done.4, ...), custom_call_target="tpu_custom_call" | custom-call | flops 1 | bytes 1 | tf_op jit(solution)/shard_map/pallas_call | solution.py:97
  317.6 18.5 %collective-permute-done.14.th.refs_3_ = bf16[256,1536]{1,0:T(8,128)(2,1)S(1)} collective-permute-done((bf16[256,1536]{1,0:T(8,128)(2,1)S(1)}, bf16[256,1536]{1,0:T(8,128)(2,1)S(1)}, u32[]{:S(2)}, u32[]{:S(2)}) %collective-permute-start.14) | collective-permute-done | bytes 786464 | tf_op jit(solution)/shard_map/ppermute | solution.py:42
  336.1 14.7 %collective-permute-done.15.tl.refs_2_ = bf16[256,1536]{1,0:T(8,128)(2,1)S(1)} collective-permute-done((bf16[256,1536]{1,0:T(8,128)(2,1)S(1)}, bf16[256,1536]{1,0:T(8,128)(2,1)S(1)}, u32[]{:S(2)}, u32[]{:S(2)}) %collective-permute-start.15) | collective-permute-done | bytes 786464 | tf_op jit(solution)/shard_map/ppermute | solution.py:42
  350.8 14.2 %shard_map.234.refs_0_ = bf16[3,1024,768]{2,1,0:T(8,128)(2,1)S(1)} custom-call(s32[7]{0:T(128)S(1)} %stack.40._.p, bf16[3,1024,384]{2,1,0:T(8,128)(2,1)S(1)} %shard_map.217.q_ref.k_ref.v_ref, bf16[3,1024,384]{2,1,0:T(8,128)(2,1)S(1)} %shard_map.217.q_ref.k_ref.v_ref, bf16[3,1024,384]{2,1,0:T(8,128)(2,1)S(1)} %shard_map.217.q_ref.k_ref.v_ref, ...), custom_call_target="tpu_custom_call" | custom-call | flops 1 | bytes 1 | tf_op jit(solution)/shard_map/pallas_call | solution.py:97
  371.4 13.8 %shard_map.236.refs_4_.proj = bf16[3,1024,768]{2,1,0:T(8,128)(2,1)S(1)} custom-call(s32[7]{0:T(128)S(1)} %stack.40._.p, bf16[3,1024,384]{2,1,0:T(8,128)(2,1)S(1)} %copy-done.2, bf16[3,1024,384]{2,1,0:T(8,128)(2,1)S(1)} %copy-done.2, bf16[3,1024,384]{2,1,0:T(8,128)(2,1)S(1)} %copy-done.2, ...), custom_call_target="tpu_custom_call", output_to_operand_aliasing={{}: (11, {})} | custom-call | flops 1 | bytes 1 | tf_op jit(solution)/shard_map/pallas_call | solution.py:97
  385.2 8.0 %shard_map.237 = (bf16[2,2,768,384]{3,2,1,0:T(8,128)(2,1)}, bf16[2,2,768,384]{3,2,1,0:T(8,128)(2,1)}) custom-call(s32[7]{0:T(128)S(1)} %stack.40._.p, bf16[256,1536]{1,0:T(8,128)(2,1)} %get-tuple-element.500.ol.refs_0_, bf16[256,1536]{1,0:T(8,128)(2,1)S(1)} %get-tuple-element.501.oh.refs_1_, bf16[256,1536]{1,0:T(8,128)(2,1)} %collective-permute-done.tl.refs_2_, ...), custom_call_target="tpu_custom_call" | custom-call | flops 1 | bytes 1 | tf_op jit(solution)/shard_map/pallas_call | solution.py:97
  399.4 5.9 %shard_map.240.stay = f32[512,1536]{1,0:T(8,128)S(1)} custom-call(s32[7]{0:T(128)S(1)} %stack.40._.p, bf16[3,1024,768]{2,1,0:T(8,128)(2,1)S(1)} %shard_map.236.refs_4_.proj, bf16[3,1536,384]{2,1,0:T(8,128)(2,1)S(1)} %copy-done.58, bf16[3,1536,384]{2,1,0:T(8,128)(2,1)S(1)} %bitcast.37), custom_call_target="tpu_custom_call" | custom-call | flops 199999995904 | bytes 1 | tf_op jit(solution)/shard_map/pallas_call | solution.py:97
  407.0 8.4 %shard_map.241 = (bf16[2,2,384,384]{3,2,1,0:T(8,128)(2,1)S(1)}, bf16[2,2,384,384]{3,2,1,0:T(8,128)(2,1)}, bf16[2,2,384,384]{3,2,1,0:T(8,128)(2,1)S(1)}, bf16[2,2,384,384]{3,2,1,0:T(8,128)(2,1)}) custom-call(s32[7]{0:T(128)S(1)} %stack.40._.p, bf16[256,1536]{1,0:T(8,128)(2,1)} %get-tuple-element.500.ol.refs_0_, ...), custom_call_target="tpu_custom_call" | custom-call | flops 1 | bytes 1 | tf_op jit(solution)/shard_map/pallas_call | solution.py:97
  420.0 6.5 %shard_map.243 = bf16[512,1536]{1,0:T(8,128)(2,1)} custom-call(s32[7]{0:T(128)S(1)} %stack.40._.p, bf16[3,1024,768]{2,1,0:T(8,128)(2,1)S(1)} %shard_map.236.refs_4_.proj, bf16[3,1536,384]{2,1,0:T(8,128)(2,1)S(1)} %copy-done.58, bf16[3,1536,384]{2,1,0:T(8,128)(2,1)S(1)} %bitcast.38), custom_call_target="tpu_custom_call" | custom-call | flops 199999995904 | bytes 1 | tf_op jit(solution)/shard_map/pallas_call | solution.py:97
  428.9 12.8 %shard_map.244 = (bf16[256,1536]{1,0:T(8,128)(2,1)S(1)}, bf16[256,1536]{1,0:T(8,128)(2,1)S(1)}, f32[256,1536]{1,0:T(8,128)S(1)}, f32[256,1536]{1,0:T(8,128)S(1)}) custom-call(s32[7]{0:T(128)S(1)} %stack.40._.p, bf16[1024,1536]{1,0:T(8,128)(2,1)S(1)} %copy-done.16, bf16[1024,1536]{1,0:T(8,128)(2,1)S(1)} %copy-done.21, bf16[1536,1536]{1,0:T(8,128)(2,1)S(1)} %copy-done.52, ...), custom_call_target="tpu_custom_call" | custom-call | flops 199999995904 | bytes 1 | tf_op jit(solution)/shard_map/pallas_call | solution.py:97
  441.8 13.3 %collective-permute-done.27.refs_3_ = bf16[2,2,384,384]{3,2,1,0:T(8,128)(2,1)} collective-permute-done((bf16[2,2,384,384]{3,2,1,0:T(8,128)(2,1)}, bf16[2,2,384,384]{3,2,1,0:T(8,128)(2,1)}, u32[]{:S(2)}, u32[]{:S(2)}) %collective-permute-start.27) | collective-permute-done | bytes 1179680 | tf_op jit(solution)/shard_map/ppermute | solution.py:42
  467.7 7.7 %collective-permute-done.28.refs_1_ = bf16[2,2,192,384]{3,2,1,0:T(8,128)(2,1)} collective-permute-done((bf16[2,2,192,384]{3,2,1,0:T(8,128)(2,1)}, bf16[2,2,192,384]{3,2,1,0:T(8,128)(2,1)}, u32[]{:S(2)}, u32[]{:S(2)}) %collective-permute-start.28) | collective-permute-done | bytes 589856 | tf_op jit(solution)/shard_map/ppermute | solution.py:42
  491.7 5.8 shard_map.248
  501.8 6.3 %collective-permute-done.33.theirs = bf16[4,192,384]{2,1,0:T(8,128)(2,1)} collective-permute-done((bf16[4,192,384]{2,1,0:T(8,128)(2,1)}, bf16[4,192,384]{2,1,0:T(8,128)(2,1)}, u32[]{:S(2)}, u32[]{:S(2)}) %collective-permute-start.33) | collective-permute-done | bytes 589856 | tf_op jit(solution)/shard_map/ppermute | solution.py:42
  518.6 28.3 %collective-permute-done.35 = f32[4,1536]{1,0:T(4,128)S(1)} collective-permute-done((f32[4,1536]{1,0:T(4,128)S(1)}, f32[4,1536]{1,0:T(4,128)S(1)}, u32[]{:S(2)}, u32[]{:S(2)}) %collective-permute-start.35) | collective-permute-done | bytes 24608 | tf_op jit(solution)/shard_map/ppermute | solution.py:42
  558.1 7.2 %shard_map.251 = (f32[1536,1536]{1,0:T(8,128)}, f32[1536,1536]{1,0:T(8,128)}) custom-call(s32[16]{0:T(128)S(1)} %copy-done.80, bf16[8,2,192,1536]{3,2,1,0:T(8,128)(2,1)S(1)} %bitcast.31, bf16[8,2,192,1536]{3,2,1,0:T(8,128)(2,1)S(1)} %bitcast.32), custom_call_target="tpu_custom_call" | custom-call | flops 1 | bytes 1 | tf_op jit(solution)/shard_map/pallas_call | solution.py:97
  (311 shorter events, 192.0 us)
Async XLA Ops:
  7.2 88.4 %all-gather.9.cloned.1.call-start = ((), (), s32[]{:S(2)}) async-start(), calls=%async_computation | async-start | bytes 3981312 | tf_op jit(solution)/shard_map/all_gather | solution.py:68
  9.2 24.1 %collective-permute-start.1 = (bf16[576,384]{1,0:T(8,128)(2,1)}, bf16[576,384]{1,0:T(8,128)(2,1)}, u32[]{:S(2)}, u32[]{:S(2)}) collective-permute-start(bf16[576,384]{1,0:T(8,128)(2,1)} %constant_dynamic-slice_fusion.1), channel_id=1, source_target_pairs={{0,2},{1,3},{2,0},{3,1},{4,6},{5,7},{6,4},{7,5},{8,10},{9,11},{10,... | collective-permute-start | bytes 1327112 | tf_op jit(solution)/shard_map/ppermute | solution.py:42
  21.4 27.6 %collective-permute-start = (bf16[256,1536]{1,0:T(8,128)(2,1)}, bf16[256,1536]{1,0:T(8,128)(2,1)}, u32[]{:S(2)}, u32[]{:S(2)}) collective-permute-start(bf16[256,1536]{1,0:T(8,128)(2,1)} %get-tuple-element.500.ol.refs_0_), channel_id=1, source_target_pairs={{0,1},{1,0},{2,3},{3,2},{4,5},{5,4},{6,7},{7,6},{8,9},{9,8},{10,11... | collective-permute-start | bytes 2359304 | tf_op jit(solution)/shard_map/ppermute | solution.py:42
  49.0 80.0 %all-gather.11.cloned.1.call-start = ((), (), s32[]{:S(2)}) async-start(), calls=%async_computation.1 | async-start | bytes 1327104 | tf_op jit(solution)/shard_map/all_gather | solution.py:68
  49.1 22.0 %collective-permute-start.2 = (bf16[256,1536]{1,0:T(8,128)(2,1)S(1)}, bf16[256,1536]{1,0:T(8,128)(2,1)S(1)}, u32[]{:S(2)}, u32[]{:S(2)}) collective-permute-start(bf16[256,1536]{1,0:T(8,128)(2,1)S(1)} %get-tuple-element.501.oh.refs_1_), channel_id=1, source_target_pairs={{0,1},{1,0},{2,3},{3,2},{4,5},{5,4},{6,7},{7,6},{8,9},{9,8},{10,11... | collective-permute-start | bytes 2359304 | tf_op jit(solution)/shard_map/ppermute | solution.py:42
  50.1 21.0 %collective-permute-start.3 = (bf16[48,1536]{1,0:T(8,128)(2,1)S(1)}, bf16[48,1536]{1,0:T(8,128)(2,1)S(1)}, u32[]{:S(2)}, u32[]{:S(2)}) collective-permute-start(bf16[48,1536]{1,0:T(8,128)(2,1)S(1)} %constant_dynamic-slice_fusion), channel_id=1, source_target_pairs={{0,2},{1,3},{2,0},{3,1},{4,6},{5,7},{6,4},{7,5},{8,10},{9,11},{10,... | collective-permute-start | bytes 442376 | tf_op jit(solution)/shard_map/ppermute | solution.py:42
  71.8 121.4 %all-gather.13.cloned.1.call-start = ((), (), s32[]{:S(2)}) async-start(), calls=%async_computation.2 | async-start | bytes 10616832 | tf_op jit(solution)/shard_map/all_gather | solution.py:72
  74.5 54.4 %collective-permute-start.5 = (bf16[2,192,1536]{2,1,0:T(8,128)(2,1)}, bf16[2,192,1536]{2,1,0:T(8,128)(2,1)}, u32[]{:S(2)}, u32[]{:S(2)}) collective-permute-start(bf16[2,192,1536]{2,1,0:T(8,128)(2,1)} %pad_maximum_fusion), channel_id=1, source_target_pairs={{0,2},{1,3},{2,0},{3,1},{4,6},{5,7},{6,4},{7,5},{8,10},{9,11},{10,... | collective-permute-start | bytes 3538952 | tf_op jit(solution)/shard_map/ppermute | solution.py:42
  85.4 43.5 %collective-permute-start.4 = (bf16[256,1536]{1,0:T(8,128)(2,1)}, bf16[256,1536]{1,0:T(8,128)(2,1)}, u32[]{:S(2)}, u32[]{:S(2)}) collective-permute-start(bf16[256,1536]{1,0:T(8,128)(2,1)} %get-tuple-element.332), channel_id=1, source_target_pairs={{0,1},{1,0},{2,3},{3,2},{4,5},{5,4},{6,7},{7,6},{8,9},{9,8},{10,11... | collective-permute-start | bytes 2359304 | tf_op jit(solution)/shard_map/ppermute | solution.py:42
  129.0 425.4 %all-gather.17.cloned.1.call-start = ((), (), s32[]{:S(2)}) async-start(), calls=%async_computation.4 | async-start | bytes 10616832 | tf_op jit(solution)/shard_map/all_gather | solution.py:1016
  135.7 20.5 %collective-permute-start.8 = (bf16[256,1536]{1,0:T(8,128)(2,1)S(1)}, bf16[256,1536]{1,0:T(8,128)(2,1)S(1)}, u32[]{:S(2)}, u32[]{:S(2)}) collective-permute-start(bf16[256,1536]{1,0:T(8,128)(2,1)S(1)} %get-tuple-element.346), channel_id=1, source_target_pairs={{0,1},{1,0},{2,3},{3,2},{4,5},{5,4},{6,7},{7,6},{8,9},{9,8},{10,11... | collective-permute-start | bytes 2359304 | tf_op jit(solution)/shard_map/ppermute | solution.py:42
  135.7 37.3 %collective-permute-start.7 = (bf16[256,1536]{1,0:T(8,128)(2,1)}, bf16[256,1536]{1,0:T(8,128)(2,1)S(1)}, u32[]{:S(2)}, u32[]{:S(2)}) collective-permute-start(bf16[256,1536]{1,0:T(8,128)(2,1)} %copy-done.89), channel_id=1, source_target_pairs={{0,1},{1,0},{2,3},{3,2},{4,5},{5,4},{6,7},{7,6},{8,9},{9,8},{10,11... | collective-permute-start | bytes 2359304 | tf_op jit(solution)/shard_map/ppermute | solution.py:42
  137.7 52.2 %collective-permute-start.6 = (bf16[256,1536]{1,0:T(8,128)(2,1)S(1)}, bf16[256,1536]{1,0:T(8,128)(2,1)S(1)}, u32[]{:S(2)}, u32[]{:S(2)}) collective-permute-start(bf16[256,1536]{1,0:T(8,128)(2,1)S(1)} %get-tuple-element.339), channel_id=1, source_target_pairs={{0,1},{1,0},{2,3},{3,2},{4,5},{5,4},{6,7},{7,6},{8,9},{9,8},{10,11... | collective-permute-start | bytes 2359304 | tf_op jit(solution)/shard_map/ppermute | solution.py:42
  159.4 48.4 %collective-permute-start.10 = (bf16[256,1536]{1,0:T(8,128)(2,1)}, bf16[256,1536]{1,0:T(8,128)(2,1)}, u32[]{:S(2)}, u32[]{:S(2)}) collective-permute-start(bf16[256,1536]{1,0:T(8,128)(2,1)} %get-tuple-element.368.own), channel_id=1, source_target_pairs={{0,1},{1,0},{2,3},{3,2},{4,5},{5,4},{6,7},{7,6},{8,9},{9,8},{10,11... | collective-permute-start | bytes 2359304 | tf_op jit(solution)/shard_map/ppermute | solution.py:42
  193.2 39.9 %collective-permute-start.9 = (bf16[256,1536]{1,0:T(8,128)(2,1)}, bf16[256,1536]{1,0:T(8,128)(2,1)}, u32[]{:S(2)}, u32[]{:S(2)}) collective-permute-start(bf16[256,1536]{1,0:T(8,128)(2,1)} %get-tuple-element.384.own), channel_id=1, source_target_pairs={{0,1},{1,0},{2,3},{3,2},{4,5},{5,4},{6,7},{7,6},{8,9},{9,8},{10,11... | collective-permute-start | bytes 2359304 | tf_op jit(solution)/shard_map/ppermute | solution.py:42
  231.0 25.0 %collective-permute-start.12 = (bf16[256,1536]{1,0:T(8,128)(2,1)S(1)}, bf16[256,1536]{1,0:T(8,128)(2,1)S(1)}, u32[]{:S(2)}, u32[]{:S(2)}) collective-permute-start(bf16[256,1536]{1,0:T(8,128)(2,1)S(1)} %get-tuple-element.410), channel_id=1, source_target_pairs={{0,1},{1,0},{2,3},{3,2},{4,5},{5,4},{6,7},{7,6},{8,9},{9,8},{10,11... | collective-permute-start | bytes 2359304 | tf_op jit(solution)/shard_map/ppermute | solution.py:42
  280.7 23.3 %collective-permute-start.16 = (bf16[2,1,768,1536]{3,2,1,0:T(8,128)(2,1)}, bf16[2,1,768,1536]{3,2,1,0:T(8,128)(2,1)}, u32[]{:S(2)}, u32[]{:S(2)}) collective-permute-start(bf16[2,1,768,1536]{3,2,1,0:T(8,128)(2,1)} %shard_map.230), channel_id=1, source_target_pairs={{0,4},{1,5},{2,6},{3,7},{4,0},{5,1},{6,2},{7,3},{8,12},{9,13},{10,... | collective-permute-start | bytes 14155784 | tf_op jit(solution)/shard_map/ppermute | solution.py:42
  313.8 52.4 %collective-permute-start.18 = (bf16[2,1,384,1536]{3,2,1,0:T(8,128)(2,1)S(1)}, bf16[2,1,384,1536]{3,2,1,0:T(8,128)(2,1)S(1)}, u32[]{:S(2)}, u32[]{:S(2)}) collective-permute-start(bf16[2,1,384,1536]{3,2,1,0:T(8,128)(2,1)S(1)} %get-tuple-element.455), channel_id=1, source_target_pairs={{0,16},{1,17},{2,18},{3,19},{4,20},{5,21},{6,22},{7,23},{8,24},{9,... | collective-permute-start | bytes 7077896 | tf_op jit(solution)/shard_map/ppermute | solution.py:42
  313.9 52.4 %collective-permute-start.17 = (bf16[2,1,384,1536]{3,2,1,0:T(8,128)(2,1)S(1)}, bf16[2,1,384,1536]{3,2,1,0:T(8,128)(2,1)S(1)}, u32[]{:S(2)}, u32[]{:S(2)}) collective-permute-start(bf16[2,1,384,1536]{3,2,1,0:T(8,128)(2,1)S(1)} %copy-done.82), channel_id=1, source_target_pairs={{0,8},{1,9},{2,10},{3,11},{4,12},{5,13},{6,14},{7,15},{8,0},{9,1},... | collective-permute-start | bytes 7077896 | tf_op jit(solution)/shard_map/ppermute | solution.py:42
  315.6 20.5 %collective-permute-start.14 = (bf16[256,1536]{1,0:T(8,128)(2,1)S(1)}, bf16[256,1536]{1,0:T(8,128)(2,1)S(1)}, u32[]{:S(2)}, u32[]{:S(2)}) collective-permute-start(bf16[256,1536]{1,0:T(8,128)(2,1)S(1)} %get-tuple-element.511.oh.refs_1_), channel_id=1, source_target_pairs={{0,1},{1,0},{2,3},{3,2},{4,5},{5,4},{6,7},{7,6},{8,9},{9,8},{10,11... | collective-permute-start | bytes 2359304 | tf_op jit(solution)/shard_map/ppermute | solution.py:42
  315.9 34.9 %collective-permute-start.15 = (bf16[256,1536]{1,0:T(8,128)(2,1)S(1)}, bf16[256,1536]{1,0:T(8,128)(2,1)S(1)}, u32[]{:S(2)}, u32[]{:S(2)}) collective-permute-start(bf16[256,1536]{1,0:T(8,128)(2,1)S(1)} %get-tuple-element.510.ol.refs_0_), channel_id=1, source_target_pairs={{0,1},{1,0},{2,3},{3,2},{4,5},{5,4},{6,7},{7,6},{8,9},{9,8},{10,11... | collective-permute-start | bytes 2359304 | tf_op jit(solution)/shard_map/ppermute | solution.py:42
  368.0 29.2 %collective-permute-start.21 = (bf16[2,1,192,1536]{3,2,1,0:T(8,128)(2,1)S(1)}, bf16[2,1,192,1536]{3,2,1,0:T(8,128)(2,1)S(1)}, u32[]{:S(2)}, u32[]{:S(2)}) collective-permute-start(bf16[2,1,192,1536]{3,2,1,0:T(8,128)(2,1)S(1)} %get-tuple-element.485), channel_id=1, source_target_pairs={{0,16},{1,17},{2,18},{3,19},{4,20},{5,21},{6,22},{7,23},{8,24},{9,... | collective-permute-start | bytes 3538952 | tf_op jit(solution)/shard_map/ppermute | solution.py:42
  369.7 27.5 %collective-permute-start.22 = (bf16[2,1,192,1536]{3,2,1,0:T(8,128)(2,1)S(1)}, bf16[2,1,192,1536]{3,2,1,0:T(8,128)(2,1)S(1)}, u32[]{:S(2)}, u32[]{:S(2)}) collective-permute-start(bf16[2,1,192,1536]{3,2,1,0:T(8,128)(2,1)S(1)} %get-tuple-element.486), channel_id=1, source_target_pairs={{0,8},{1,9},{2,10},{3,11},{4,12},{5,13},{6,14},{7,15},{8,0},{9,1},... | collective-permute-start | bytes 3538952 | tf_op jit(solution)/shard_map/ppermute | solution.py:42
  399.3 65.0 %collective-permute-start.30 = (bf16[2,192,1536]{2,1,0:T(8,128)(2,1)}, bf16[2,192,1536]{2,1,0:T(8,128)(2,1)}, u32[]{:S(2)}, u32[]{:S(2)}) collective-permute-start(bf16[2,192,1536]{2,1,0:T(8,128)(2,1)} %get-tuple-element.544), channel_id=1, source_target_pairs={{0,2},{1,3},{2,0},{3,1},{4,6},{5,7},{6,4},{7,5},{8,10},{9,11},{10,... | collective-permute-start | bytes 3538952 | tf_op jit(solution)/shard_map/ppermute | solution.py:42
  426.6 61.8 %collective-permute-start.25 = (bf16[512,1536]{1,0:T(8,128)(2,1)}, bf16[512,1536]{1,0:T(8,128)(2,1)}, u32[]{:S(2)}, u32[]{:S(2)}) collective-permute-start(bf16[512,1536]{1,0:T(8,128)(2,1)} %shard_map.243), channel_id=1, source_target_pairs={{0,1},{1,0},{2,3},{3,2},{4,5},{5,4},{6,7},{7,6},{8,9},{9,8},{10,11... | collective-permute-start | bytes 4718600 | tf_op jit(solution)/shard_map/ppermute | solution.py:42
  427.1 27.9 %collective-permute-start.27 = (bf16[2,2,384,384]{3,2,1,0:T(8,128)(2,1)}, bf16[2,2,384,384]{3,2,1,0:T(8,128)(2,1)}, u32[]{:S(2)}, u32[]{:S(2)}) collective-permute-start(bf16[2,2,384,384]{3,2,1,0:T(8,128)(2,1)} %get-tuple-element.535), channel_id=1, source_target_pairs={{0,16},{1,17},{2,18},{3,19},{4,20},{5,21},{6,22},{7,23},{8,24},{9,... | collective-permute-start | bytes 3538952 | tf_op jit(solution)/shard_map/ppermute | solution.py:42
  427.5 27.7 %collective-permute-start.26 = (bf16[2,2,384,384]{3,2,1,0:T(8,128)(2,1)}, bf16[2,2,384,384]{3,2,1,0:T(8,128)(2,1)}, u32[]{:S(2)}, u32[]{:S(2)}) collective-permute-start(bf16[2,2,384,384]{3,2,1,0:T(8,128)(2,1)} %get-tuple-element.534), channel_id=1, source_target_pairs={{0,8},{1,9},{2,10},{3,11},{4,12},{5,13},{6,14},{7,15},{8,0},{9,1},... | collective-permute-start | bytes 3538952 | tf_op jit(solution)/shard_map/ppermute | solution.py:42
  467.5 100.7 %all-gather.15.cloned.1.call-start = ((), (), s32[]{:S(2)}) async-start(), calls=%async_computation.3 | async-start | bytes 5308416 | tf_op jit(solution)/shard_map/all_gather | solution.py:1016
  481.4 26.7 %collective-permute-start.33 = (bf16[4,192,384]{2,1,0:T(8,128)(2,1)}, bf16[4,192,384]{2,1,0:T(8,128)(2,1)}, u32[]{:S(2)}, u32[]{:S(2)}) collective-permute-start(bf16[4,192,384]{2,1,0:T(8,128)(2,1)} %get-tuple-element.571), channel_id=1, source_target_pairs={{0,2},{1,3},{2,0},{3,1},{4,6},{5,7},{6,4},{7,5},{8,10},{9,11},{10,... | collective-permute-start | bytes 1769480 | tf_op jit(solution)/shard_map/ppermute | solution.py:42
  510.7 41.0 %collective-permute-start.23 = (bf16[256,1536]{1,0:T(8,128)(2,1)}, bf16[256,1536]{1,0:T(8,128)(2,1)S(1)}, u32[]{:S(2)}, u32[]{:S(2)}) collective-permute-start(bf16[256,1536]{1,0:T(8,128)(2,1)} %copy-done.88), channel_id=1, source_target_pairs={{0,1},{1,0},{2,3},{3,2},{4,5},{5,4},{6,7},{7,6},{8,9},{9,8},{10,11... | collective-permute-start | bytes 2359304 | tf_op jit(solution)/shard_map/ppermute | solution.py:42
  510.9 40.8 %collective-permute-start.24 = (bf16[256,1536]{1,0:T(8,128)(2,1)}, bf16[256,1536]{1,0:T(8,128)(2,1)S(1)}, u32[]{:S(2)}, u32[]{:S(2)}) collective-permute-start(bf16[256,1536]{1,0:T(8,128)(2,1)} %copy-done.87), channel_id=1, source_target_pairs={{0,1},{1,0},{2,3},{3,2},{4,5},{5,4},{6,7},{7,6},{8,9},{9,8},{10,11... | collective-permute-start | bytes 2359304 | tf_op jit(solution)/shard_map/ppermute | solution.py:42
  518.4 28.5 %collective-permute-start.35 = (f32[4,1536]{1,0:T(4,128)S(1)}, f32[4,1536]{1,0:T(4,128)S(1)}, u32[]{:S(2)}, u32[]{:S(2)}) collective-permute-start(f32[4,1536]{1,0:T(4,128)S(1)} %add.44), channel_id=1, source_target_pairs={{0,1},{1,0},{2,3},{3,2},{4,5},{5,4},{6,7},{7,6},{8,9},{9,8},{10,11... | collective-permute-start | bytes 73736 | tf_op jit(solution)/shard_map/ppermute | solution.py:42
  (107 other events, 891.7 us)
Sparse Core Ops, SparseCore 0:
  49.1 34.0 all-gather.8
  85.7 24.0 all-gather.10
  129.1 57.2 all-gather.12
  467.6 59.6 all-gather.16
  529.6 38.5 all-gather.14

commit v4 on v3

--- a/solution.py
+++ b/solution.py
@@ -903,10 +903,10 @@
     heads = chain(lambda *a: attend(place, 0, *a), qkv_near)
     (qkv_far,) = run(project, normed, normed_far, w_qkv_far, tables)
     (heads,) = chain(lambda *a: attend(place, 1, *a), qkv_far, heads)
+    low, high = chain(lambda *a: head_rows(place, True, *a), heads, w_out, w_out_far)
+    high, low = swap(high, 0, 1), swap(low, 0, 1)
     cot_far[1], piece_pair = chain.wait(cot_far[1], piece_pair)
     far_pair = stacked_from_all(piece_pair)
-    low, high = chain(lambda *a: head_rows(place, True, *a), heads, w_out, w_out_far)
-    high, low = swap(high, 0, 1), swap(low, 0, 1)
     stay_low, stay_high = chain(lambda *a: head_rows(place, False, *a), heads, w_out, w_out_far)
     norm_args = (gain_two, shift_two)
     normed_high, resid_high = chain(

time: 591 us -> 584 us (0.988)
  waiting for transfers between devices: 201 us -> 187 us
  local copies, waits for them, and re-layouts: 66.5 us -> 72.5 us
    ppermute x37, waiting for transfers between devices: 198 us -> 183 us  [swap(): return lax.ppermute(value, AXES, pairs)]
    unnamed x194 -> x198, local copies, waits for them, and re-layouts: 59.4 us -> 65.4 us
where the time goes in v4:
time: 584 us; the launch traced here: 575 us
  Pallas kernels  258 us (44%)
  waiting for transfers between devices  187 us (32%)
  local copies, waits for them, and re-layouts  72.5 us (12%)
  starting transfers between devices  38.3 us (7%)
  between operations  16.2 us (3%)
    pallas_call x40, Pallas kernels, call(): pl.pallas_call(body, grid_spec=pltpu.PrefetchScalarGridSpec(num_scalar_pr...  258 us
    ppermute x37, waiting for transfers between devices, swap(): return lax.ppermute(value, AXES, pairs)  183 us
    unnamed x198, local copies, waits for them, and re-layouts  65.4 us
    ppermute x37, starting transfers between devices, swap(): return lax.ppermute(value, AXES, pairs)  37.8 us
  transfers between devices with their start and end apart: 42, of which 24 were waited for; matrix products, arithmetic and copies ran while one was open for 1% of the time, Pallas kernels for 40%

profile of v4, /device:TPU:0, one launch (start us, length us, event | category | flops | bytes accessed | tf_op | source)
XLA Modules:
  0.0 574.9 jit_solution(16026007694253704986)
XLA Ops:
  33.3 15.7 %collective-permute-done.tl.refs_2_ = bf16[256,1536]{1,0:T(8,128)(2,1)} collective-permute-done((bf16[256,1536]{1,0:T(8,128)(2,1)}, bf16[256,1536]{1,0:T(8,128)(2,1)}, u32[]{:S(2)}, u32[]{:S(2)}) %collective-permute-start) | collective-permute-done | bytes 786464 | tf_op jit(solution)/shard_map/ppermute | solution.py:42
  53.1 18.0 %collective-permute-done.2.th.refs_3_ = bf16[256,1536]{1,0:T(8,128)(2,1)S(1)} collective-permute-done((bf16[256,1536]{1,0:T(8,128)(2,1)S(1)}, bf16[256,1536]{1,0:T(8,128)(2,1)S(1)}, u32[]{:S(2)}, u32[]{:S(2)}) %collective-permute-start.2) | collective-permute-done | bytes 786464 | tf_op jit(solution)/shard_map/ppermute | solution.py:42
  75.7 8.8 %shard_map.215 = (bf16[3,1024,384]{2,1,0:T(8,128)(2,1)S(1)}, bf16[256,1536]{1,0:T(8,128)(2,1)S(1)}, bf16[256,1536]{1,0:T(8,128)(2,1)}) custom-call(s32[7]{0:T(128)S(1)} %stack.40._.p, bf16[256,1536]{1,0:T(8,128)(2,1)} %get-tuple-element.500.ol.refs_0_, bf16[256,1536]{1,0:T(8,128)(2,1)S(1)} %get-tuple-element.501.oh.refs_1_, ...), custom_call_target="tpu_custom_call" | custom-call | flops 1 | bytes 1 | tf_op jit(solution)/shard_map/pallas_call | solution.py:97
  86.6 6.4 %shard_map.216.refs_0_ = bf16[1024,768]{1,0:T(8,128)(2,1)S(1)} custom-call(s32[7]{0:T(128)S(1)} %stack.40._.p, bf16[3,1024,384]{2,1,0:T(8,128)(2,1)S(1)} %get-tuple-element.463.q_ref.k_ref.v_ref, bf16[3,1024,384]{2,1,0:T(8,128)(2,1)S(1)} %get-tuple-element.463.q_ref.k_ref.v_ref, bf16[3,1024,384]{2,1,0:T(8,128)(2,1)S(1)} %get-tuple-element.463.q_ref.k_ref.v_ref), custom_call_target="tpu_custom_call" | custom-call | flops 1 | bytes 1 | tf_op jit(solution)/shard_map/pallas_call | solution.py:97
  100.8 8.1 %shard_map.217.q_ref.k_ref.v_ref = bf16[3,1024,384]{2,1,0:T(8,128)(2,1)S(1)} custom-call(s32[7]{0:T(128)S(1)} %stack.40._.p, bf16[256,1536]{1,0:T(8,128)(2,1)} %get-tuple-element.500.ol.refs_0_, bf16[256,1536]{1,0:T(8,128)(2,1)S(1)} %get-tuple-element.501.oh.refs_1_, bf16[256,1536]{1,0:T(8,128)(2,1)} %collective-permute-done.tl.refs_2_, ...), custom_call_target="tpu_custom_call" | custom-call | flops 1 | bytes 1 | tf_op jit(solution)/shard_map/pallas_call | solution.py:97
  108.9 6.4 %shard_map.218.heads = bf16[1024,768]{1,0:T(8,128)(2,1)S(1)} custom-call(s32[7]{0:T(128)S(1)} %stack.40._.p, bf16[3,1024,384]{2,1,0:T(8,128)(2,1)S(1)} %shard_map.217.q_ref.k_ref.v_ref, bf16[3,1024,384]{2,1,0:T(8,128)(2,1)S(1)} %shard_map.217.q_ref.k_ref.v_ref, ...), custom_call_target="tpu_custom_call", output_to_operand_aliasing={{}: (4, {})} | custom-call | flops 1 | bytes 1 | tf_op jit(solution)/shard_map/pallas_call | solution.py:97
  138.3 11.5 %collective-permute-done.8.arrived = bf16[256,1536]{1,0:T(8,128)(2,1)S(1)} collective-permute-done((bf16[256,1536]{1,0:T(8,128)(2,1)}, bf16[256,1536]{1,0:T(8,128)(2,1)S(1)}, u32[]{:S(2)}, u32[]{:S(2)}) %collective-permute-start.8) | collective-permute-done | bytes 786464 | tf_op jit(solution)/shard_map/ppermute | solution.py:42
  153.0 13.6 %collective-permute-done.7.refs_0_.g_other = bf16[256,1536]{1,0:T(8,128)(2,1)S(1)} collective-permute-done((bf16[256,1536]{1,0:T(8,128)(2,1)}, bf16[256,1536]{1,0:T(8,128)(2,1)S(1)}, u32[]{:S(2)}, u32[]{:S(2)}) %collective-permute-start.7) | collective-permute-done | bytes 786464 | tf_op jit(solution)/shard_map/ppermute | solution.py:42
  173.6 9.9 %collective-permute-done.6.arrived = bf16[256,1536]{1,0:T(8,128)(2,1)S(1)} collective-permute-done((bf16[256,1536]{1,0:T(8,128)(2,1)}, bf16[256,1536]{1,0:T(8,128)(2,1)S(1)}, u32[]{:S(2)}, u32[]{:S(2)}) %collective-permute-start.6) | collective-permute-done | bytes 786464 | tf_op jit(solution)/shard_map/ppermute | solution.py:42
  191.5 4.8 shard_map.224.gft
  201.3 22.8 %shard_map.226 = (bf16[1024,1536]{1,0:T(8,128)(2,1)}, bf16[1024,1536]{1,0:T(8,128)(2,1)}, bf16[1024,1536]{1,0:T(8,128)(2,1)}, bf16[1024,1536]{1,0:T(8,128)(2,1)}...) custom-call(s32[7]{0:T(128)S(1)} %stack.40._.p, ...), custom_call_target="tpu_custom_call" | custom-call | flops 1 | bytes 1 | tf_op jit(solution)/shard_map/pallas_call | solution.py:97
  226.2 22.9 %shard_map.227 = (bf16[1024,1536]{1,0:T(8,128)(2,1)}, bf16[1024,1536]{1,0:T(8,128)(2,1)}, bf16[1024,1536]{1,0:T(8,128)(2,1)}, bf16[1024,1536]{1,0:T(8,128)(2,1)}...) custom-call(s32[7]{0:T(128)S(1)} %stack.40._.p, ...), custom_call_target="tpu_custom_call", output_to_operand_aliasing={{0}: (11, {}), {1}: (12, {}), {2}: (13, {}), {3}: (14, {}),... | custom-call | flops 1 | bytes 1 | tf_op jit(solution)/shard_map/pallas_call | solution.py:97
  256.1 8.3 %shard_map.229 = bf16[2,1,768,1536]{3,2,1,0:T(8,128)(2,1)S(1)} custom-call(s32[7]{0:T(128)S(1)} %stack.40._.p, bf16[1024,1536]{1,0:T(8,128)(2,1)S(1)} %copy-done.3, bf16[1024,1536]{1,0:T(8,128)(2,1)S(1)} %copy-done.3, bf16[1024,1536]{1,0:T(8,128)(2,1)S(1)} %copy-done.17, bf16[1024,1536]{1,0:T(8,128)(2,1)S(1)} %copy-done.22), custom_call_target="tpu_custom_call" | custom-call | flops 1 | bytes 1 | tf_op jit(solution)/shard_map/pallas_call | solution.py:97
  264.5 9.2 %shard_map.230 = bf16[2,1,768,1536]{3,2,1,0:T(8,128)(2,1)} custom-call(s32[7]{0:T(128)S(1)} %stack.40._.p, bf16[1024,1536]{1,0:T(8,128)(2,1)S(1)} %copy-done.16, bf16[1024,1536]{1,0:T(8,128)(2,1)S(1)} %copy-done.19, bf16[1024,1536]{1,0:T(8,128)(2,1)S(1)} %copy-done.4, bf16[1024,1536]{1,0:T(8,128)(2,1)S(1)} %copy-done.4), custom_call_target="tpu_custom_call" | custom-call | flops 1 | bytes 1 | tf_op jit(solution)/shard_map/pallas_call | solution.py:97
  282.6 8.7 %shard_map.231 = (bf16[2,1,384,1536]{3,2,1,0:T(8,128)(2,1)S(1)}, bf16[2,1,384,1536]{3,2,1,0:T(8,128)(2,1)S(1)}) custom-call(s32[7]{0:T(128)S(1)} %stack.40._.p, bf16[1024,1536]{1,0:T(8,128)(2,1)S(1)} %copy-done.3, bf16[1024,1536]{1,0:T(8,128)(2,1)S(1)} %copy-done.3, bf16[1024,1536]{1,0:T(8,128)(2,1)S(1)} %copy-done.18, bf16[1024,1536]{1,0:T(8,128)(2,1)S(1)} %copy-done.23, ...), custom_call_target="tpu_custom_call" | custom-call | flops 1 | bytes 1 | tf_op jit(solution)/shard_map/pallas_call | solution.py:97
  297.1 9.7 %shard_map.233 = (bf16[2,1,384,1536]{3,2,1,0:T(8,128)(2,1)S(1)}, bf16[2,1,384,1536]{3,2,1,0:T(8,128)(2,1)S(1)}) custom-call(s32[7]{0:T(128)S(1)} %stack.40._.p, bf16[1024,1536]{1,0:T(8,128)(2,1)S(1)} %copy-done.16, bf16[1024,1536]{1,0:T(8,128)(2,1)S(1)} %copy-done.20, bf16[1024,1536]{1,0:T(8,128)(2,1)S(1)} %copy-done.4, bf16[1024,1536]{1,0:T(8,128)(2,1)S(1)} %copy-done.4, ...), custom_call_target="tpu_custom_call" | custom-call | flops 1 | bytes 1 | tf_op jit(solution)/shard_map/pallas_call | solution.py:97
  310.7 18.5 %collective-permute-done.14.th.refs_3_ = bf16[256,1536]{1,0:T(8,128)(2,1)S(1)} collective-permute-done((bf16[256,1536]{1,0:T(8,128)(2,1)S(1)}, bf16[256,1536]{1,0:T(8,128)(2,1)S(1)}, u32[]{:S(2)}, u32[]{:S(2)}) %collective-permute-start.14) | collective-permute-done | bytes 786464 | tf_op jit(solution)/shard_map/ppermute | solution.py:42
  329.1 14.7 %collective-permute-done.15.tl.refs_2_ = bf16[256,1536]{1,0:T(8,128)(2,1)S(1)} collective-permute-done((bf16[256,1536]{1,0:T(8,128)(2,1)S(1)}, bf16[256,1536]{1,0:T(8,128)(2,1)S(1)}, u32[]{:S(2)}, u32[]{:S(2)}) %collective-permute-start.15) | collective-permute-done | bytes 786464 | tf_op jit(solution)/shard_map/ppermute | solution.py:42
  343.9 14.2 %shard_map.234.refs_0_ = bf16[3,1024,768]{2,1,0:T(8,128)(2,1)S(1)} custom-call(s32[7]{0:T(128)S(1)} %stack.40._.p, bf16[3,1024,384]{2,1,0:T(8,128)(2,1)S(1)} %shard_map.217.q_ref.k_ref.v_ref, bf16[3,1024,384]{2,1,0:T(8,128)(2,1)S(1)} %shard_map.217.q_ref.k_ref.v_ref, bf16[3,1024,384]{2,1,0:T(8,128)(2,1)S(1)} %shard_map.217.q_ref.k_ref.v_ref, ...), custom_call_target="tpu_custom_call" | custom-call | flops 1 | bytes 1 | tf_op jit(solution)/shard_map/pallas_call | solution.py:97
  363.1 13.8 %shard_map.236.refs_4_.proj = bf16[3,1024,768]{2,1,0:T(8,128)(2,1)S(1)} custom-call(s32[7]{0:T(128)S(1)} %stack.40._.p, bf16[3,1024,384]{2,1,0:T(8,128)(2,1)S(1)} %copy-done.2, bf16[3,1024,384]{2,1,0:T(8,128)(2,1)S(1)} %copy-done.2, bf16[3,1024,384]{2,1,0:T(8,128)(2,1)S(1)} %copy-done.2, ...), custom_call_target="tpu_custom_call", output_to_operand_aliasing={{}: (11, {})} | custom-call | flops 1 | bytes 1 | tf_op jit(solution)/shard_map/pallas_call | solution.py:97
  376.9 8.0 %shard_map.237 = (bf16[2,2,768,384]{3,2,1,0:T(8,128)(2,1)}, bf16[2,2,768,384]{3,2,1,0:T(8,128)(2,1)}) custom-call(s32[7]{0:T(128)S(1)} %stack.40._.p, bf16[256,1536]{1,0:T(8,128)(2,1)} %get-tuple-element.500.ol.refs_0_, bf16[256,1536]{1,0:T(8,128)(2,1)S(1)} %get-tuple-element.501.oh.refs_1_, bf16[256,1536]{1,0:T(8,128)(2,1)} %collective-permute-done.tl.refs_2_, ...), custom_call_target="tpu_custom_call" | custom-call | flops 1 | bytes 1 | tf_op jit(solution)/shard_map/pallas_call | solution.py:97
  391.1 5.9 %shard_map.240.stay = f32[512,1536]{1,0:T(8,128)S(1)} custom-call(s32[7]{0:T(128)S(1)} %stack.40._.p, bf16[3,1024,768]{2,1,0:T(8,128)(2,1)S(1)} %shard_map.236.refs_4_.proj, bf16[3,1536,384]{2,1,0:T(8,128)(2,1)S(1)} %copy-done.58, bf16[3,1536,384]{2,1,0:T(8,128)(2,1)S(1)} %bitcast.37), custom_call_target="tpu_custom_call" | custom-call | flops 199999995904 | bytes 1 | tf_op jit(solution)/shard_map/pallas_call | solution.py:97
  398.7 8.4 %shard_map.241 = (bf16[2,2,384,384]{3,2,1,0:T(8,128)(2,1)S(1)}, bf16[2,2,384,384]{3,2,1,0:T(8,128)(2,1)}, bf16[2,2,384,384]{3,2,1,0:T(8,128)(2,1)S(1)}, bf16[2,2,384,384]{3,2,1,0:T(8,128)(2,1)}) custom-call(s32[7]{0:T(128)S(1)} %stack.40._.p, bf16[256,1536]{1,0:T(8,128)(2,1)} %get-tuple-element.500.ol.refs_0_, ...), custom_call_target="tpu_custom_call" | custom-call | flops 1 | bytes 1 | tf_op jit(solution)/shard_map/pallas_call | solution.py:97
  407.1 4.7 shard_map.242
  411.8 6.5 %shard_map.243 = bf16[512,1536]{1,0:T(8,128)(2,1)} custom-call(s32[7]{0:T(128)S(1)} %stack.40._.p, bf16[3,1024,768]{2,1,0:T(8,128)(2,1)S(1)} %shard_map.236.refs_4_.proj, bf16[3,1536,384]{2,1,0:T(8,128)(2,1)S(1)} %copy-done.58, bf16[3,1536,384]{2,1,0:T(8,128)(2,1)S(1)} %bitcast.38), custom_call_target="tpu_custom_call" | custom-call | flops 199999995904 | bytes 1 | tf_op jit(solution)/shard_map/pallas_call | solution.py:97
  422.3 12.8 %shard_map.244 = (bf16[256,1536]{1,0:T(8,128)(2,1)S(1)}, bf16[256,1536]{1,0:T(8,128)(2,1)S(1)}, f32[256,1536]{1,0:T(8,128)S(1)}, f32[256,1536]{1,0:T(8,128)S(1)}) custom-call(s32[7]{0:T(128)S(1)} %stack.40._.p, bf16[1024,1536]{1,0:T(8,128)(2,1)S(1)} %copy-done.16, bf16[1024,1536]{1,0:T(8,128)(2,1)S(1)} %copy-done.21, bf16[1536,1536]{1,0:T(8,128)(2,1)S(1)} %copy-done.52, ...), custom_call_target="tpu_custom_call" | custom-call | flops 199999995904 | bytes 1 | tf_op jit(solution)/shard_map/pallas_call | solution.py:97
  435.2 11.6 %collective-permute-done.27.refs_3_ = bf16[2,2,384,384]{3,2,1,0:T(8,128)(2,1)} collective-permute-done((bf16[2,2,384,384]{3,2,1,0:T(8,128)(2,1)}, bf16[2,2,384,384]{3,2,1,0:T(8,128)(2,1)}, u32[]{:S(2)}, u32[]{:S(2)}) %collective-permute-start.27) | collective-permute-done | bytes 1179680 | tf_op jit(solution)/shard_map/ppermute | solution.py:42
  460.8 7.4 %collective-permute-done.28.refs_1_ = bf16[2,2,192,384]{3,2,1,0:T(8,128)(2,1)} collective-permute-done((bf16[2,2,192,384]{3,2,1,0:T(8,128)(2,1)}, bf16[2,2,192,384]{3,2,1,0:T(8,128)(2,1)}, u32[]{:S(2)}, u32[]{:S(2)}) %collective-permute-start.28) | collective-permute-done | bytes 589856 | tf_op jit(solution)/shard_map/ppermute | solution.py:42
  483.4 5.8 %shard_map.248 = (f32[512,1536]{1,0:T(8,128)}, f32[1,1536]{1,0:T(1,128)S(1)}, f32[1,1536]{1,0:T(1,128)S(1)}) custom-call(s32[7]{0:T(128)S(1)} %stack.40._.p, bf16[512,1536]{1,0:T(8,128)(2,1)S(1)} %copy-done.28, f32[512,1536]{1,0:T(8,128)S(1)} %copy-done.93, bf16[512,1536]{1,0:T(8,128)(2,1)} %collective-permute-done.25.arrived, f32[256,1536]{1,0:T(8,128)S(1)} %copy-done.86, ...), custom_call_target="tpu_custom_call" | custom-call | flops 199999995904 | bytes 1 | tf_op jit(solution)/shard_map/pallas_call | solution.py:97
  493.5 6.9 %collective-permute-done.33.theirs = bf16[4,192,384]{2,1,0:T(8,128)(2,1)} collective-permute-done((bf16[4,192,384]{2,1,0:T(8,128)(2,1)}, bf16[4,192,384]{2,1,0:T(8,128)(2,1)}, u32[]{:S(2)}, u32[]{:S(2)}) %collective-permute-start.33) | collective-permute-done | bytes 589856 | tf_op jit(solution)/shard_map/ppermute | solution.py:42
  510.9 28.2 %collective-permute-done.35 = f32[4,1536]{1,0:T(4,128)S(1)} collective-permute-done((f32[4,1536]{1,0:T(4,128)S(1)}, f32[4,1536]{1,0:T(4,128)S(1)}, u32[]{:S(2)}, u32[]{:S(2)}) %collective-permute-start.35) | collective-permute-done | bytes 24608 | tf_op jit(solution)/shard_map/ppermute | solution.py:42
  550.3 7.2 %shard_map.251 = (f32[1536,1536]{1,0:T(8,128)}, f32[1536,1536]{1,0:T(8,128)}) custom-call(s32[16]{0:T(128)S(1)} %copy-done.80, bf16[8,2,192,1536]{3,2,1,0:T(8,128)(2,1)S(1)} %bitcast.31, bf16[8,2,192,1536]{3,2,1,0:T(8,128)(2,1)S(1)} %bitcast.32), custom_call_target="tpu_custom_call" | custom-call | flops 1 | bytes 1 | tf_op jit(solution)/shard_map/pallas_call | solution.py:97
  (315 shorter events, 199.2 us)
Async XLA Ops:
  7.2 88.4 %all-gather.9.cloned.1.call-start = ((), (), s32[]{:S(2)}) async-start(), calls=%async_computation | async-start | bytes 3981312 | tf_op jit(solution)/shard_map/all_gather | solution.py:68
  9.2 24.1 %collective-permute-start.1 = (bf16[576,384]{1,0:T(8,128)(2,1)}, bf16[576,384]{1,0:T(8,128)(2,1)}, u32[]{:S(2)}, u32[]{:S(2)}) collective-permute-start(bf16[576,384]{1,0:T(8,128)(2,1)} %constant_dynamic-slice_fusion.1), channel_id=1, source_target_pairs={{0,2},{1,3},{2,0},{3,1},{4,6},{5,7},{6,4},{7,5},{8,10},{9,11},{10,... | collective-permute-start | bytes 1327112 | tf_op jit(solution)/shard_map/ppermute | solution.py:42
  21.4 27.6 %collective-permute-start = (bf16[256,1536]{1,0:T(8,128)(2,1)}, bf16[256,1536]{1,0:T(8,128)(2,1)}, u32[]{:S(2)}, u32[]{:S(2)}) collective-permute-start(bf16[256,1536]{1,0:T(8,128)(2,1)} %get-tuple-element.500.ol.refs_0_), channel_id=1, source_target_pairs={{0,1},{1,0},{2,3},{3,2},{4,5},{5,4},{6,7},{7,6},{8,9},{9,8},{10,11... | collective-permute-start | bytes 2359304 | tf_op jit(solution)/shard_map/ppermute | solution.py:42
  49.0 67.4 %all-gather.11.cloned.1.call-start = ((), (), s32[]{:S(2)}) async-start(), calls=%async_computation.1 | async-start | bytes 1327104 | tf_op jit(solution)/shard_map/all_gather | solution.py:68
  49.1 22.0 %collective-permute-start.2 = (bf16[256,1536]{1,0:T(8,128)(2,1)S(1)}, bf16[256,1536]{1,0:T(8,128)(2,1)S(1)}, u32[]{:S(2)}, u32[]{:S(2)}) collective-permute-start(bf16[256,1536]{1,0:T(8,128)(2,1)S(1)} %get-tuple-element.501.oh.refs_1_), channel_id=1, source_target_pairs={{0,1},{1,0},{2,3},{3,2},{4,5},{5,4},{6,7},{7,6},{8,9},{9,8},{10,11... | collective-permute-start | bytes 2359304 | tf_op jit(solution)/shard_map/ppermute | solution.py:42
  50.1 21.0 %collective-permute-start.3 = (bf16[48,1536]{1,0:T(8,128)(2,1)S(1)}, bf16[48,1536]{1,0:T(8,128)(2,1)S(1)}, u32[]{:S(2)}, u32[]{:S(2)}) collective-permute-start(bf16[48,1536]{1,0:T(8,128)(2,1)S(1)} %constant_dynamic-slice_fusion), channel_id=1, source_target_pairs={{0,2},{1,3},{2,0},{3,1},{4,6},{5,7},{6,4},{7,5},{8,10},{9,11},{10,... | collective-permute-start | bytes 442376 | tf_op jit(solution)/shard_map/ppermute | solution.py:42
  71.8 114.9 %all-gather.13.cloned.1.call-start = ((), (), s32[]{:S(2)}) async-start(), calls=%async_computation.2 | async-start | bytes 10616832 | tf_op jit(solution)/shard_map/all_gather | solution.py:72
  74.5 54.4 %collective-permute-start.5 = (bf16[2,192,1536]{2,1,0:T(8,128)(2,1)}, bf16[2,192,1536]{2,1,0:T(8,128)(2,1)}, u32[]{:S(2)}, u32[]{:S(2)}) collective-permute-start(bf16[2,192,1536]{2,1,0:T(8,128)(2,1)} %pad_maximum_fusion), channel_id=1, source_target_pairs={{0,2},{1,3},{2,0},{3,1},{4,6},{5,7},{6,4},{7,5},{8,10},{9,11},{10,... | collective-permute-start | bytes 3538952 | tf_op jit(solution)/shard_map/ppermute | solution.py:42
  85.4 43.5 %collective-permute-start.4 = (bf16[256,1536]{1,0:T(8,128)(2,1)}, bf16[256,1536]{1,0:T(8,128)(2,1)}, u32[]{:S(2)}, u32[]{:S(2)}) collective-permute-start(bf16[256,1536]{1,0:T(8,128)(2,1)} %get-tuple-element.332), channel_id=1, source_target_pairs={{0,1},{1,0},{2,3},{3,2},{4,5},{5,4},{6,7},{7,6},{8,9},{9,8},{10,11... | collective-permute-start | bytes 2359304 | tf_op jit(solution)/shard_map/ppermute | solution.py:42
  128.9 417.6 %all-gather.17.cloned.1.call-start = ((), (), s32[]{:S(2)}) async-start(), calls=%async_computation.4 | async-start | bytes 10616832 | tf_op jit(solution)/shard_map/all_gather | solution.py:1016
  129.0 20.8 %collective-permute-start.8 = (bf16[256,1536]{1,0:T(8,128)(2,1)}, bf16[256,1536]{1,0:T(8,128)(2,1)S(1)}, u32[]{:S(2)}, u32[]{:S(2)}) collective-permute-start(bf16[256,1536]{1,0:T(8,128)(2,1)} %copy-done.91), channel_id=1, source_target_pairs={{0,1},{1,0},{2,3},{3,2},{4,5},{5,4},{6,7},{7,6},{8,9},{9,8},{10,11... | collective-permute-start | bytes 2359304 | tf_op jit(solution)/shard_map/ppermute | solution.py:42
  129.1 37.5 %collective-permute-start.7 = (bf16[256,1536]{1,0:T(8,128)(2,1)}, bf16[256,1536]{1,0:T(8,128)(2,1)S(1)}, u32[]{:S(2)}, u32[]{:S(2)}) collective-permute-start(bf16[256,1536]{1,0:T(8,128)(2,1)} %copy-done.89), channel_id=1, source_target_pairs={{0,1},{1,0},{2,3},{3,2},{4,5},{5,4},{6,7},{7,6},{8,9},{9,8},{10,11... | collective-permute-start | bytes 2359304 | tf_op jit(solution)/shard_map/ppermute | solution.py:42
  131.1 52.4 %collective-permute-start.6 = (bf16[256,1536]{1,0:T(8,128)(2,1)}, bf16[256,1536]{1,0:T(8,128)(2,1)S(1)}, u32[]{:S(2)}, u32[]{:S(2)}) collective-permute-start(bf16[256,1536]{1,0:T(8,128)(2,1)} %copy-done.90), channel_id=1, source_target_pairs={{0,1},{1,0},{2,3},{3,2},{4,5},{5,4},{6,7},{7,6},{8,9},{9,8},{10,11... | collective-permute-start | bytes 2359304 | tf_op jit(solution)/shard_map/ppermute | solution.py:42
  153.0 48.4 %collective-permute-start.10 = (bf16[256,1536]{1,0:T(8,128)(2,1)}, bf16[256,1536]{1,0:T(8,128)(2,1)}, u32[]{:S(2)}, u32[]{:S(2)}) collective-permute-start(bf16[256,1536]{1,0:T(8,128)(2,1)} %get-tuple-element.368.own), channel_id=1, source_target_pairs={{0,1},{1,0},{2,3},{3,2},{4,5},{5,4},{6,7},{7,6},{8,9},{9,8},{10,11... | collective-permute-start | bytes 2359304 | tf_op jit(solution)/shard_map/ppermute | solution.py:42
  186.7 39.5 %collective-permute-start.9 = (bf16[256,1536]{1,0:T(8,128)(2,1)}, bf16[256,1536]{1,0:T(8,128)(2,1)}, u32[]{:S(2)}, u32[]{:S(2)}) collective-permute-start(bf16[256,1536]{1,0:T(8,128)(2,1)} %get-tuple-element.384.own), channel_id=1, source_target_pairs={{0,1},{1,0},{2,3},{3,2},{4,5},{5,4},{6,7},{7,6},{8,9},{9,8},{10,11... | collective-permute-start | bytes 2359304 | tf_op jit(solution)/shard_map/ppermute | solution.py:42
  224.1 25.0 %collective-permute-start.12 = (bf16[256,1536]{1,0:T(8,128)(2,1)S(1)}, bf16[256,1536]{1,0:T(8,128)(2,1)S(1)}, u32[]{:S(2)}, u32[]{:S(2)}) collective-permute-start(bf16[256,1536]{1,0:T(8,128)(2,1)S(1)} %get-tuple-element.410), channel_id=1, source_target_pairs={{0,1},{1,0},{2,3},{3,2},{4,5},{5,4},{6,7},{7,6},{8,9},{9,8},{10,11... | collective-permute-start | bytes 2359304 | tf_op jit(solution)/shard_map/ppermute | solution.py:42
  273.8 23.3 %collective-permute-start.16 = (bf16[2,1,768,1536]{3,2,1,0:T(8,128)(2,1)}, bf16[2,1,768,1536]{3,2,1,0:T(8,128)(2,1)}, u32[]{:S(2)}, u32[]{:S(2)}) collective-permute-start(bf16[2,1,768,1536]{3,2,1,0:T(8,128)(2,1)} %shard_map.230), channel_id=1, source_target_pairs={{0,4},{1,5},{2,6},{3,7},{4,0},{5,1},{6,2},{7,3},{8,12},{9,13},{10,... | collective-permute-start | bytes 14155784 | tf_op jit(solution)/shard_map/ppermute | solution.py:42
  306.9 52.4 %collective-permute-start.18 = (bf16[2,1,384,1536]{3,2,1,0:T(8,128)(2,1)S(1)}, bf16[2,1,384,1536]{3,2,1,0:T(8,128)(2,1)S(1)}, u32[]{:S(2)}, u32[]{:S(2)}) collective-permute-start(bf16[2,1,384,1536]{3,2,1,0:T(8,128)(2,1)S(1)} %get-tuple-element.455), channel_id=1, source_target_pairs={{0,16},{1,17},{2,18},{3,19},{4,20},{5,21},{6,22},{7,23},{8,24},{9,... | collective-permute-start | bytes 7077896 | tf_op jit(solution)/shard_map/ppermute | solution.py:42
  308.6 52.1 %collective-permute-start.17 = (bf16[2,1,384,1536]{3,2,1,0:T(8,128)(2,1)S(1)}, bf16[2,1,384,1536]{3,2,1,0:T(8,128)(2,1)S(1)}, u32[]{:S(2)}, u32[]{:S(2)}) collective-permute-start(bf16[2,1,384,1536]{3,2,1,0:T(8,128)(2,1)S(1)} %copy-done.82), channel_id=1, source_target_pairs={{0,8},{1,9},{2,10},{3,11},{4,12},{5,13},{6,14},{7,15},{8,0},{9,1},... | collective-permute-start | bytes 7077896 | tf_op jit(solution)/shard_map/ppermute | solution.py:42
  308.6 20.5 %collective-permute-start.14 = (bf16[256,1536]{1,0:T(8,128)(2,1)S(1)}, bf16[256,1536]{1,0:T(8,128)(2,1)S(1)}, u32[]{:S(2)}, u32[]{:S(2)}) collective-permute-start(bf16[256,1536]{1,0:T(8,128)(2,1)S(1)} %get-tuple-element.511.oh.refs_1_), channel_id=1, source_target_pairs={{0,1},{1,0},{2,3},{3,2},{4,5},{5,4},{6,7},{7,6},{8,9},{9,8},{10,11... | collective-permute-start | bytes 2359304 | tf_op jit(solution)/shard_map/ppermute | solution.py:42
  308.9 34.9 %collective-permute-start.15 = (bf16[256,1536]{1,0:T(8,128)(2,1)S(1)}, bf16[256,1536]{1,0:T(8,128)(2,1)S(1)}, u32[]{:S(2)}, u32[]{:S(2)}) collective-permute-start(bf16[256,1536]{1,0:T(8,128)(2,1)S(1)} %get-tuple-element.510.ol.refs_0_), channel_id=1, source_target_pairs={{0,1},{1,0},{2,3},{3,2},{4,5},{5,4},{6,7},{7,6},{8,9},{9,8},{10,11... | collective-permute-start | bytes 2359304 | tf_op jit(solution)/shard_map/ppermute | solution.py:42
  362.4 26.6 %collective-permute-start.21 = (bf16[2,1,192,1536]{3,2,1,0:T(8,128)(2,1)S(1)}, bf16[2,1,192,1536]{3,2,1,0:T(8,128)(2,1)S(1)}, u32[]{:S(2)}, u32[]{:S(2)}) collective-permute-start(bf16[2,1,192,1536]{3,2,1,0:T(8,128)(2,1)S(1)} %get-tuple-element.485), channel_id=1, source_target_pairs={{0,16},{1,17},{2,18},{3,19},{4,20},{5,21},{6,22},{7,23},{8,24},{9,... | collective-permute-start | bytes 3538952 | tf_op jit(solution)/shard_map/ppermute | solution.py:42
  362.8 26.2 %collective-permute-start.22 = (bf16[2,1,192,1536]{3,2,1,0:T(8,128)(2,1)S(1)}, bf16[2,1,192,1536]{3,2,1,0:T(8,128)(2,1)S(1)}, u32[]{:S(2)}, u32[]{:S(2)}) collective-permute-start(bf16[2,1,192,1536]{3,2,1,0:T(8,128)(2,1)S(1)} %get-tuple-element.486), channel_id=1, source_target_pairs={{0,8},{1,9},{2,10},{3,11},{4,12},{5,13},{6,14},{7,15},{8,0},{9,1},... | collective-permute-start | bytes 3538952 | tf_op jit(solution)/shard_map/ppermute | solution.py:42
  391.0 66.4 %collective-permute-start.30 = (bf16[2,192,1536]{2,1,0:T(8,128)(2,1)}, bf16[2,192,1536]{2,1,0:T(8,128)(2,1)}, u32[]{:S(2)}, u32[]{:S(2)}) collective-permute-start(bf16[2,192,1536]{2,1,0:T(8,128)(2,1)} %get-tuple-element.544), channel_id=1, source_target_pairs={{0,2},{1,3},{2,0},{3,1},{4,6},{5,7},{6,4},{7,5},{8,10},{9,11},{10,... | collective-permute-start | bytes 3538952 | tf_op jit(solution)/shard_map/ppermute | solution.py:42
  418.3 61.8 %collective-permute-start.25 = (bf16[512,1536]{1,0:T(8,128)(2,1)}, bf16[512,1536]{1,0:T(8,128)(2,1)}, u32[]{:S(2)}, u32[]{:S(2)}) collective-permute-start(bf16[512,1536]{1,0:T(8,128)(2,1)} %shard_map.243), channel_id=1, source_target_pairs={{0,1},{1,0},{2,3},{3,2},{4,5},{5,4},{6,7},{7,6},{8,9},{9,8},{10,11... | collective-permute-start | bytes 4718600 | tf_op jit(solution)/shard_map/ppermute | solution.py:42
  418.8 27.9 %collective-permute-start.27 = (bf16[2,2,384,384]{3,2,1,0:T(8,128)(2,1)}, bf16[2,2,384,384]{3,2,1,0:T(8,128)(2,1)}, u32[]{:S(2)}, u32[]{:S(2)}) collective-permute-start(bf16[2,2,384,384]{3,2,1,0:T(8,128)(2,1)} %get-tuple-element.535), channel_id=1, source_target_pairs={{0,16},{1,17},{2,18},{3,19},{4,20},{5,21},{6,22},{7,23},{8,24},{9,... | collective-permute-start | bytes 3538952 | tf_op jit(solution)/shard_map/ppermute | solution.py:42
  420.5 27.7 %collective-permute-start.26 = (bf16[2,2,384,384]{3,2,1,0:T(8,128)(2,1)}, bf16[2,2,384,384]{3,2,1,0:T(8,128)(2,1)}, u32[]{:S(2)}, u32[]{:S(2)}) collective-permute-start(bf16[2,2,384,384]{3,2,1,0:T(8,128)(2,1)} %get-tuple-element.534), channel_id=1, source_target_pairs={{0,8},{1,9},{2,10},{3,11},{4,12},{5,13},{6,14},{7,15},{8,0},{9,1},... | collective-permute-start | bytes 3538952 | tf_op jit(solution)/shard_map/ppermute | solution.py:42
  460.5 100.7 %all-gather.15.cloned.1.call-start = ((), (), s32[]{:S(2)}) async-start(), calls=%async_computation.3 | async-start | bytes 5308416 | tf_op jit(solution)/shard_map/all_gather | solution.py:1016
  473.5 26.9 %collective-permute-start.33 = (bf16[4,192,384]{2,1,0:T(8,128)(2,1)}, bf16[4,192,384]{2,1,0:T(8,128)(2,1)}, u32[]{:S(2)}, u32[]{:S(2)}) collective-permute-start(bf16[4,192,384]{2,1,0:T(8,128)(2,1)} %get-tuple-element.571), channel_id=1, source_target_pairs={{0,2},{1,3},{2,0},{3,1},{4,6},{5,7},{6,4},{7,5},{8,10},{9,11},{10,... | collective-permute-start | bytes 1769480 | tf_op jit(solution)/shard_map/ppermute | solution.py:42
  503.0 40.9 %collective-permute-start.23 = (bf16[256,1536]{1,0:T(8,128)(2,1)}, bf16[256,1536]{1,0:T(8,128)(2,1)S(1)}, u32[]{:S(2)}, u32[]{:S(2)}) collective-permute-start(bf16[256,1536]{1,0:T(8,128)(2,1)} %copy-done.88), channel_id=1, source_target_pairs={{0,1},{1,0},{2,3},{3,2},{4,5},{5,4},{6,7},{7,6},{8,9},{9,8},{10,11... | collective-permute-start | bytes 2359304 | tf_op jit(solution)/shard_map/ppermute | solution.py:42
  503.2 40.8 %collective-permute-start.24 = (bf16[256,1536]{1,0:T(8,128)(2,1)}, bf16[256,1536]{1,0:T(8,128)(2,1)S(1)}, u32[]{:S(2)}, u32[]{:S(2)}) collective-permute-start(bf16[256,1536]{1,0:T(8,128)(2,1)} %copy-done.87), channel_id=1, source_target_pairs={{0,1},{1,0},{2,3},{3,2},{4,5},{5,4},{6,7},{7,6},{8,9},{9,8},{10,11... | collective-permute-start | bytes 2359304 | tf_op jit(solution)/shard_map/ppermute | solution.py:42
  510.7 28.4 %collective-permute-start.35 = (f32[4,1536]{1,0:T(4,128)S(1)}, f32[4,1536]{1,0:T(4,128)S(1)}, u32[]{:S(2)}, u32[]{:S(2)}) collective-permute-start(f32[4,1536]{1,0:T(4,128)S(1)} %add.44), channel_id=1, source_target_pairs={{0,1},{1,0},{2,3},{3,2},{4,5},{5,4},{6,7},{7,6},{8,9},{9,8},{10,11... | collective-permute-start | bytes 73736 | tf_op jit(solution)/shard_map/ppermute | solution.py:42
  (109 other events, 879.7 us)
Sparse Core Ops, SparseCore 0:
  49.1 34.0 all-gather.8
  85.7 24.0 all-gather.10
  129.1 57.2 all-gather.12
  460.7 59.4 all-gather.16
  522.4 38.7 all-gather.14
